TPU v7x, 32 devices: a whole 2x2x4 slice. The times are simulated.
32 devices in a mesh: ctx: 8 (over z, x), tp: 4 (over y, core).
Axes of the slice: x: 2, y: 2, z: 4, core: 2. Of those that a mesh axis runs over, the one named last changes fastest.
Arguments:
- q_pre: bfloat16 [2, 512, 4096], P(None, 'ctx', 'tp'), may hold values from -8 to 8
- k_pre: bfloat16 [2, 512, 512], P(None, 'ctx', 'tp'), may hold values from -8 to 8
- value_before_filter: bfloat16 [2, 512, 512], P(None, 'ctx', 'tp'), may hold values from -8 to 8
- d_out: bfloat16 [2, 512, 4096], P(None, 'ctx', 'tp'), may hold values from -8 to 8
- filters: float32 [3, 3, 128], replicated, may hold values from 0.5 to 1.5
- doc_lengths: int32 [8], replicated, may hold values from 1 to 512, 1024 in all
Outputs:
- d_q_pre: float32 [2, 512, 4096], P(None, 'ctx', 'tp')
- d_k_pre: float32 [2, 512, 512], P(None, 'ctx', 'tp')
- d_v_pre: float32 [2, 512, 512], P(None, 'ctx', 'tp')
- d_filters: float32 [3, 3, 128], replicated
Inputs may be any that keep to these rules, and one draw needn't show every extreme that they name: `doc_lengths`: the lengths sum to 1024, and the longest document has exactly 512 positions.
All inputs are finite; a program needn't handle non-finite values.
Results may differ from a plain program's by a relative error of at most 0.009.
The roundings to bfloat16 on the way count: a program that leaves them out, or rounds other values in their place, can miss the bound.
Values may be sent and summed in bfloat16 or wider, within the bound.
No kernel may reach another device: no remote copies, remote signals or barrier semaphores. Data moves between devices by JAX's collectives and lax.ppermute only.
A program may use at most 128 MiB of HBM per device.

v0:
```python
import functools

import jax
import jax.numpy as jnp
import numpy as np
from jax import lax
from jax.experimental import pallas as pl
from jax.experimental.pallas import tpu as pltpu
from jax.sharding import PartitionSpec as P

LANES = 128
NT = (((1,), (1,)), ((), ()))
NN = (((1,), (0,)), ((), ()))
TN = (((0,), (0,)), ((), ()))
TAIL = 16
MAX_CHUNK = 640
MAX_DIRECT = 4
MIB = 1 << 20


def loop(count, body, init, unrolled=16):
    if count <= unrolled:
        for step in range(count):
            init = body(step, init)
        return init
    return lax.fori_loop(0, count, body, init)


def aligned(start, multiple):
    return start if isinstance(start, int) else pl.multiple_of(start, multiple)


def doc_starts(lengths_ref):
    starts = [jnp.int32(0)]
    for index in range(lengths_ref.shape[0] - 1):
        starts.append(starts[-1] + lengths_ref[index])
    return starts


def fold_rows(terms):
    rows, lanes = terms.shape
    return jnp.sum(terms.reshape(rows // 8, 8, lanes), axis=0)


def split_bits(values):
    high = values.astype(jnp.bfloat16)
    low = (values - high.astype(jnp.float32)).astype(jnp.bfloat16)
    return high, low


def joined(pair):
    rows = pair.shape[0] // 2
    pair = pair.astype(jnp.float32)
    return pair[:rows] + pair[rows:]


class Slots:
    def __init__(self, refs, me):
        self.refs, self.me = refs, me

    def __getitem__(self, flip):
        if len(self.refs) == 1:
            place = lax.rem(self.me, jnp.int32(self.refs[0].shape[0]))
            return self.refs[0].at[partner(place, flip)]
        return self.refs[flip]


def partner(me, flip):
    return lax.bitwise_xor(me, jnp.int32(flip))


def pack_kernel(k_ref, v_ref, q_ref, out_ref):
    span = k_ref.shape[1]
    kv = jnp.concatenate([k_ref[...], v_ref[...]], axis=2).reshape(2 * span, 2 * LANES)
    tails = []
    for half in range(2):
        last = q_ref[half].astype(jnp.float32)[TAIL - 2 :]
        tails += [last[:, at : at + 2 * LANES] for at in range(0, last.shape[1], 2 * LANES)]
    out_ref[: 2 * span] = kv
    out_ref[2 * span :] = jnp.concatenate(tails, axis=0).astype(jnp.bfloat16)


def grads_kernel(ctx_count, direct, lengths_ref, filters_ref, q_hbm, d_out_hbm, *refs):
    group = ctx_count // 2
    arrays = group if direct else 1
    near_in, far_in, refs = refs[:arrays], refs[arrays : 2 * arrays], refs[2 * arrays :]
    dq_hbm, own_near_ref, own_far_ref = refs[:3]
    arrays = group - 1 if direct else 1
    out_refs, refs = refs[3 : 3 + arrays], refs[3 + arrays :]
    same_scr, kv_scr, conv_scr, dkv_scr, q_scr, qc_scr, do_scr, dq_scr = refs[:8]
    s_scr, dp_scr, rim_scr, q_ref, d_out_ref, dq_ref, sems = refs[8:]
    f32, bf16 = jnp.float32, jnp.bfloat16
    loads = [
        pltpu.make_async_copy(q_hbm, q_ref, sems.at[0]),
        pltpu.make_async_copy(d_out_hbm, d_out_ref, sems.at[1]),
    ]
    for load in loads:
        load.start()
    span = q_ref.shape[1]
    heads = q_ref.shape[2] // LANES
    half_rows = span * ctx_count
    length = 2 * half_rows
    blocks = 2 * ctx_count
    me = lax.axis_index("ctx")
    near_in, far_in = Slots(near_in, me), Slots(far_in, me)
    sent = Slots((own_far_ref,) + out_refs if direct else out_refs, me)
    scale = LANES**-0.5
    log2_scale = scale * 1.4426950408889634
    starts = doc_starts(lengths_ref)

    def fill_same(index, carry):
        place = index * span + lax.broadcasted_iota(jnp.int32, (span, LANES), 0)
        cut = place == starts[0]
        for start in starts[1:]:
            cut = cut | (place == start)
        same_scr[pl.ds(aligned(8 + index * span, 8), span)] = jnp.where(cut, 0.0, 1.0)
        return carry

    same_scr[:8] = jnp.zeros((8, LANES), f32)
    same_scr[8 + length :] = jnp.zeros((8, LANES), f32)
    loop(blocks, fill_same, 0)

    kv_scr[:8] = jnp.zeros((8, 2 * LANES), f32)
    kv_scr[8 + length :] = jnp.zeros((8, 2 * LANES), f32)

    def place_blocks(flip, carry):
        for message, index in (
            (near_in[flip], partner(me, flip)),
            (far_in[flip], partner(me, flip + group)),
        ):
            early = aligned(8 + index * span, 8)
            late = aligned(8 + (blocks - 1 - index) * span, 8)
            kv_scr[pl.ds(early, span)] = message[:span].astype(f32)
            kv_scr[pl.ds(late, span)] = message[span : 2 * span].astype(f32)
            rim_scr[index] = message[2 * span :].astype(f32)
        return carry

    loop(group, place_blocks, 0)

    def kv_taps(tap):
        return jnp.concatenate([filters_ref[1, tap : tap + 1], filters_ref[2, tap : tap + 1]], axis=1)

    def twice(mask):
        return jnp.concatenate([mask, mask], axis=1)

    def back_masks(same, first):
        one = same[first : first + span]
        return one, one * same[first - 1 : first - 1 + span]

    def convolve_kv(index, carry):
        rows = pl.ds(aligned(index * span, 8), span + 8)
        values = kv_scr[rows]
        one, two = back_masks(same_scr[rows], 8)
        total = kv_taps(0) * values[8:]
        total = total + twice(one) * (kv_taps(1) * values[7 : 7 + span])
        total = total + twice(two) * (kv_taps(2) * values[6 : 6 + span])
        conv_scr[pl.ds(aligned(index * span, 16), span)] = total.astype(bf16)
        return carry

    loop(blocks, convolve_kv, 0)

    middle = me == ctx_count - 1
    rim_rows = rim_scr.shape[1] // 2
    rim_before = rim_scr[jnp.maximum(me - 1, 0)]
    rim_after = rim_scr[jnp.minimum(me + 1, ctx_count - 1)]
    late_rim = jnp.where(middle, rim_after[:rim_rows], rim_after[rim_rows:])
    rims = [rim_before[:rim_rows], late_rim]
    first_place = [me * span, (blocks - 1 - me) * span]

    for load in loads:
        load.wait()
    for half in range(2):
        rows = [rims[half][2 * at : 2 * at + 2] for at in range(rim_rows // 2)]
        q_scr[half, 6:8] = jnp.concatenate(rows, axis=1)
        q_scr[half, 8:] = q_ref[half].astype(f32)
        same = same_scr[pl.ds(aligned(first_place[half], 8), span + 16)]
        one, two = back_masks(same, 8)
        for head in range(heads):
            lanes = slice(head * LANES, (head + 1) * LANES)
            total = filters_ref[0, 0:1] * q_scr[half, 8:, lanes]
            total = total + one * (filters_ref[0, 1:2] * q_scr[half, 7 : 7 + span, lanes])
            total = total + two * (filters_ref[0, 2:3] * q_scr[half, 6 : 6 + span, lanes])
            qc_scr[half, head * span : (head + 1) * span] = total.astype(bf16)
            do_scr[half, head * span : (head + 1) * span] = d_out_ref[half, :, lanes]

    def attend(half, window, first_key, add):
        chunks = 1
        while window // chunks > MAX_CHUNK or window % (16 * chunks):
            chunks += 1
        size = window // chunks
        query = first_place[half] + lax.rem(
            lax.broadcasted_iota(jnp.int32, (1, LANES), 1), jnp.int32(span)
        )
        lowest = jnp.zeros((1, LANES), jnp.int32)
        for start in starts[1:]:
            lowest = jnp.where(query >= start, start, lowest)
        wide = 2 * LANES
        whole_window = pl.ds(aligned(first_key, 16), window)
        keys_t = conv_scr[whole_window, :LANES].T if chunks == 1 else None
        for at in range(heads * span // wide):
            slot = (half * (heads * span // wide) + at) % s_scr.shape[0]
            cols = slice(at * wide, (at + 1) * wide)
            queries = qc_scr[half, cols]
            grads = do_scr[half, cols]

            def key_rows(step):
                return pl.ds(aligned(first_key + step * size, 16), size)

            def score(step, top):
                places = first_key + step * size + lax.broadcasted_iota(jnp.int32, (size, LANES), 0)
                allowed = (places >= lowest) & (places <= query)
                bias = jnp.where(allowed, 0.0, -1e30)
                keys = conv_scr[key_rows(step), :LANES]
                scores = lax.dot_general(keys, queries, NT, preferred_element_type=f32)
                scores = scores + twice(bias)
                s_scr[slot, pl.ds(aligned(step * size, 16), size)] = scores
                return jnp.maximum(top, jnp.max(scores, axis=0, keepdims=True))

            top = loop(chunks, score, jnp.full((1, wide), -1e30, f32), 1)

            def weigh(step, carry):
                total, weighted = carry
                rows = pl.ds(aligned(step * size, 16), size)
                weights = jnp.exp2((s_scr[slot, rows] - top) * log2_scale)
                values = conv_scr[key_rows(step), LANES:]
                prob_grads = lax.dot_general(values, grads, NT, preferred_element_type=f32)
                s_scr[slot, rows] = weights
                dp_scr[slot, rows] = prob_grads
                total = total + jnp.sum(weights, axis=0, keepdims=True)
                weighted = weighted + jnp.sum(weights * prob_grads, axis=0, keepdims=True)
                return total, weighted

            zeros = jnp.zeros((1, wide), f32)
            total, weighted = loop(chunks, weigh, (zeros, zeros), 1)
            inverse = 1.0 / total
            mean = weighted * inverse
            slope = inverse * scale

            def accumulate(step, dq):
                rows = pl.ds(aligned(step * size, 16), size)
                weights = s_scr[slot, rows]
                probs = (weights * inverse).astype(bf16)
                score_grads = (weights * slope * (dp_scr[slot, rows] - mean)).astype(bf16)
                dk = lax.dot_general(score_grads, queries, NN, preferred_element_type=f32)
                dv = lax.dot_general(probs, grads, NN, preferred_element_type=f32)
                terms = jnp.concatenate([dk, dv], axis=1)
                target = pl.ds(aligned(first_key + step * size, 16), size)
                if add or at:
                    dkv_scr[target] += terms
                else:
                    dkv_scr[target] = terms
                if keys_t is not None:
                    return lax.dot_general(keys_t, score_grads, NN, preferred_element_type=f32)
                keys = conv_scr[key_rows(step), :LANES]
                return dq + lax.dot_general(keys, score_grads, TN, preferred_element_type=f32)

            dq = loop(chunks, accumulate, jnp.zeros((LANES, wide), f32), 1)
            dq = dq.T
            for part in range(wide // span):
                head = at * (wide // span) + part
                dq_scr[half, :span, head * LANES : (head + 1) * LANES] = dq[
                    part * span : (part + 1) * span
                ]

    dkv_scr[half_rows:] = jnp.zeros((half_rows + 8, 2 * LANES), f32)
    attend(0, half_rows, 0, False)
    attend(1, half_rows + span, (ctx_count - 1 - me) * span, True)

    next_rows = jnp.where(middle, dq_scr[1, :8], 0.0)
    dq_scr[0, span:] = next_rows
    dq_scr[1, span:] = jnp.zeros_like(next_rows)
    sums = [jnp.zeros((8, LANES), f32) for _ in range(3)]
    for half in range(2):
        same = same_scr[pl.ds(aligned(first_place[half], 8), span + 16)]
        one, two = back_masks(same, 8)
        ahead_one = same[9 : 9 + span]
        ahead_two = same[10 : 10 + span] * ahead_one
        for head in range(heads):
            lanes = slice(head * LANES, (head + 1) * LANES)
            grads = dq_scr[half, :span, lanes]
            out = filters_ref[0, 0:1] * grads
            out = out + ahead_one * (filters_ref[0, 1:2] * dq_scr[half, 1 : 1 + span, lanes])
            out = out + ahead_two * (filters_ref[0, 2:3] * dq_scr[half, 2 : 2 + span, lanes])
            dq_ref[half, :, lanes] = out
            sums[0] += fold_rows(grads * q_scr[half, 8:, lanes])
            sums[1] += fold_rows(grads * one * q_scr[half, 7 : 7 + span, lanes])
            sums[2] += fold_rows(grads * two * q_scr[half, 6 : 6 + span, lanes])
    q_sums = [jnp.sum(term, axis=0, keepdims=True) for term in sums]
    store = pltpu.make_async_copy(dq_ref, dq_hbm, sems.at[2])
    store.start()

    def finish_block(index, carry):
        base = aligned(index * span, 8)
        grads = dkv_scr[pl.ds(base, span + 8)]
        values = kv_scr[pl.ds(base, span + 8)]
        same = same_scr[pl.ds(base, span + 16)]
        one, two = back_masks(same, 8)
        ahead_one = same[9 : 9 + span]
        ahead_two = same[10 : 10 + span] * ahead_one
        out = kv_taps(0) * grads[:span]
        out = out + twice(ahead_one) * (kv_taps(1) * grads[1 : 1 + span])
        out = out + twice(ahead_two) * (kv_taps(2) * grads[2 : 2 + span])
        own = grads[:span]
        return out, (
            carry[0] + fold_rows(own * values[8:]),
            carry[1] + fold_rows(own * twice(one) * values[7 : 7 + span]),
            carry[2] + fold_rows(own * twice(two) * values[6 : 6 + span]),
        )

    def finish_pair(index, carry):
        early, carry = finish_block(index, carry)
        late, carry = finish_block(blocks - 1 - index, carry)
        return jnp.concatenate([early, late], axis=0), carry

    low = me < group

    def finish(step, carry):
        flip = step + 1
        owner = partner(me, flip)
        far_owner = partner(me, flip + group)
        near_late = blocks - 1 - owner
        places = [
            far_owner,
            jnp.where(low, blocks - 1 - far_owner, owner),
            jnp.where(low & (me > owner), owner, near_late),
        ]
        for at, place in enumerate(places):
            terms, carry = finish_block(place, carry)
            sent[flip][at * span : (at + 1) * span] = terms.astype(bf16)
        return carry

    zeros = jnp.zeros((8, 2 * LANES), f32)
    own_far_ref[: 2 * span], kv_sums = finish_pair(partner(me, group), (zeros, zeros, zeros))
    own_near_ref[...], kv_sums = finish_pair(me, kv_sums)
    kv_sums = loop(group - 1, finish, kv_sums)
    kv_sums = [jnp.sum(term, axis=0, keepdims=True) for term in kv_sums]

    sums_tile = jnp.concatenate(
        [jnp.concatenate([term, jnp.zeros_like(term)], axis=1) for term in q_sums]
        + kv_sums
        + [jnp.zeros((2, 2 * LANES), f32)],
        axis=0,
    )
    sums_pair = jnp.concatenate(split_bits(sums_tile), axis=0)
    own_far_ref[2 * span :] = joined(sums_pair)
    rims = []
    for half in range(2):
        rows = dq_scr[half, :2]
        rows = [rows[:, at : at + 2 * LANES] for at in range(0, rows.shape[1], 2 * LANES)]
        rims.append(jnp.concatenate(rows, axis=0))

    def rim_for(index):
        return jnp.concatenate(split_bits(jnp.where(index < me, rims[0], rims[1])), axis=0)

    def store_rims(step, carry):
        flip = step + 1
        owner = partner(me, flip)
        sent[flip][3 * span : 3 * span + 16] = sums_pair
        if not direct or flip & (flip + 1) == 0:
            across = (flip == group - 1) & (jnp.abs(owner - me) != 1)
            target = jnp.where(across, partner(owner, group), owner)
            sent[flip][3 * span + 16 :] = rim_for(target)
        return carry

    loop(group - 1, store_rims, 0, 16 if direct else 1)
    store.wait()


def merge_kernel(ctx_count, direct, own_near_ref, own_far_ref, *refs):
    received_refs = refs[:-6]
    near_ref, far_ref, half_sums_ref, rims_ref, sums_scr, rim_scr = refs[-6:]
    f32, bf16 = jnp.float32, jnp.bfloat16
    group = ctx_count // 2
    me = lax.axis_index("ctx")
    low = me < group
    received = Slots((own_far_ref,) + received_refs if direct else received_refs, me)
    place = lax.rem(me, jnp.int32(group))
    span = own_near_ref.shape[0] // 2
    rows = 2 * span
    sums_scr[place] = own_far_ref[rows:]
    neighbours = [jnp.minimum(me + 1, ctx_count - 1), jnp.maximum(me - 1, 0)]
    for index in neighbours:
        rim_scr[index] = jnp.zeros(rim_scr.shape[1:], f32)

    def add(step, carry):
        flip = step + 1
        source = partner(me, flip)
        message = received[flip]
        parts = [message[at * span : (at + 1) * span].astype(f32) for at in range(3)]
        near_early, near_late, far_early, far_late = carry
        sums_scr[partner(place, flip)] = joined(message[3 * span : 3 * span + 16])
        if not direct or flip & (flip + 1) == 0:
            rim_scr[source] = joined(message[3 * span + 16 :])
        to_early = low & (source > me)
        zero = jnp.zeros_like(parts[0])
        return (
            near_early + jnp.where(low, jnp.where(to_early, parts[2], zero), parts[1]),
            near_late + jnp.where(to_early, zero, parts[2]),
            far_early + parts[0],
            far_late + jnp.where(low, parts[1], zero),
        )

    init = (own_near_ref[:span], own_near_ref[span:], own_far_ref[:span], own_far_ref[span:rows])
    totals = loop(group - 1, add, init, 16 if direct else 1)
    near_ref[:span] = totals[0]
    near_ref[span:] = totals[1]
    far_ref[:span] = totals[2].astype(bf16)
    far_ref[span:rows] = totals[3].astype(bf16)
    sums = loop(group, lambda index, carry: carry + sums_scr[index], jnp.zeros((8, 2 * LANES), f32))
    pair = jnp.concatenate(split_bits(sums), axis=0)
    half_sums_ref[...] = joined(pair)
    far_ref[rows : rows + 16] = pair
    far_ref[rows + 16 :] = received[group - 1][3 * span + 16 :]
    for at, index in enumerate(neighbours):
        rims_ref[at] = rim_scr[index]


def sums_kernel(span, half_sums_ref, far_ref, out_ref):
    sums = half_sums_ref[...] + joined(far_ref[2 * span : 2 * span + 16])
    out_ref[0] = sums[0:3, :LANES]
    out_ref[1] = sums[3:6, :LANES]
    out_ref[2] = sums[3:6, LANES:]


def finish_kernel(
    ctx_count, lengths_ref, filters_ref, dq_in_ref, near_ref, far_ref, rims_ref, dq_ref, dk_ref, dv_ref
):
    f32 = jnp.float32
    group = ctx_count // 2
    span = dk_ref.shape[1]
    me = lax.axis_index("ctx")
    starts = doc_starts(lengths_ref)
    blocks = 2 * ctx_count

    total = near_ref[...] + far_ref[: 2 * span].astype(f32)
    for half in range(2):
        dk_ref[half] = total[half * span : (half + 1) * span, :LANES]
        dv_ref[half] = total[half * span : (half + 1) * span, LANES:]

    def same(place):
        cut = place >= blocks * span
        for start in starts:
            cut = cut | (place == start)
        return jnp.where(cut, 0.0, 1.0).astype(f32)

    heads = dq_ref.shape[2] // LANES
    taps = [jnp.concatenate([filters_ref[0, tap : tap + 1]] * heads, axis=1) for tap in range(3)]
    row = lax.broadcasted_iota(jnp.int32, dq_ref.shape[1:], 0)
    far_rim = joined(far_ref[2 * span + 16 :])
    crosses = [me == group - 1, me == group]
    first_place = [me * span, (blocks - 1 - me) * span]
    present = [me < ctx_count - 1, me > 0]
    for half in range(2):
        rim = jnp.where(crosses[half], far_rim, rims_ref[half])
        rows = jnp.concatenate([rim[2 * at : 2 * at + 2] for at in range(rim.shape[0] // 2)], axis=1)
        end = first_place[half] + span
        zero, one, two = same(end - 1), same(end), same(end + 1)
        one = jnp.where(present[half], one, 0.0)
        last_but_one = (zero * one) * (taps[2] * rows[0:1])
        last = one * (taps[1] * rows[0:1]) + (one * two) * (taps[2] * rows[1:2])
        extra = jnp.where(row == 6, last_but_one, jnp.where(row == 7, last, 0.0))
        dq_ref[half] = dq_in_ref[half] + extra


def shards(q_pre, k_pre, value_before_filter, d_out, filters, doc_lengths):
    f32, bf16 = jnp.float32, jnp.bfloat16
    ctx_count = lax.axis_size("ctx")
    span, width = q_pre.shape[1:]
    length = 2 * span * ctx_count
    rim = 4 * width // (2 * LANES)
    vmem = pl.BlockSpec(memory_space=pltpu.VMEM)
    smem = pl.BlockSpec(memory_space=pltpu.SMEM)
    hbm = pl.BlockSpec(memory_space=pltpu.HBM)

    group = ctx_count // 2
    direct = group <= MAX_DIRECT
    halves = [[half * group + at for at in range(group)] for half in range(2)]
    msg_rows = 2 * span + rim

    def whole(shape):
        return pl.BlockSpec(shape, lambda i: (0,) * len(shape))

    def flipped(array, flip):
        return lax.ppermute(array, "ctx", [(i, i ^ flip) for i in range(ctx_count)])

    def gathered(array):
        if direct:
            return [array] + [flipped(array, flip) for flip in range(1, group)]
        return [lax.all_gather(array, "ctx", axis_index_groups=halves)]

    def delivered(arrays):
        if direct:
            return [flipped(array, step + 1) for step, array in enumerate(arrays)]
        return [lax.all_to_all(arrays[0], "ctx", 0, 0, axis_index_groups=halves, tiled=True)]

    packed = pl.pallas_call(
        pack_kernel,
        grid=(1,),
        out_shape=jax.ShapeDtypeStruct((msg_rows, 2 * LANES), bf16),
        in_specs=[
            whole(k_pre.shape),
            whole(k_pre.shape),
            pl.BlockSpec((2, TAIL, width), lambda i: (0, span // TAIL - 1, 0)),
        ],
        out_specs=whole((msg_rows, 2 * LANES)),
        compiler_params=pltpu.CompilerParams(vmem_limit_bytes=4 * MIB),
        name="pack",
    )(k_pre, value_before_filter, q_pre)
    across = flipped(packed, group)
    received = gathered(packed) + gathered(across)

    window = span * ctx_count + span
    if direct:
        sent_shapes = [
            (3 * span + (32 if flip & (flip + 1) == 0 else 16), 2 * LANES) for flip in range(1, group)
        ]
    else:
        sent_shapes = [(group, 3 * span + 32, 2 * LANES)]
    scratch = [
        pltpu.VMEM((length + 16, LANES), f32),
        pltpu.VMEM((length + 16, 2 * LANES), f32),
        pltpu.VMEM((length, 2 * LANES), bf16),
        pltpu.VMEM((length + 8, 2 * LANES), f32),
        pltpu.VMEM((2, span + 8, width), f32),
        pltpu.VMEM((2, span * width // LANES, LANES), bf16),
        pltpu.VMEM((2, span * width // LANES, LANES), bf16),
        pltpu.VMEM((2, span + 8, width), f32),
        pltpu.VMEM((4 if direct else 1, window, 2 * LANES), f32),
        pltpu.VMEM((4 if direct else 1, window, 2 * LANES), f32),
        pltpu.VMEM((ctx_count, rim, 2 * LANES), f32),
        pltpu.VMEM(q_pre.shape, bf16),
        pltpu.VMEM(q_pre.shape, bf16),
        pltpu.VMEM(q_pre.shape, f32),
        pltpu.SemaphoreType.DMA((3,)),
    ]
    own_shapes = [(2 * span, 2 * LANES), (2 * span + 8, 2 * LANES)]
    d_q_main, own_near, own_far, *sent = pl.pallas_call(
        functools.partial(grads_kernel, ctx_count, direct),
        out_shape=[jax.ShapeDtypeStruct(q_pre.shape, f32)]
        + [jax.ShapeDtypeStruct(shape, f32) for shape in own_shapes]
        + [jax.ShapeDtypeStruct(shape, bf16) for shape in sent_shapes],
        in_specs=[smem, vmem, hbm, hbm] + [vmem] * len(received),
        out_specs=[hbm] + [vmem] * (2 + len(sent_shapes)),
        scratch_shapes=scratch,
        compiler_params=pltpu.CompilerParams(vmem_limit_bytes=(20 if direct else 62) * MIB),
        name="grads",
    )(doc_lengths, filters, q_pre, d_out, *received)
    half_terms = delivered(sent)
    merged_shapes = [
        jax.ShapeDtypeStruct((2 * span, 2 * LANES), f32),
        jax.ShapeDtypeStruct((2 * span + 32, 2 * LANES), bf16),
        jax.ShapeDtypeStruct((8, 2 * LANES), f32),
        jax.ShapeDtypeStruct((2, rim // 2, 2 * LANES), f32),
    ]
    near, far, half_sums, rims = pl.pallas_call(
        functools.partial(merge_kernel, ctx_count, direct),
        out_shape=merged_shapes,
        in_specs=[vmem] * (2 + len(half_terms)),
        out_specs=[vmem] * len(merged_shapes),
        scratch_shapes=[
            pltpu.VMEM((group, 8, 2 * LANES), f32),
            pltpu.VMEM((ctx_count, rim // 2, 2 * LANES), f32),
        ],
        compiler_params=pltpu.CompilerParams(vmem_limit_bytes=(4 if direct else 40) * MIB),
        name="merge",
    )(own_near, own_far, *half_terms)
    from_half = flipped(far, group)

    sums = pl.pallas_call(
        functools.partial(sums_kernel, span),
        out_shape=jax.ShapeDtypeStruct(filters.shape, f32),
        in_specs=[vmem, vmem],
        out_specs=vmem,
        compiler_params=pltpu.CompilerParams(vmem_limit_bytes=2 * MIB),
        name="sums",
    )(half_sums, from_half)
    count = lax.axis_size("tp")
    level = [sums] + [
        lax.ppermute(sums, "tp", [(i, i ^ flip) for i in range(count)]) for flip in range(1, count)
    ]

    last_rows = pl.BlockSpec((2, 8, width), lambda i: (0, span // 8 - 1, 0))
    d_q_pre, d_k_pre, d_v_pre = pl.pallas_call(
        functools.partial(finish_kernel, ctx_count),
        grid=(1,),
        out_shape=(
            jax.ShapeDtypeStruct(q_pre.shape, f32),
            jax.ShapeDtypeStruct(k_pre.shape, f32),
            jax.ShapeDtypeStruct(k_pre.shape, f32),
        ),
        in_specs=[smem, whole(filters.shape), last_rows]
        + [whole(array.shape) for array in (near, from_half, rims)],
        out_specs=(last_rows, whole(k_pre.shape), whole(k_pre.shape)),
        input_output_aliases={2: 0},
        compiler_params=pltpu.CompilerParams(vmem_limit_bytes=4 * MIB),
        name="finish",
    )(doc_lengths, filters, d_q_main, near, from_half, rims)

    while len(level) > 1:
        level = [level[at] + level[at + 1] for at in range(0, len(level), 2)]
    d_filters = level[0]
    return (d_q_pre, d_k_pre, d_v_pre, d_filters)


def solution(mesh):
    split = P(None, "ctx", "tp")
    return jax.shard_map(
        shards,
        mesh=mesh,
        in_specs=(split, split, split, split, P(), P()),
        out_specs=(split, split, split, P()),
        check_vma=False,
    )
```

profile of v0, /device:TPU:0, one launch (start us, length us, event | category | flops | bytes accessed | tf_op | source)
XLA Modules:
  0.0 42.9 jit_solution(1870396153428002631)
XLA Ops:
  0.6 0.0 copy-start
  0.6 0.9 %copy-done = bf16[2,64,1024]{2,1,0:T(8,128)(2,1)S(1)} copy-done((bf16[2,64,1024]{2,1,0:T(8,128)(2,1)S(1)}, bf16[2,64,1024]{2,1,0:T(8,128)(2,1)}, u32[]{:S(2)}) %copy-start) | copy-done | bytes 262168
  1.6 0.0 copy-start.3
  1.6 0.8 %copy-done.3 = bf16[2,64,128]{2,1,0:T(8,128)(2,1)S(1)} copy-done((bf16[2,64,128]{2,1,0:T(8,128)(2,1)S(1)}, bf16[2,64,128]{2,1,0:T(8,128)(2,1)}, u32[]{:S(2)}) %copy-start.3) | copy-done | bytes 32792
  2.3 0.0 copy-start.4
  2.3 0.8 %copy-done.4 = bf16[2,64,128]{2,1,0:T(8,128)(2,1)S(1)} copy-done((bf16[2,64,128]{2,1,0:T(8,128)(2,1)S(1)}, bf16[2,64,128]{2,1,0:T(8,128)(2,1)}, u32[]{:S(2)}) %copy-start.4) | copy-done | bytes 32792
  3.1 0.0 copy-start.1
  3.1 0.0 copy-start.5
  3.1 0.0 copy-start.6
  3.1 4.1 %collective-permute-start.3 = (bf16[144,256]{1,0:T(8,128)(2,1)S(1)}, bf16[144,256]{1,0:T(8,128)(2,1)S(1)}, u32[]{:S(2)}, u32[]{:S(2)}) collective-permute-start(bf16[144,256]{1,0:T(8,128)(2,1)S(1)} %pack.1.refs_0_), channel_id=1, source_target_pairs={{0,16},{4,20},{8,24},{12,28},{16,0},{20,4},{24,8},{28,12},{1,17},{... | collective-permute-start | bytes 221192 | tf_op jit(solution)/shard_map/ppermute | solution.py:484
  7.2 2.5 %collective-permute-start.2 = (bf16[144,256]{1,0:T(8,128)(2,1)S(1)}, bf16[144,256]{1,0:T(8,128)(2,1)S(1)}, u32[]{:S(2)}, u32[]{:S(2)}) collective-permute-start(bf16[144,256]{1,0:T(8,128)(2,1)S(1)} %pack.1.refs_0_), channel_id=1, source_target_pairs={{0,12},{4,8},{8,4},{12,0},{16,28},{20,24},{24,20},{28,16},{1,13},{... | collective-permute-start | bytes 221192 | tf_op jit(solution)/shard_map/ppermute | solution.py:484
  9.7 0.4 %collective-permute-start.1 = (bf16[144,256]{1,0:T(8,128)(2,1)S(1)}, bf16[144,256]{1,0:T(8,128)(2,1)S(1)}, u32[]{:S(2)}, u32[]{:S(2)}) collective-permute-start(bf16[144,256]{1,0:T(8,128)(2,1)S(1)} %pack.1.refs_0_), channel_id=1, source_target_pairs={{0,8},{4,12},{8,0},{12,4},{16,24},{20,28},{24,16},{28,20},{1,9},{5... | collective-permute-start | bytes 221192 | tf_op jit(solution)/shard_map/ppermute | solution.py:484
  10.2 0.5 %collective-permute-start = (bf16[144,256]{1,0:T(8,128)(2,1)S(1)}, bf16[144,256]{1,0:T(8,128)(2,1)S(1)}, u32[]{:S(2)}, u32[]{:S(2)}) collective-permute-start(bf16[144,256]{1,0:T(8,128)(2,1)S(1)} %pack.1.refs_0_), channel_id=1, source_target_pairs={{0,4},{4,0},{8,12},{12,8},{16,20},{20,16},{24,28},{28,24},{1,5},{5... | collective-permute-start | bytes 221192 | tf_op jit(solution)/shard_map/ppermute | solution.py:484
  10.7 0.0 collective-permute-done.3.refs_4_
  10.7 2.5 %collective-permute-start.6 = (bf16[144,256]{1,0:T(8,128)(2,1)S(1)}, bf16[144,256]{1,0:T(8,128)(2,1)S(1)}, u32[]{:S(2)}, u32[]{:S(2)}) collective-permute-start(bf16[144,256]{1,0:T(8,128)(2,1)S(1)} %collective-permute-done.3.refs_4_), channel_id=1, source_target_pairs={{0,12},{4,8},{8,4},{12,0},{16,28},{20,24},{24,20},{28,16},{1,13},{... | collective-permute-start | bytes 221192 | tf_op jit(solution)/shard_map/ppermute | solution.py:484
  13.2 0.7 %collective-permute-start.5 = (bf16[144,256]{1,0:T(8,128)(2,1)S(1)}, bf16[144,256]{1,0:T(8,128)(2,1)S(1)}, u32[]{:S(2)}, u32[]{:S(2)}) collective-permute-start(bf16[144,256]{1,0:T(8,128)(2,1)S(1)} %collective-permute-done.3.refs_4_), channel_id=1, source_target_pairs={{0,8},{4,12},{8,0},{12,4},{16,24},{20,28},{24,16},{28,20},{1,9},{5... | collective-permute-start | bytes 221192 | tf_op jit(solution)/shard_map/ppermute | solution.py:484
  13.9 0.0 collective-permute-done.2.refs_3_
  13.9 0.9 %collective-permute-start.4 = (bf16[144,256]{1,0:T(8,128)(2,1)S(1)}, bf16[144,256]{1,0:T(8,128)(2,1)S(1)}, u32[]{:S(2)}, u32[]{:S(2)}) collective-permute-start(bf16[144,256]{1,0:T(8,128)(2,1)S(1)} %collective-permute-done.3.refs_4_), channel_id=1, source_target_pairs={{0,4},{4,0},{8,12},{12,8},{16,20},{20,16},{24,28},{28,24},{1,5},{5... | collective-permute-start | bytes 221192 | tf_op jit(solution)/shard_map/ppermute | solution.py:484
  14.9 0.1 collective-permute-done.1.refs_2_
  14.9 0.9 %collective-permute-done.refs_1_ = bf16[144,256]{1,0:T(8,128)(2,1)S(1)} collective-permute-done((bf16[144,256]{1,0:T(8,128)(2,1)S(1)}, bf16[144,256]{1,0:T(8,128)(2,1)S(1)}, u32[]{:S(2)}, u32[]{:S(2)}) %collective-permute-start) | collective-permute-done | bytes 73760 | tf_op jit(solution)/shard_map/ppermute | solution.py:484
  15.9 0.8 %collective-permute-done.6.refs_7_ = bf16[144,256]{1,0:T(8,128)(2,1)S(1)} collective-permute-done((bf16[144,256]{1,0:T(8,128)(2,1)S(1)}, bf16[144,256]{1,0:T(8,128)(2,1)S(1)}, u32[]{:S(2)}, u32[]{:S(2)}) %collective-permute-start.6) | collective-permute-done | bytes 73760 | tf_op jit(solution)/shard_map/ppermute | solution.py:484
  16.7 0.9 %collective-permute-done.5.refs_6_ = bf16[144,256]{1,0:T(8,128)(2,1)S(1)} collective-permute-done((bf16[144,256]{1,0:T(8,128)(2,1)S(1)}, bf16[144,256]{1,0:T(8,128)(2,1)S(1)}, u32[]{:S(2)}, u32[]{:S(2)}) %collective-permute-start.5) | collective-permute-done | bytes 73760 | tf_op jit(solution)/shard_map/ppermute | solution.py:484
  17.6 0.7 %collective-permute-done.4.refs_5_ = bf16[144,256]{1,0:T(8,128)(2,1)S(1)} collective-permute-done((bf16[144,256]{1,0:T(8,128)(2,1)S(1)}, bf16[144,256]{1,0:T(8,128)(2,1)S(1)}, u32[]{:S(2)}, u32[]{:S(2)}) %collective-permute-start.4) | collective-permute-done | bytes 73760 | tf_op jit(solution)/shard_map/ppermute | solution.py:484
  18.3 0.0 copy-done.1
  18.3 0.0 copy-done.5
  18.3 0.0 copy-done.6
  18.3 0.0 copy-start.2
  18.3 0.9 %copy-done.2 = bf16[2,64,1024]{2,1,0:T(8,128)(2,1)S(1)} copy-done((bf16[2,64,1024]{2,1,0:T(8,128)(2,1)S(1)}, bf16[2,64,1024]{2,1,0:T(8,128)(2,1)}, u32[]{:S(2)}) %copy-start.2) | copy-done | bytes 262168
  19.3 6.2 %grads.1 = (f32[2,64,1024]{2,1,0:T(8,128)}, f32[128,256]{1,0:T(8,128)S(1)}, f32[136,256]{1,0:T(8,128)S(1)}, bf16[224,256]{1,0:T(8,128)(2,1)S(1)}, bf16[208,256]{...) custom-call(s32[8]{0:T(128)S(1)} %copy-done.6, f32[3,3,128]{2,1,0:T(4,128)S(1)} %copy-done.5, ...), custom_call_target="tpu_custom_call" | custom-call | tf_op jit(solution)/shard_map/grads/pallas_call | solution.py:537
  25.5 1.0 %collective-permute-start.7 = (bf16[224,256]{1,0:T(8,128)(2,1)S(1)}, bf16[224,256]{1,0:T(8,128)(2,1)S(1)}, u32[]{:S(2)}, u32[]{:S(2)}) collective-permute-start(bf16[224,256]{1,0:T(8,128)(2,1)S(1)} %get-tuple-element.20), channel_id=1, source_target_pairs={{0,4},{4,0},{8,12},{12,8},{16,20},{20,16},{24,28},{28,24},{1,5},{5... | collective-permute-start | bytes 344072 | tf_op jit(solution)/shard_map/ppermute | solution.py:484
  26.5 1.9 %collective-permute-start.9 = (bf16[224,256]{1,0:T(8,128)(2,1)S(1)}, bf16[224,256]{1,0:T(8,128)(2,1)S(1)}, u32[]{:S(2)}, u32[]{:S(2)}) collective-permute-start(bf16[224,256]{1,0:T(8,128)(2,1)S(1)} %get-tuple-element.22), channel_id=1, source_target_pairs={{0,12},{4,8},{8,4},{12,0},{16,28},{20,24},{24,20},{28,16},{1,13},{... | collective-permute-start | bytes 344072 | tf_op jit(solution)/shard_map/ppermute | solution.py:484
  28.3 0.7 %collective-permute-start.8 = (bf16[208,256]{1,0:T(8,128)(2,1)S(1)}, bf16[208,256]{1,0:T(8,128)(2,1)S(1)}, u32[]{:S(2)}, u32[]{:S(2)}) collective-permute-start(bf16[208,256]{1,0:T(8,128)(2,1)S(1)} %get-tuple-element.21), channel_id=1, source_target_pairs={{0,8},{4,12},{8,0},{12,4},{16,24},{20,28},{24,16},{28,20},{1,9},{5... | collective-permute-start | bytes 319496 | tf_op jit(solution)/shard_map/ppermute | solution.py:484
  29.1 4.0 %collective-permute-done.8.refs_1_ = bf16[208,256]{1,0:T(8,128)(2,1)S(1)} collective-permute-done((bf16[208,256]{1,0:T(8,128)(2,1)S(1)}, bf16[208,256]{1,0:T(8,128)(2,1)S(1)}, u32[]{:S(2)}, u32[]{:S(2)}) %collective-permute-start.8) | collective-permute-done | bytes 106528 | tf_op jit(solution)/shard_map/ppermute | solution.py:484
  33.0 0.0 collective-permute-done.7.refs_0_
  33.1 0.0 collective-permute-done.9.refs_2_
  33.1 0.1 merge.1
  33.2 2.9 %collective-permute-start.10 = (bf16[160,256]{1,0:T(8,128)(2,1)S(1)}, bf16[160,256]{1,0:T(8,128)(2,1)S(1)}, u32[]{:S(2)}, u32[]{:S(2)}) collective-permute-start(bf16[160,256]{1,0:T(8,128)(2,1)S(1)} %get-tuple-element.24), channel_id=1, source_target_pairs={{0,16},{4,20},{8,24},{12,28},{16,0},{20,4},{24,8},{28,12},{1,17},{... | collective-permute-start | bytes 245768 | tf_op jit(solution)/shard_map/ppermute | solution.py:484
  36.1 2.5 %collective-permute-done.10.far_ref = bf16[160,256]{1,0:T(8,128)(2,1)S(1)} collective-permute-done((bf16[160,256]{1,0:T(8,128)(2,1)S(1)}, bf16[160,256]{1,0:T(8,128)(2,1)S(1)}, u32[]{:S(2)}, u32[]{:S(2)}) %collective-permute-start.10) | collective-permute-done | bytes 81952 | tf_op jit(solution)/shard_map/ppermute | solution.py:484
  38.6 0.0 collective-permute-start.13
  38.6 1.6 %collective-permute-start.12 = (f32[3,3,128]{2,1,0:T(4,128)S(1)}, f32[3,3,128]{2,1,0:T(4,128)S(1)}, u32[]{:S(2)}, u32[]{:S(2)}) collective-permute-start(f32[3,3,128]{2,1,0:T(4,128)S(1)} %sums.1), channel_id=1, source_target_pairs={{0,2},{1,3},{2,0},{3,1},{4,6},{5,7},{6,4},{7,5},{8,10},{9,11},{10,... | collective-permute-start | bytes 13832 | tf_op jit(solution)/shard_map/ppermute | solution.py:579
  40.2 0.3 collective-permute-start.11
  40.5 1.6 %finish.1 = (f32[2,64,1024]{2,1,0:T(8,128)}, f32[2,64,128]{2,1,0:T(8,128)}, f32[2,64,128]{2,1,0:T(8,128)}) custom-call(s32[8]{0:T(128)S(1)} %copy-done.6, f32[3,3,128]{2,1,0:T(4,128)S(1)} %copy-done.5, f32[2,64,1024]{2,1,0:T(8,128)} %get-tuple-element.17.dq_in_ref, f32[128,256]{1,0:T(8,128)S(1)} %get-tuple-element.23.near_ref, ...), custom_call_target="tpu_custom_call", output_to_operand_aliasing={{0}: (2, {})} | custom-call | tf_op jit(solution)/shard_map/finish/pallas_call | solution.py:583
  42.0 0.0 collective-permute-done.13
  42.0 0.3 collective-permute-done.12
  42.3 0.0 collective-permute-done.11
  42.3 0.6 %add_add_fusion = f32[3,3,128]{2,1,0:T(4,128)} fusion(f32[3,3,128]{2,1,0:T(4,128)S(1)} %collective-permute-done.12, f32[3,3,128]{2,1,0:T(4,128)S(1)} %collective-permute-done.13, f32[3,3,128]{2,1,0:T(4,128)S(1)} %sums.1, f32[3,3,128]{2,1,0:T(4,128)S(1)} %collective-permute-done.11), kind=kLoop, calls=%fused_computation | loop fusion | flops 3456 | bytes 23040 | tf_op jit(solution)/shard_map/add | solution.py:600
  (2 shorter events, 0.0 us)
Async XLA Ops:
  0.6 1.0 %copy-start = (bf16[2,64,1024]{2,1,0:T(8,128)(2,1)S(1)}, bf16[2,64,1024]{2,1,0:T(8,128)(2,1)}, u32[]{:S(2)}) copy-start(bf16[2,64,1024]{2,1,0:T(8,128)(2,1)} %q_hbm.1) | copy-start | bytes 786436
  1.6 0.8 %copy-start.3 = (bf16[2,64,128]{2,1,0:T(8,128)(2,1)S(1)}, bf16[2,64,128]{2,1,0:T(8,128)(2,1)}, u32[]{:S(2)}) copy-start(bf16[2,64,128]{2,1,0:T(8,128)(2,1)} %k_ref.1) | copy-start | bytes 98308
  2.3 0.8 %copy-start.4 = (bf16[2,64,128]{2,1,0:T(8,128)(2,1)S(1)}, bf16[2,64,128]{2,1,0:T(8,128)(2,1)}, u32[]{:S(2)}) copy-start(bf16[2,64,128]{2,1,0:T(8,128)(2,1)} %v_ref.1) | copy-start | bytes 98308
  3.1 15.2 %copy-start.1 = (bf16[2,64,1024]{2,1,0:T(8,128)(2,1)S(1)}, bf16[2,64,1024]{2,1,0:T(8,128)(2,1)}, u32[]{:S(2)}) copy-start(bf16[2,64,1024]{2,1,0:T(8,128)(2,1)} %q_hbm.1) | copy-start | bytes 786436
  3.1 15.2 %copy-start.5 = (f32[3,3,128]{2,1,0:T(4,128)S(1)}, f32[3,3,128]{2,1,0:T(4,128)}, u32[]{:S(2)}) copy-start(f32[3,3,128]{2,1,0:T(4,128)} %filters_ref.3) | copy-start | bytes 13828
  3.1 15.2 %copy-start.6 = (s32[8]{0:T(128)S(1)}, s32[8]{0:T(128)}, u32[]{:S(2)}) copy-start(s32[8]{0:T(128)} %lengths_ref.3) | copy-start | bytes 100
  3.1 7.6 %collective-permute-start.3 = (bf16[144,256]{1,0:T(8,128)(2,1)S(1)}, bf16[144,256]{1,0:T(8,128)(2,1)S(1)}, u32[]{:S(2)}, u32[]{:S(2)}) collective-permute-start(bf16[144,256]{1,0:T(8,128)(2,1)S(1)} %pack.1.refs_0_), channel_id=1, source_target_pairs={{0,16},{4,20},{8,24},{12,28},{16,0},{20,4},{24,8},{28,12},{1,17},{... | collective-permute-start | bytes 221192 | tf_op jit(solution)/shard_map/ppermute | solution.py:484
  7.2 6.7 %collective-permute-start.2 = (bf16[144,256]{1,0:T(8,128)(2,1)S(1)}, bf16[144,256]{1,0:T(8,128)(2,1)S(1)}, u32[]{:S(2)}, u32[]{:S(2)}) collective-permute-start(bf16[144,256]{1,0:T(8,128)(2,1)S(1)} %pack.1.refs_0_), channel_id=1, source_target_pairs={{0,12},{4,8},{8,4},{12,0},{16,28},{20,24},{24,20},{28,16},{1,13},{... | collective-permute-start | bytes 221192 | tf_op jit(solution)/shard_map/ppermute | solution.py:484
  9.7 5.2 %collective-permute-start.1 = (bf16[144,256]{1,0:T(8,128)(2,1)S(1)}, bf16[144,256]{1,0:T(8,128)(2,1)S(1)}, u32[]{:S(2)}, u32[]{:S(2)}) collective-permute-start(bf16[144,256]{1,0:T(8,128)(2,1)S(1)} %pack.1.refs_0_), channel_id=1, source_target_pairs={{0,8},{4,12},{8,0},{12,4},{16,24},{20,28},{24,16},{28,20},{1,9},{5... | collective-permute-start | bytes 221192 | tf_op jit(solution)/shard_map/ppermute | solution.py:484
  10.2 5.7 %collective-permute-start = (bf16[144,256]{1,0:T(8,128)(2,1)S(1)}, bf16[144,256]{1,0:T(8,128)(2,1)S(1)}, u32[]{:S(2)}, u32[]{:S(2)}) collective-permute-start(bf16[144,256]{1,0:T(8,128)(2,1)S(1)} %pack.1.refs_0_), channel_id=1, source_target_pairs={{0,4},{4,0},{8,12},{12,8},{16,20},{20,16},{24,28},{28,24},{1,5},{5... | collective-permute-start | bytes 221192 | tf_op jit(solution)/shard_map/ppermute | solution.py:484
  10.7 6.0 %collective-permute-start.6 = (bf16[144,256]{1,0:T(8,128)(2,1)S(1)}, bf16[144,256]{1,0:T(8,128)(2,1)S(1)}, u32[]{:S(2)}, u32[]{:S(2)}) collective-permute-start(bf16[144,256]{1,0:T(8,128)(2,1)S(1)} %collective-permute-done.3.refs_4_), channel_id=1, source_target_pairs={{0,12},{4,8},{8,4},{12,0},{16,28},{20,24},{24,20},{28,16},{1,13},{... | collective-permute-start | bytes 221192 | tf_op jit(solution)/shard_map/ppermute | solution.py:484
  13.2 4.4 %collective-permute-start.5 = (bf16[144,256]{1,0:T(8,128)(2,1)S(1)}, bf16[144,256]{1,0:T(8,128)(2,1)S(1)}, u32[]{:S(2)}, u32[]{:S(2)}) collective-permute-start(bf16[144,256]{1,0:T(8,128)(2,1)S(1)} %collective-permute-done.3.refs_4_), channel_id=1, source_target_pairs={{0,8},{4,12},{8,0},{12,4},{16,24},{20,28},{24,16},{28,20},{1,9},{5... | collective-permute-start | bytes 221192 | tf_op jit(solution)/shard_map/ppermute | solution.py:484
  13.9 4.4 %collective-permute-start.4 = (bf16[144,256]{1,0:T(8,128)(2,1)S(1)}, bf16[144,256]{1,0:T(8,128)(2,1)S(1)}, u32[]{:S(2)}, u32[]{:S(2)}) collective-permute-start(bf16[144,256]{1,0:T(8,128)(2,1)S(1)} %collective-permute-done.3.refs_4_), channel_id=1, source_target_pairs={{0,4},{4,0},{8,12},{12,8},{16,20},{20,16},{24,28},{28,24},{1,5},{5... | collective-permute-start | bytes 221192 | tf_op jit(solution)/shard_map/ppermute | solution.py:484
  18.3 1.0 %copy-start.2 = (bf16[2,64,1024]{2,1,0:T(8,128)(2,1)S(1)}, bf16[2,64,1024]{2,1,0:T(8,128)(2,1)}, u32[]{:S(2)}) copy-start(bf16[2,64,1024]{2,1,0:T(8,128)(2,1)} %d_out_hbm.1) | copy-start | bytes 786436
  25.5 7.5 %collective-permute-start.7 = (bf16[224,256]{1,0:T(8,128)(2,1)S(1)}, bf16[224,256]{1,0:T(8,128)(2,1)S(1)}, u32[]{:S(2)}, u32[]{:S(2)}) collective-permute-start(bf16[224,256]{1,0:T(8,128)(2,1)S(1)} %get-tuple-element.20), channel_id=1, source_target_pairs={{0,4},{4,0},{8,12},{12,8},{16,20},{20,16},{24,28},{28,24},{1,5},{5... | collective-permute-start | bytes 344072 | tf_op jit(solution)/shard_map/ppermute | solution.py:484
  26.5 6.6 %collective-permute-start.9 = (bf16[224,256]{1,0:T(8,128)(2,1)S(1)}, bf16[224,256]{1,0:T(8,128)(2,1)S(1)}, u32[]{:S(2)}, u32[]{:S(2)}) collective-permute-start(bf16[224,256]{1,0:T(8,128)(2,1)S(1)} %get-tuple-element.22), channel_id=1, source_target_pairs={{0,12},{4,8},{8,4},{12,0},{16,28},{20,24},{24,20},{28,16},{1,13},{... | collective-permute-start | bytes 344072 | tf_op jit(solution)/shard_map/ppermute | solution.py:484
  28.3 4.7 %collective-permute-start.8 = (bf16[208,256]{1,0:T(8,128)(2,1)S(1)}, bf16[208,256]{1,0:T(8,128)(2,1)S(1)}, u32[]{:S(2)}, u32[]{:S(2)}) collective-permute-start(bf16[208,256]{1,0:T(8,128)(2,1)S(1)} %get-tuple-element.21), channel_id=1, source_target_pairs={{0,8},{4,12},{8,0},{12,4},{16,24},{20,28},{24,16},{28,20},{1,9},{5... | collective-permute-start | bytes 319496 | tf_op jit(solution)/shard_map/ppermute | solution.py:484
  33.2 5.4 %collective-permute-start.10 = (bf16[160,256]{1,0:T(8,128)(2,1)S(1)}, bf16[160,256]{1,0:T(8,128)(2,1)S(1)}, u32[]{:S(2)}, u32[]{:S(2)}) collective-permute-start(bf16[160,256]{1,0:T(8,128)(2,1)S(1)} %get-tuple-element.24), channel_id=1, source_target_pairs={{0,16},{4,20},{8,24},{12,28},{16,0},{20,4},{24,8},{28,12},{1,17},{... | collective-permute-start | bytes 245768 | tf_op jit(solution)/shard_map/ppermute | solution.py:484
  38.6 3.4 %collective-permute-start.13 = (f32[3,3,128]{2,1,0:T(4,128)S(1)}, f32[3,3,128]{2,1,0:T(4,128)S(1)}, u32[]{:S(2)}, u32[]{:S(2)}) collective-permute-start(f32[3,3,128]{2,1,0:T(4,128)S(1)} %sums.1), channel_id=1, source_target_pairs={{0,3},{1,2},{2,1},{3,0},{4,7},{5,6},{6,5},{7,4},{8,11},{9,10},{10,... | collective-permute-start | bytes 13832 | tf_op jit(solution)/shard_map/ppermute | solution.py:579
  38.6 3.7 %collective-permute-start.12 = (f32[3,3,128]{2,1,0:T(4,128)S(1)}, f32[3,3,128]{2,1,0:T(4,128)S(1)}, u32[]{:S(2)}, u32[]{:S(2)}) collective-permute-start(f32[3,3,128]{2,1,0:T(4,128)S(1)} %sums.1), channel_id=1, source_target_pairs={{0,2},{1,3},{2,0},{3,1},{4,6},{5,7},{6,4},{7,5},{8,10},{9,11},{10,... | collective-permute-start | bytes 13832 | tf_op jit(solution)/shard_map/ppermute | solution.py:579
  40.2 2.1 %collective-permute-start.11 = (f32[3,3,128]{2,1,0:T(4,128)S(1)}, f32[3,3,128]{2,1,0:T(4,128)S(1)}, u32[]{:S(2)}, u32[]{:S(2)}) collective-permute-start(f32[3,3,128]{2,1,0:T(4,128)S(1)} %sums.1), channel_id=1, source_target_pairs={{0,1},{1,0},{2,3},{3,2},{4,5},{5,4},{6,7},{7,6},{8,9},{9,8},{10,11... | collective-permute-start | bytes 13832 | tf_op jit(solution)/shard_map/ppermute | solution.py:579
where the time goes:
time: 43.4 us; the launch traced here: 42.9 us
  starting transfers between devices  20.1 us (46%)
  waiting for transfers between devices  10.2 us (24%)
  Pallas kernels  7.95 us (18%)
  local copies, waits for them, and re-layouts  3.41 us (8%)
  between operations  0.69 us (2%)
  other arithmetic  0.6 us (1%)
    ppermute x11, starting transfers between devices, flipped(): return lax.ppermute(array, 'ctx', [(i, i ^ flip) for i in range(ctx_count)])  18.2 us
    ppermute x11, waiting for transfers between devices, flipped(): return lax.ppermute(array, 'ctx', [(i, i ^ flip) for i in range(ctx_count)])  9.92 us
    pallas_call x1, Pallas kernels, shards(): pl.pallas_call(functools.partial(grads_kernel, ctx_count, direct), out_sh...  6.23 us
    unnamed x14, local copies, waits for them, and re-layouts  3.41 us
    ppermute x3, starting transfers between devices, shards(): lax.ppermute(sums, 'tp', [(i, i ^ flip) for i in range(count)])  1.86 us
    pallas_call x1, Pallas kernels, shards(): pl.pallas_call(functools.partial(finish_kernel, ctx_count), grid=(1,), ou...  1.57 us
  transfers between devices with their start and end apart: 14, of which 8 were waited for; matrix products, arithmetic and copies ran while one was open for 0% of the time, Pallas kernels for 4%

commit v1 on v0

--- a/solution.py
+++ b/solution.py
@@ -84,11 +84,11 @@
     group = ctx_count // 2
     arrays = group if direct else 1
     near_in, far_in, refs = refs[:arrays], refs[arrays : 2 * arrays], refs[2 * arrays :]
-    dq_hbm, own_near_ref, own_far_ref = refs[:3]
+    dq_hbm, dq_tail_ref, own_near_ref, own_far_ref = refs[:4]
     arrays = group - 1 if direct else 1
-    out_refs, refs = refs[3 : 3 + arrays], refs[3 + arrays :]
-    same_scr, kv_scr, conv_scr, dkv_scr, q_scr, qc_scr, do_scr, dq_scr = refs[:8]
-    s_scr, dp_scr, rim_scr, q_ref, d_out_ref, dq_ref, sems = refs[8:]
+    out_refs, refs = refs[4 : 4 + arrays], refs[4 + arrays :]
+    same_scr, same_two_scr, kv_scr, conv_scr, dkv_scr, q_scr, qc_scr, do_scr, dq_scr = refs[:9]
+    bias_scr, s_scr, dp_scr, rim_scr, q_ref, d_out_ref, dq_ref, sems = refs[9:]
     f32, bf16 = jnp.float32, jnp.bfloat16
     loads = [
         pltpu.make_async_copy(q_hbm, q_ref, sems.at[0]),
@@ -108,20 +108,23 @@
     log2_scale = scale * 1.4426950408889634
     starts = doc_starts(lengths_ref)
 
-    def fill_same(index, carry):
-        place = index * span + lax.broadcasted_iota(jnp.int32, (span, LANES), 0)
-        cut = place == starts[0]
-        for start in starts[1:]:
-            cut = cut | (place == start)
-        same_scr[pl.ds(aligned(8 + index * span, 8), span)] = jnp.where(cut, 0.0, 1.0)
+    def fill(index, carry):
+        rows = pl.ds(aligned(8 + index * span, 8), span)
+        same_scr[rows] = jnp.ones((span, LANES), f32)
+        same_two_scr[rows] = jnp.ones((span, LANES), f32)
         return carry
 
-    same_scr[:8] = jnp.zeros((8, LANES), f32)
-    same_scr[8 + length :] = jnp.zeros((8, LANES), f32)
-    loop(blocks, fill_same, 0)
-
-    kv_scr[:8] = jnp.zeros((8, 2 * LANES), f32)
-    kv_scr[8 + length :] = jnp.zeros((8, 2 * LANES), f32)
+    loop(blocks, fill, 0)
+    zeros = jnp.zeros((8, LANES), f32)
+    for rows in (slice(0, 8), slice(8 + length, 16 + length)):
+        same_scr[rows] = zeros
+        same_two_scr[rows] = zeros
+        for tensor in range(2):
+            kv_scr[tensor, rows] = zeros
+    for start in starts:
+        same_scr[pl.ds(8 + start, 1)] = zeros[:1]
+        same_two_scr[pl.ds(8 + start, 1)] = zeros[:1]
+        same_two_scr[pl.ds(9 + start, 1)] = zeros[:1]
 
     def place_blocks(flip, carry):
         for message, index in (
@@ -130,31 +133,31 @@
         ):
             early = aligned(8 + index * span, 8)
             late = aligned(8 + (blocks - 1 - index) * span, 8)
-            kv_scr[pl.ds(early, span)] = message[:span].astype(f32)
-            kv_scr[pl.ds(late, span)] = message[span : 2 * span].astype(f32)
+            for tensor in range(2):
+                lanes = slice(tensor * LANES, (tensor + 1) * LANES)
+                kv_scr[tensor, pl.ds(early, span)] = message[:span, lanes].astype(f32)
+                kv_scr[tensor, pl.ds(late, span)] = message[span : 2 * span, lanes].astype(f32)
             rim_scr[index] = message[2 * span :].astype(f32)
         return carry
 
     loop(group, place_blocks, 0)
 
-    def kv_taps(tap):
-        return jnp.concatenate([filters_ref[1, tap : tap + 1], filters_ref[2, tap : tap + 1]], axis=1)
-
-    def twice(mask):
-        return jnp.concatenate([mask, mask], axis=1)
-
-    def back_masks(same, first):
-        one = same[first : first + span]
-        return one, one * same[first - 1 : first - 1 + span]
+    def taps(tensor):
+        return [filters_ref[tensor, tap : tap + 1] for tap in range(3)]
+
+    def masks(base, ahead):
+        one = same_scr[pl.ds(base + 8 + min(ahead, 1), span)]
+        return one, same_two_scr[pl.ds(base + 8 + ahead, span)]
 
     def convolve_kv(index, carry):
-        rows = pl.ds(aligned(index * span, 8), span + 8)
-        values = kv_scr[rows]
-        one, two = back_masks(same_scr[rows], 8)
-        total = kv_taps(0) * values[8:]
-        total = total + twice(one) * (kv_taps(1) * values[7 : 7 + span])
-        total = total + twice(two) * (kv_taps(2) * values[6 : 6 + span])
-        conv_scr[pl.ds(aligned(index * span, 16), span)] = total.astype(bf16)
+        base = index * span
+        one, two = masks(base, 0)
+        for tensor in range(2):
+            zero_tap, one_tap, two_tap = taps(tensor + 1)
+            total = zero_tap * kv_scr[tensor, pl.ds(aligned(base + 8, 8), span)]
+            total = total + one * (one_tap * kv_scr[tensor, pl.ds(base + 7, span)])
+            total = total + two * (two_tap * kv_scr[tensor, pl.ds(base + 6, span)])
+            conv_scr[tensor, pl.ds(aligned(base, 16), span)] = total.astype(bf16)
         return carry
 
     loop(blocks, convolve_kv, 0)
@@ -170,16 +173,16 @@
     for load in loads:
         load.wait()
     for half in range(2):
-        rows = [rims[half][2 * at : 2 * at + 2] for at in range(rim_rows // 2)]
-        q_scr[half, 6:8] = jnp.concatenate(rows, axis=1)
-        q_scr[half, 8:] = q_ref[half].astype(f32)
-        same = same_scr[pl.ds(aligned(first_place[half], 8), span + 16)]
-        one, two = back_masks(same, 8)
+        one, two = masks(first_place[half], 0)
+        zero_tap, one_tap, two_tap = taps(0)
         for head in range(heads):
             lanes = slice(head * LANES, (head + 1) * LANES)
-            total = filters_ref[0, 0:1] * q_scr[half, 8:, lanes]
-            total = total + one * (filters_ref[0, 1:2] * q_scr[half, 7 : 7 + span, lanes])
-            total = total + two * (filters_ref[0, 2:3] * q_scr[half, 6 : 6 + span, lanes])
+            at = 2 * (head // 2)
+            q_scr[half, head, 6:8] = rims[half][at : at + 2, (head % 2) * LANES : (head % 2 + 1) * LANES]
+            q_scr[half, head, 8:] = q_ref[half, :, lanes].astype(f32)
+            total = zero_tap * q_scr[half, head, 8:]
+            total = total + one * (one_tap * q_scr[half, head, 7 : 7 + span])
+            total = total + two * (two_tap * q_scr[half, head, 6 : 6 + span])
             qc_scr[half, head * span : (head + 1) * span] = total.astype(bf16)
             do_scr[half, head * span : (head + 1) * span] = d_out_ref[half, :, lanes]
 
@@ -195,8 +198,16 @@
         for start in starts[1:]:
             lowest = jnp.where(query >= start, start, lowest)
         wide = 2 * LANES
+
+        def fill_bias(step, carry):
+            places = first_key + step * size + lax.broadcasted_iota(jnp.int32, (size, LANES), 0)
+            allowed = (places >= lowest) & (places <= query)
+            bias_scr[pl.ds(aligned(step * size, 16), size)] = jnp.where(allowed, 0.0, -1e30)
+            return carry
+
+        loop(chunks, fill_bias, 0, 1)
         whole_window = pl.ds(aligned(first_key, 16), window)
-        keys_t = conv_scr[whole_window, :LANES].T if chunks == 1 else None
+        keys_t = conv_scr[0, whole_window].T if chunks == 1 else None
         for at in range(heads * span // wide):
             slot = (half * (heads * span // wide) + at) % s_scr.shape[0]
             cols = slice(at * wide, (at + 1) * wide)
@@ -207,12 +218,10 @@
                 return pl.ds(aligned(first_key + step * size, 16), size)
 
             def score(step, top):
-                places = first_key + step * size + lax.broadcasted_iota(jnp.int32, (size, LANES), 0)
-                allowed = (places >= lowest) & (places <= query)
-                bias = jnp.where(allowed, 0.0, -1e30)
-                keys = conv_scr[key_rows(step), :LANES]
+                keys = conv_scr[0, key_rows(step)]
                 scores = lax.dot_general(keys, queries, NT, preferred_element_type=f32)
-                scores = scores + twice(bias)
+                bias = bias_scr[pl.ds(aligned(step * size, 16), size)]
+                scores = scores + jnp.concatenate([bias, bias], axis=1)
                 s_scr[slot, pl.ds(aligned(step * size, 16), size)] = scores
                 return jnp.maximum(top, jnp.max(scores, axis=0, keepdims=True))
 
@@ -222,7 +231,7 @@
                 total, weighted = carry
                 rows = pl.ds(aligned(step * size, 16), size)
                 weights = jnp.exp2((s_scr[slot, rows] - top) * log2_scale)
-                values = conv_scr[key_rows(step), LANES:]
+                values = conv_scr[1, key_rows(step)]
                 prob_grads = lax.dot_general(values, grads, NT, preferred_element_type=f32)
                 s_scr[slot, rows] = weights
                 dp_scr[slot, rows] = prob_grads
@@ -243,74 +252,71 @@
                 score_grads = (weights * slope * (dp_scr[slot, rows] - mean)).astype(bf16)
                 dk = lax.dot_general(score_grads, queries, NN, preferred_element_type=f32)
                 dv = lax.dot_general(probs, grads, NN, preferred_element_type=f32)
-                terms = jnp.concatenate([dk, dv], axis=1)
                 target = pl.ds(aligned(first_key + step * size, 16), size)
-                if add or at:
-                    dkv_scr[target] += terms
-                else:
-                    dkv_scr[target] = terms
+                for tensor, terms in enumerate((dk, dv)):
+                    if add or at:
+                        dkv_scr[tensor, target] += terms
+                    else:
+                        dkv_scr[tensor, target] = terms
                 if keys_t is not None:
                     return lax.dot_general(keys_t, score_grads, NN, preferred_element_type=f32)
-                keys = conv_scr[key_rows(step), :LANES]
+                keys = conv_scr[0, key_rows(step)]
                 return dq + lax.dot_general(keys, score_grads, TN, preferred_element_type=f32)
 
             dq = loop(chunks, accumulate, jnp.zeros((LANES, wide), f32), 1)
             dq = dq.T
             for part in range(wide // span):
                 head = at * (wide // span) + part
-                dq_scr[half, :span, head * LANES : (head + 1) * LANES] = dq[
-                    part * span : (part + 1) * span
-                ]
-
-    dkv_scr[half_rows:] = jnp.zeros((half_rows + 8, 2 * LANES), f32)
+                dq_scr[half, head, :span] = dq[part * span : (part + 1) * span]
+
+    for tensor in range(2):
+        dkv_scr[tensor, half_rows:] = jnp.zeros((half_rows + 8, LANES), f32)
     attend(0, half_rows, 0, False)
     attend(1, half_rows + span, (ctx_count - 1 - me) * span, True)
 
-    next_rows = jnp.where(middle, dq_scr[1, :8], 0.0)
-    dq_scr[0, span:] = next_rows
-    dq_scr[1, span:] = jnp.zeros_like(next_rows)
+    next_rows = jnp.where(middle, dq_scr[1, :, :8], 0.0)
+    dq_scr[0, :, span:] = next_rows
+    dq_scr[1, :, span:] = jnp.zeros_like(next_rows)
     sums = [jnp.zeros((8, LANES), f32) for _ in range(3)]
     for half in range(2):
-        same = same_scr[pl.ds(aligned(first_place[half], 8), span + 16)]
-        one, two = back_masks(same, 8)
-        ahead_one = same[9 : 9 + span]
-        ahead_two = same[10 : 10 + span] * ahead_one
+        one, two = masks(first_place[half], 0)
+        ahead_one = same_scr[pl.ds(first_place[half] + 9, span)]
+        ahead_two = same_two_scr[pl.ds(first_place[half] + 10, span)]
+        zero_tap, one_tap, two_tap = taps(0)
         for head in range(heads):
             lanes = slice(head * LANES, (head + 1) * LANES)
-            grads = dq_scr[half, :span, lanes]
-            out = filters_ref[0, 0:1] * grads
-            out = out + ahead_one * (filters_ref[0, 1:2] * dq_scr[half, 1 : 1 + span, lanes])
-            out = out + ahead_two * (filters_ref[0, 2:3] * dq_scr[half, 2 : 2 + span, lanes])
+            grads = dq_scr[half, head, :span]
+            out = zero_tap * grads
+            out = out + ahead_one * (one_tap * dq_scr[half, head, 1 : 1 + span])
+            out = out + ahead_two * (two_tap * dq_scr[half, head, 2 : 2 + span])
             dq_ref[half, :, lanes] = out
-            sums[0] += fold_rows(grads * q_scr[half, 8:, lanes])
-            sums[1] += fold_rows(grads * one * q_scr[half, 7 : 7 + span, lanes])
-            sums[2] += fold_rows(grads * two * q_scr[half, 6 : 6 + span, lanes])
+            dq_tail_ref[half, :, lanes] = out[span - 8 :]
+            sums[0] += fold_rows(grads * q_scr[half, head, 8:])
+            sums[1] += fold_rows(grads * one * q_scr[half, head, 7 : 7 + span])
+            sums[2] += fold_rows(grads * two * q_scr[half, head, 6 : 6 + span])
     q_sums = [jnp.sum(term, axis=0, keepdims=True) for term in sums]
     store = pltpu.make_async_copy(dq_ref, dq_hbm, sems.at[2])
     store.start()
 
-    def finish_block(index, carry):
-        base = aligned(index * span, 8)
-        grads = dkv_scr[pl.ds(base, span + 8)]
-        values = kv_scr[pl.ds(base, span + 8)]
-        same = same_scr[pl.ds(base, span + 16)]
-        one, two = back_masks(same, 8)
-        ahead_one = same[9 : 9 + span]
-        ahead_two = same[10 : 10 + span] * ahead_one
-        out = kv_taps(0) * grads[:span]
-        out = out + twice(ahead_one) * (kv_taps(1) * grads[1 : 1 + span])
-        out = out + twice(ahead_two) * (kv_taps(2) * grads[2 : 2 + span])
-        own = grads[:span]
-        return out, (
-            carry[0] + fold_rows(own * values[8:]),
-            carry[1] + fold_rows(own * twice(one) * values[7 : 7 + span]),
-            carry[2] + fold_rows(own * twice(two) * values[6 : 6 + span]),
-        )
-
-    def finish_pair(index, carry):
-        early, carry = finish_block(index, carry)
-        late, carry = finish_block(blocks - 1 - index, carry)
-        return jnp.concatenate([early, late], axis=0), carry
+    def finish_block(index, carry, target, row):
+        base = pl.multiple_of(index * span, 8)
+        one, two = masks(base, 0)
+        ahead_one = same_scr[pl.ds(base + 9, span)]
+        ahead_two = same_two_scr[pl.ds(base + 10, span)]
+        carry = list(carry)
+        for tensor in range(2):
+            zero_tap, one_tap, two_tap = taps(tensor + 1)
+            own = dkv_scr[tensor, pl.ds(base, span)]
+            out = zero_tap * own
+            out = out + ahead_one * (one_tap * dkv_scr[tensor, pl.ds(base + 1, span)])
+            out = out + ahead_two * (two_tap * dkv_scr[tensor, pl.ds(base + 2, span)])
+            lanes = slice(tensor * LANES, (tensor + 1) * LANES)
+            target[row : row + span, lanes] = out.astype(target.dtype)
+            at = 3 * tensor
+            carry[at] += fold_rows(own * kv_scr[tensor, pl.ds(base + 8, span)])
+            carry[at + 1] += fold_rows(own * one * kv_scr[tensor, pl.ds(base + 7, span)])
+            carry[at + 2] += fold_rows(own * two * kv_scr[tensor, pl.ds(base + 6, span)])
+        return tuple(carry)
 
     low = me < group
 
@@ -325,28 +331,26 @@
             jnp.where(low & (me > owner), owner, near_late),
         ]
         for at, place in enumerate(places):
-            terms, carry = finish_block(place, carry)
-            sent[flip][at * span : (at + 1) * span] = terms.astype(bf16)
+            carry = finish_block(place, carry, sent[flip], at * span)
         return carry
 
-    zeros = jnp.zeros((8, 2 * LANES), f32)
-    own_far_ref[: 2 * span], kv_sums = finish_pair(partner(me, group), (zeros, zeros, zeros))
-    own_near_ref[...], kv_sums = finish_pair(me, kv_sums)
+    kv_sums = (zeros,) * 6
+    for target, index in ((own_far_ref, partner(me, group)), (own_near_ref, me)):
+        kv_sums = finish_block(index, kv_sums, target, 0)
+        kv_sums = finish_block(blocks - 1 - index, kv_sums, target, span)
     kv_sums = loop(group - 1, finish, kv_sums)
     kv_sums = [jnp.sum(term, axis=0, keepdims=True) for term in kv_sums]
 
-    sums_tile = jnp.concatenate(
-        [jnp.concatenate([term, jnp.zeros_like(term)], axis=1) for term in q_sums]
-        + kv_sums
-        + [jnp.zeros((2, 2 * LANES), f32)],
-        axis=0,
-    )
+    padding = [jnp.zeros((2, LANES), f32)]
+    left = jnp.concatenate(q_sums + kv_sums[:3] + padding, axis=0)
+    right = jnp.concatenate([jnp.zeros((3, LANES), f32)] + kv_sums[3:] + padding, axis=0)
+    sums_tile = jnp.concatenate([left, right], axis=1)
     sums_pair = jnp.concatenate(split_bits(sums_tile), axis=0)
     own_far_ref[2 * span :] = joined(sums_pair)
     rims = []
     for half in range(2):
-        rows = dq_scr[half, :2]
-        rows = [rows[:, at : at + 2 * LANES] for at in range(0, rows.shape[1], 2 * LANES)]
+        rows = [dq_scr[half, head, :2] for head in range(heads)]
+        rows = [jnp.concatenate(rows[at : at + 2], axis=1) for at in range(0, heads, 2)]
         rims.append(jnp.concatenate(rows, axis=0))
 
     def rim_for(index):
@@ -423,8 +427,9 @@
 
 
 def finish_kernel(
-    ctx_count, lengths_ref, filters_ref, dq_in_ref, near_ref, far_ref, rims_ref, dq_ref, dk_ref, dv_ref
+    ctx_count, lengths_ref, filters_ref, dq_in_hbm, tail_ref, near_ref, far_ref, rims_ref, *refs
 ):
+    dq_hbm, dk_hbm, dv_hbm, dq_ref, dk_ref, dv_ref, sems = refs
     f32 = jnp.float32
     group = ctx_count // 2
     span = dk_ref.shape[1]
@@ -436,6 +441,13 @@
     for half in range(2):
         dk_ref[half] = total[half * span : (half + 1) * span, :LANES]
         dv_ref[half] = total[half * span : (half + 1) * span, LANES:]
+    stores = [
+        pltpu.make_async_copy(dk_ref, dk_hbm, sems.at[0]),
+        pltpu.make_async_copy(dv_ref, dv_hbm, sems.at[1]),
+        pltpu.make_async_copy(dq_ref, dq_hbm.at[:, pl.ds(span - 8, 8)], sems.at[2]),
+    ]
+    for store in stores[:2]:
+        store.start()
 
     def same(place):
         cut = place >= blocks * span
@@ -459,7 +471,10 @@
         last_but_one = (zero * one) * (taps[2] * rows[0:1])
         last = one * (taps[1] * rows[0:1]) + (one * two) * (taps[2] * rows[1:2])
         extra = jnp.where(row == 6, last_but_one, jnp.where(row == 7, last, 0.0))
-        dq_ref[half] = dq_in_ref[half] + extra
+        dq_ref[half] = tail_ref[half] + extra
+    stores[2].start()
+    for store in stores:
+        store.wait()
 
 
 def shards(q_pre, k_pre, value_before_filter, d_out, filters, doc_lengths):
@@ -479,6 +494,9 @@
 
     def whole(shape):
         return pl.BlockSpec(shape, lambda i: (0,) * len(shape))
+
+    def in_hbm(array):
+        return pltpu.with_memory_space_constraint(array, pltpu.HBM)
 
     def flipped(array, flip):
         return lax.ppermute(array, "ctx", [(i, i ^ flip) for i in range(ctx_count)])
@@ -505,7 +523,7 @@
         out_specs=whole((msg_rows, 2 * LANES)),
         compiler_params=pltpu.CompilerParams(vmem_limit_bytes=4 * MIB),
         name="pack",
-    )(k_pre, value_before_filter, q_pre)
+    )(*[in_hbm(array) for array in (k_pre, value_before_filter, q_pre)])
     across = flipped(packed, group)
     received = gathered(packed) + gathered(across)
 
@@ -516,17 +534,21 @@
         ]
     else:
         sent_shapes = [(group, 3 * span + 32, 2 * LANES)]
+    slots = 4 if direct else 1
+    heads = width // LANES
     scratch = [
         pltpu.VMEM((length + 16, LANES), f32),
-        pltpu.VMEM((length + 16, 2 * LANES), f32),
-        pltpu.VMEM((length, 2 * LANES), bf16),
-        pltpu.VMEM((length + 8, 2 * LANES), f32),
-        pltpu.VMEM((2, span + 8, width), f32),
-        pltpu.VMEM((2, span * width // LANES, LANES), bf16),
-        pltpu.VMEM((2, span * width // LANES, LANES), bf16),
-        pltpu.VMEM((2, span + 8, width), f32),
-        pltpu.VMEM((4 if direct else 1, window, 2 * LANES), f32),
-        pltpu.VMEM((4 if direct else 1, window, 2 * LANES), f32),
+        pltpu.VMEM((length + 16, LANES), f32),
+        pltpu.VMEM((2, length + 16, LANES), f32),
+        pltpu.VMEM((2, length, LANES), bf16),
+        pltpu.VMEM((2, length + 8, LANES), f32),
+        pltpu.VMEM((2, heads, span + 8, LANES), f32),
+        pltpu.VMEM((2, span * heads, LANES), bf16),
+        pltpu.VMEM((2, span * heads, LANES), bf16),
+        pltpu.VMEM((2, heads, span + 8, LANES), f32),
+        pltpu.VMEM((window, LANES), f32),
+        pltpu.VMEM((slots, window, 2 * LANES), f32),
+        pltpu.VMEM((slots, window, 2 * LANES), f32),
         pltpu.VMEM((ctx_count, rim, 2 * LANES), f32),
         pltpu.VMEM(q_pre.shape, bf16),
         pltpu.VMEM(q_pre.shape, bf16),
@@ -534,17 +556,17 @@
         pltpu.SemaphoreType.DMA((3,)),
     ]
     own_shapes = [(2 * span, 2 * LANES), (2 * span + 8, 2 * LANES)]
-    d_q_main, own_near, own_far, *sent = pl.pallas_call(
+    d_q_main, d_q_tail, own_near, own_far, *sent = pl.pallas_call(
         functools.partial(grads_kernel, ctx_count, direct),
         out_shape=[jax.ShapeDtypeStruct(q_pre.shape, f32)]
-        + [jax.ShapeDtypeStruct(shape, f32) for shape in own_shapes]
+        + [jax.ShapeDtypeStruct(shape, f32) for shape in [(2, 8, width)] + own_shapes]
         + [jax.ShapeDtypeStruct(shape, bf16) for shape in sent_shapes],
         in_specs=[smem, vmem, hbm, hbm] + [vmem] * len(received),
-        out_specs=[hbm] + [vmem] * (2 + len(sent_shapes)),
+        out_specs=[hbm] + [vmem] * (3 + len(sent_shapes)),
         scratch_shapes=scratch,
         compiler_params=pltpu.CompilerParams(vmem_limit_bytes=(20 if direct else 62) * MIB),
         name="grads",
-    )(doc_lengths, filters, q_pre, d_out, *received)
+    )(doc_lengths, filters, in_hbm(q_pre), in_hbm(d_out), *received)
     half_terms = delivered(sent)
     merged_shapes = [
         jax.ShapeDtypeStruct((2 * span, 2 * LANES), f32),
@@ -579,22 +601,25 @@
         lax.ppermute(sums, "tp", [(i, i ^ flip) for i in range(count)]) for flip in range(1, count)
     ]
 
-    last_rows = pl.BlockSpec((2, 8, width), lambda i: (0, span // 8 - 1, 0))
     d_q_pre, d_k_pre, d_v_pre = pl.pallas_call(
         functools.partial(finish_kernel, ctx_count),
-        grid=(1,),
         out_shape=(
             jax.ShapeDtypeStruct(q_pre.shape, f32),
             jax.ShapeDtypeStruct(k_pre.shape, f32),
             jax.ShapeDtypeStruct(k_pre.shape, f32),
         ),
-        in_specs=[smem, whole(filters.shape), last_rows]
-        + [whole(array.shape) for array in (near, from_half, rims)],
-        out_specs=(last_rows, whole(k_pre.shape), whole(k_pre.shape)),
+        in_specs=[smem, vmem, hbm, vmem, vmem, vmem, vmem],
+        out_specs=(hbm, hbm, hbm),
+        scratch_shapes=[
+            pltpu.VMEM((2, 8, width), f32),
+            pltpu.VMEM(k_pre.shape, f32),
+            pltpu.VMEM(k_pre.shape, f32),
+            pltpu.SemaphoreType.DMA((3,)),
+        ],
         input_output_aliases={2: 0},
         compiler_params=pltpu.CompilerParams(vmem_limit_bytes=4 * MIB),
         name="finish",
-    )(doc_lengths, filters, d_q_main, near, from_half, rims)
+    )(doc_lengths, filters, d_q_main, d_q_tail, near, from_half, rims)
 
     while len(level) > 1:
         level = [level[at] + level[at + 1] for at in range(0, len(level), 2)]

time: 43.4 us -> 40.4 us (0.931)
  local copies, waits for them, and re-layouts: 3.41 us -> 0.01 us
    unnamed x14 -> x4, local copies, waits for them, and re-layouts: 3.41 us -> 0.01 us
    pallas_call x1, Pallas kernels: 0.02 us -> 0.91 us  [shards(): pl.pallas_call(pack_kernel, grid=(1,), out_shape=jax.ShapeDtypeStruct((ms...]
  transfers between devices with their start and end apart: 14 -> 14, of which waited for: 8 -> 8; matrix products, arithmetic and copies ran while one was open for 0% -> 0% of each run, Pallas kernels for 4% -> 3%
where the time goes in v1:
time: 40.4 us; the launch traced here: 40 us
  starting transfers between devices  20.1 us (50%)
  waiting for transfers between devices  10.5 us (26%)
  Pallas kernels  8.17 us (20%)
  between operations  0.69 us (2%)
  other arithmetic  0.6 us (1%)
    ppermute x11, starting transfers between devices, flipped(): return lax.ppermute(array, 'ctx', [(i, i ^ flip) for i in range(ctx_count)])  18.2 us
    ppermute x11, waiting for transfers between devices, flipped(): return lax.ppermute(array, 'ctx', [(i, i ^ flip) for i in range(ctx_count)])  9.9 us
    pallas_call x1, Pallas kernels, shards(): pl.pallas_call(functools.partial(grads_kernel, ctx_count, direct), out_sh...  5.87 us
    ppermute x3, starting transfers between devices, shards(): lax.ppermute(sums, 'tp', [(i, i ^ flip) for i in range(count)])  1.86 us
    pallas_call x1, Pallas kernels, shards(): pl.pallas_call(functools.partial(finish_kernel, ctx_count), out_shape=(ja...  1.26 us
    pallas_call x1, Pallas kernels, shards(): pl.pallas_call(pack_kernel, grid=(1,), out_shape=jax.ShapeDtypeStruct((ms...  0.91 us
  transfers between devices with their start and end apart: 14, of which 8 were waited for; matrix products, arithmetic and copies ran while one was open for 0% of the time, Pallas kernels for 3%

profile of v1, /device:TPU:0, one launch (start us, length us, event | category | flops | bytes accessed | tf_op | source)
XLA Modules:
  0.0 40.0 jit_solution(766461200586758239)
XLA Ops:
  0.6 0.0 copy-start.1
  0.6 0.0 copy-start
  0.7 0.9 %pack.1.refs_0_ = bf16[144,256]{1,0:T(8,128)(2,1)S(1)} custom-call(bf16[2,64,128]{2,1,0:T(8,128)(2,1)} %k_ref.1, bf16[2,64,128]{2,1,0:T(8,128)(2,1)} %v_ref.1, bf16[2,64,1024]{2,1,0:T(8,128)(2,1)} %q_hbm.1), custom_call_target="tpu_custom_call" | custom-call | tf_op jit(solution)/shard_map/pack/pallas_call | solution.py:514
  1.6 4.1 %collective-permute-start.3 = (bf16[144,256]{1,0:T(8,128)(2,1)S(1)}, bf16[144,256]{1,0:T(8,128)(2,1)S(1)}, u32[]{:S(2)}, u32[]{:S(2)}) collective-permute-start(bf16[144,256]{1,0:T(8,128)(2,1)S(1)} %pack.1.refs_0_), channel_id=1, source_target_pairs={{0,16},{4,20},{8,24},{12,28},{16,0},{20,4},{24,8},{28,12},{1,17},{... | collective-permute-start | bytes 221192 | tf_op jit(solution)/shard_map/ppermute | solution.py:502
  5.7 2.5 %collective-permute-start.2 = (bf16[144,256]{1,0:T(8,128)(2,1)S(1)}, bf16[144,256]{1,0:T(8,128)(2,1)S(1)}, u32[]{:S(2)}, u32[]{:S(2)}) collective-permute-start(bf16[144,256]{1,0:T(8,128)(2,1)S(1)} %pack.1.refs_0_), channel_id=1, source_target_pairs={{0,12},{4,8},{8,4},{12,0},{16,28},{20,24},{24,20},{28,16},{1,13},{... | collective-permute-start | bytes 221192 | tf_op jit(solution)/shard_map/ppermute | solution.py:502
  8.2 0.4 %collective-permute-start.1 = (bf16[144,256]{1,0:T(8,128)(2,1)S(1)}, bf16[144,256]{1,0:T(8,128)(2,1)S(1)}, u32[]{:S(2)}, u32[]{:S(2)}) collective-permute-start(bf16[144,256]{1,0:T(8,128)(2,1)S(1)} %pack.1.refs_0_), channel_id=1, source_target_pairs={{0,8},{4,12},{8,0},{12,4},{16,24},{20,28},{24,16},{28,20},{1,9},{5... | collective-permute-start | bytes 221192 | tf_op jit(solution)/shard_map/ppermute | solution.py:502
  8.6 0.5 %collective-permute-start = (bf16[144,256]{1,0:T(8,128)(2,1)S(1)}, bf16[144,256]{1,0:T(8,128)(2,1)S(1)}, u32[]{:S(2)}, u32[]{:S(2)}) collective-permute-start(bf16[144,256]{1,0:T(8,128)(2,1)S(1)} %pack.1.refs_0_), channel_id=1, source_target_pairs={{0,4},{4,0},{8,12},{12,8},{16,20},{20,16},{24,28},{28,24},{1,5},{5... | collective-permute-start | bytes 221192 | tf_op jit(solution)/shard_map/ppermute | solution.py:502
  9.2 0.0 collective-permute-done.3.refs_4_
  9.2 2.5 %collective-permute-start.6 = (bf16[144,256]{1,0:T(8,128)(2,1)S(1)}, bf16[144,256]{1,0:T(8,128)(2,1)S(1)}, u32[]{:S(2)}, u32[]{:S(2)}) collective-permute-start(bf16[144,256]{1,0:T(8,128)(2,1)S(1)} %collective-permute-done.3.refs_4_), channel_id=1, source_target_pairs={{0,12},{4,8},{8,4},{12,0},{16,28},{20,24},{24,20},{28,16},{1,13},{... | collective-permute-start | bytes 221192 | tf_op jit(solution)/shard_map/ppermute | solution.py:502
  11.7 0.7 %collective-permute-start.5 = (bf16[144,256]{1,0:T(8,128)(2,1)S(1)}, bf16[144,256]{1,0:T(8,128)(2,1)S(1)}, u32[]{:S(2)}, u32[]{:S(2)}) collective-permute-start(bf16[144,256]{1,0:T(8,128)(2,1)S(1)} %collective-permute-done.3.refs_4_), channel_id=1, source_target_pairs={{0,8},{4,12},{8,0},{12,4},{16,24},{20,28},{24,16},{28,20},{1,9},{5... | collective-permute-start | bytes 221192 | tf_op jit(solution)/shard_map/ppermute | solution.py:502
  12.4 0.0 collective-permute-done.2.refs_3_
  12.4 0.9 %collective-permute-start.4 = (bf16[144,256]{1,0:T(8,128)(2,1)S(1)}, bf16[144,256]{1,0:T(8,128)(2,1)S(1)}, u32[]{:S(2)}, u32[]{:S(2)}) collective-permute-start(bf16[144,256]{1,0:T(8,128)(2,1)S(1)} %collective-permute-done.3.refs_4_), channel_id=1, source_target_pairs={{0,4},{4,0},{8,12},{12,8},{16,20},{20,16},{24,28},{28,24},{1,5},{5... | collective-permute-start | bytes 221192 | tf_op jit(solution)/shard_map/ppermute | solution.py:502
  13.3 0.1 collective-permute-done.1.refs_2_
  13.4 0.9 %collective-permute-done.refs_1_ = bf16[144,256]{1,0:T(8,128)(2,1)S(1)} collective-permute-done((bf16[144,256]{1,0:T(8,128)(2,1)S(1)}, bf16[144,256]{1,0:T(8,128)(2,1)S(1)}, u32[]{:S(2)}, u32[]{:S(2)}) %collective-permute-start) | collective-permute-done | bytes 73760 | tf_op jit(solution)/shard_map/ppermute | solution.py:502
  14.3 0.8 %collective-permute-done.6.refs_7_ = bf16[144,256]{1,0:T(8,128)(2,1)S(1)} collective-permute-done((bf16[144,256]{1,0:T(8,128)(2,1)S(1)}, bf16[144,256]{1,0:T(8,128)(2,1)S(1)}, u32[]{:S(2)}, u32[]{:S(2)}) %collective-permute-start.6) | collective-permute-done | bytes 73760 | tf_op jit(solution)/shard_map/ppermute | solution.py:502
  15.1 0.9 %collective-permute-done.5.refs_6_ = bf16[144,256]{1,0:T(8,128)(2,1)S(1)} collective-permute-done((bf16[144,256]{1,0:T(8,128)(2,1)S(1)}, bf16[144,256]{1,0:T(8,128)(2,1)S(1)}, u32[]{:S(2)}, u32[]{:S(2)}) %collective-permute-start.5) | collective-permute-done | bytes 73760 | tf_op jit(solution)/shard_map/ppermute | solution.py:502
  16.0 0.7 %collective-permute-done.4.refs_5_ = bf16[144,256]{1,0:T(8,128)(2,1)S(1)} collective-permute-done((bf16[144,256]{1,0:T(8,128)(2,1)S(1)}, bf16[144,256]{1,0:T(8,128)(2,1)S(1)}, u32[]{:S(2)}, u32[]{:S(2)}) %collective-permute-start.4) | collective-permute-done | bytes 73760 | tf_op jit(solution)/shard_map/ppermute | solution.py:502
  16.7 0.0 copy-done.1
  16.7 0.0 copy-done
  16.7 5.9 %grads.1 = (f32[2,64,1024]{2,1,0:T(8,128)}, f32[2,8,1024]{2,1,0:T(8,128)S(1)}, f32[128,256]{1,0:T(8,128)S(1)}, f32[136,256]{1,0:T(8,128)S(1)}, bf16[224,256]{1,0...) custom-call(s32[8]{0:T(128)S(1)} %copy-done.1, f32[3,3,128]{2,1,0:T(4,128)S(1)} %copy-done, ...), custom_call_target="tpu_custom_call" | custom-call | tf_op jit(solution)/shard_map/grads/pallas_call | solution.py:559
  22.6 1.0 %collective-permute-start.7 = (bf16[224,256]{1,0:T(8,128)(2,1)S(1)}, bf16[224,256]{1,0:T(8,128)(2,1)S(1)}, u32[]{:S(2)}, u32[]{:S(2)}) collective-permute-start(bf16[224,256]{1,0:T(8,128)(2,1)S(1)} %get-tuple-element.22), channel_id=1, source_target_pairs={{0,4},{4,0},{8,12},{12,8},{16,20},{20,16},{24,28},{28,24},{1,5},{5... | collective-permute-start | bytes 344072 | tf_op jit(solution)/shard_map/ppermute | solution.py:502
  23.6 1.9 %collective-permute-start.9 = (bf16[224,256]{1,0:T(8,128)(2,1)S(1)}, bf16[224,256]{1,0:T(8,128)(2,1)S(1)}, u32[]{:S(2)}, u32[]{:S(2)}) collective-permute-start(bf16[224,256]{1,0:T(8,128)(2,1)S(1)} %get-tuple-element.24), channel_id=1, source_target_pairs={{0,12},{4,8},{8,4},{12,0},{16,28},{20,24},{24,20},{28,16},{1,13},{... | collective-permute-start | bytes 344072 | tf_op jit(solution)/shard_map/ppermute | solution.py:502
  25.5 0.7 %collective-permute-start.8 = (bf16[208,256]{1,0:T(8,128)(2,1)S(1)}, bf16[208,256]{1,0:T(8,128)(2,1)S(1)}, u32[]{:S(2)}, u32[]{:S(2)}) collective-permute-start(bf16[208,256]{1,0:T(8,128)(2,1)S(1)} %get-tuple-element.23), channel_id=1, source_target_pairs={{0,8},{4,12},{8,0},{12,4},{16,24},{20,28},{24,16},{28,20},{1,9},{5... | collective-permute-start | bytes 319496 | tf_op jit(solution)/shard_map/ppermute | solution.py:502
  26.2 4.0 %collective-permute-done.8.refs_1_ = bf16[208,256]{1,0:T(8,128)(2,1)S(1)} collective-permute-done((bf16[208,256]{1,0:T(8,128)(2,1)S(1)}, bf16[208,256]{1,0:T(8,128)(2,1)S(1)}, u32[]{:S(2)}, u32[]{:S(2)}) %collective-permute-start.8) | collective-permute-done | bytes 106528 | tf_op jit(solution)/shard_map/ppermute | solution.py:502
  30.2 0.0 collective-permute-done.7.refs_0_
  30.2 0.0 collective-permute-done.9.refs_2_
  30.2 0.1 merge.1
  30.3 3.0 %collective-permute-start.10 = (bf16[160,256]{1,0:T(8,128)(2,1)S(1)}, bf16[160,256]{1,0:T(8,128)(2,1)S(1)}, u32[]{:S(2)}, u32[]{:S(2)}) collective-permute-start(bf16[160,256]{1,0:T(8,128)(2,1)S(1)} %get-tuple-element.26), channel_id=1, source_target_pairs={{0,16},{4,20},{8,24},{12,28},{16,0},{20,4},{24,8},{28,12},{1,17},{... | collective-permute-start | bytes 245768 | tf_op jit(solution)/shard_map/ppermute | solution.py:502
  33.3 2.5 %collective-permute-done.10.far_ref = bf16[160,256]{1,0:T(8,128)(2,1)S(1)} collective-permute-done((bf16[160,256]{1,0:T(8,128)(2,1)S(1)}, bf16[160,256]{1,0:T(8,128)(2,1)S(1)}, u32[]{:S(2)}, u32[]{:S(2)}) %collective-permute-start.10) | collective-permute-done | bytes 81952 | tf_op jit(solution)/shard_map/ppermute | solution.py:502
  35.7 0.0 collective-permute-start.13
  35.7 1.6 %collective-permute-start.12 = (f32[3,3,128]{2,1,0:T(4,128)S(1)}, f32[3,3,128]{2,1,0:T(4,128)S(1)}, u32[]{:S(2)}, u32[]{:S(2)}) collective-permute-start(f32[3,3,128]{2,1,0:T(4,128)S(1)} %sums.1), channel_id=1, source_target_pairs={{0,2},{1,3},{2,0},{3,1},{4,6},{5,7},{6,4},{7,5},{8,10},{9,11},{10,... | collective-permute-start | bytes 13832 | tf_op jit(solution)/shard_map/ppermute | solution.py:601
  37.3 0.3 collective-permute-start.11
  37.6 1.3 %finish.1 = (f32[2,64,1024]{2,1,0:T(8,128)}, f32[2,64,128]{2,1,0:T(8,128)}, f32[2,64,128]{2,1,0:T(8,128)}) custom-call(s32[8]{0:T(128)S(1)} %copy-done.1, f32[3,3,128]{2,1,0:T(4,128)S(1)} %copy-done, f32[2,64,1024]{2,1,0:T(8,128)} %get-tuple-element.18.dq_in_hbm, f32[2,8,1024]{2,1,0:T(8,128)S(1)} %get-tuple-element.19.tail_ref, ...), custom_call_target="tpu_custom_call", output_to_operand_aliasing={{0}: (2, {})} | custom-call | tf_op jit(solution)/shard_map/finish/pallas_call | solution.py:604
  38.8 0.0 collective-permute-done.13
  38.9 0.6 %collective-permute-done.12 = f32[3,3,128]{2,1,0:T(4,128)S(1)} collective-permute-done((f32[3,3,128]{2,1,0:T(4,128)S(1)}, f32[3,3,128]{2,1,0:T(4,128)S(1)}, u32[]{:S(2)}, u32[]{:S(2)}) %collective-permute-start.12) | collective-permute-done | bytes 4640 | tf_op jit(solution)/shard_map/ppermute | solution.py:601
  39.4 0.0 collective-permute-done.11
  39.4 0.6 %add_add_fusion = f32[3,3,128]{2,1,0:T(4,128)} fusion(f32[3,3,128]{2,1,0:T(4,128)S(1)} %collective-permute-done.12, f32[3,3,128]{2,1,0:T(4,128)S(1)} %collective-permute-done.13, f32[3,3,128]{2,1,0:T(4,128)S(1)} %sums.1, f32[3,3,128]{2,1,0:T(4,128)S(1)} %collective-permute-done.11), kind=kLoop, calls=%fused_computation | loop fusion | flops 3456 | bytes 23040 | tf_op jit(solution)/shard_map/add | solution.py:625
  (1 shorter events, 0.0 us)
Async XLA Ops:
  0.6 16.1 %copy-start.1 = (s32[8]{0:T(128)S(1)}, s32[8]{0:T(128)}, u32[]{:S(2)}) copy-start(s32[8]{0:T(128)} %lengths_ref.3) | copy-start | bytes 100
  0.6 16.1 %copy-start = (f32[3,3,128]{2,1,0:T(4,128)S(1)}, f32[3,3,128]{2,1,0:T(4,128)}, u32[]{:S(2)}) copy-start(f32[3,3,128]{2,1,0:T(4,128)} %filters_ref.3) | copy-start | bytes 13828
  1.6 7.6 %collective-permute-start.3 = (bf16[144,256]{1,0:T(8,128)(2,1)S(1)}, bf16[144,256]{1,0:T(8,128)(2,1)S(1)}, u32[]{:S(2)}, u32[]{:S(2)}) collective-permute-start(bf16[144,256]{1,0:T(8,128)(2,1)S(1)} %pack.1.refs_0_), channel_id=1, source_target_pairs={{0,16},{4,20},{8,24},{12,28},{16,0},{20,4},{24,8},{28,12},{1,17},{... | collective-permute-start | bytes 221192 | tf_op jit(solution)/shard_map/ppermute | solution.py:502
  5.7 6.7 %collective-permute-start.2 = (bf16[144,256]{1,0:T(8,128)(2,1)S(1)}, bf16[144,256]{1,0:T(8,128)(2,1)S(1)}, u32[]{:S(2)}, u32[]{:S(2)}) collective-permute-start(bf16[144,256]{1,0:T(8,128)(2,1)S(1)} %pack.1.refs_0_), channel_id=1, source_target_pairs={{0,12},{4,8},{8,4},{12,0},{16,28},{20,24},{24,20},{28,16},{1,13},{... | collective-permute-start | bytes 221192 | tf_op jit(solution)/shard_map/ppermute | solution.py:502
  8.2 5.2 %collective-permute-start.1 = (bf16[144,256]{1,0:T(8,128)(2,1)S(1)}, bf16[144,256]{1,0:T(8,128)(2,1)S(1)}, u32[]{:S(2)}, u32[]{:S(2)}) collective-permute-start(bf16[144,256]{1,0:T(8,128)(2,1)S(1)} %pack.1.refs_0_), channel_id=1, source_target_pairs={{0,8},{4,12},{8,0},{12,4},{16,24},{20,28},{24,16},{28,20},{1,9},{5... | collective-permute-start | bytes 221192 | tf_op jit(solution)/shard_map/ppermute | solution.py:502
  8.6 5.7 %collective-permute-start = (bf16[144,256]{1,0:T(8,128)(2,1)S(1)}, bf16[144,256]{1,0:T(8,128)(2,1)S(1)}, u32[]{:S(2)}, u32[]{:S(2)}) collective-permute-start(bf16[144,256]{1,0:T(8,128)(2,1)S(1)} %pack.1.refs_0_), channel_id=1, source_target_pairs={{0,4},{4,0},{8,12},{12,8},{16,20},{20,16},{24,28},{28,24},{1,5},{5... | collective-permute-start | bytes 221192 | tf_op jit(solution)/shard_map/ppermute | solution.py:502
  9.2 6.0 %collective-permute-start.6 = (bf16[144,256]{1,0:T(8,128)(2,1)S(1)}, bf16[144,256]{1,0:T(8,128)(2,1)S(1)}, u32[]{:S(2)}, u32[]{:S(2)}) collective-permute-start(bf16[144,256]{1,0:T(8,128)(2,1)S(1)} %collective-permute-done.3.refs_4_), channel_id=1, source_target_pairs={{0,12},{4,8},{8,4},{12,0},{16,28},{20,24},{24,20},{28,16},{1,13},{... | collective-permute-start | bytes 221192 | tf_op jit(solution)/shard_map/ppermute | solution.py:502
  11.7 4.4 %collective-permute-start.5 = (bf16[144,256]{1,0:T(8,128)(2,1)S(1)}, bf16[144,256]{1,0:T(8,128)(2,1)S(1)}, u32[]{:S(2)}, u32[]{:S(2)}) collective-permute-start(bf16[144,256]{1,0:T(8,128)(2,1)S(1)} %collective-permute-done.3.refs_4_), channel_id=1, source_target_pairs={{0,8},{4,12},{8,0},{12,4},{16,24},{20,28},{24,16},{28,20},{1,9},{5... | collective-permute-start | bytes 221192 | tf_op jit(solution)/shard_map/ppermute | solution.py:502
  12.4 4.4 %collective-permute-start.4 = (bf16[144,256]{1,0:T(8,128)(2,1)S(1)}, bf16[144,256]{1,0:T(8,128)(2,1)S(1)}, u32[]{:S(2)}, u32[]{:S(2)}) collective-permute-start(bf16[144,256]{1,0:T(8,128)(2,1)S(1)} %collective-permute-done.3.refs_4_), channel_id=1, source_target_pairs={{0,4},{4,0},{8,12},{12,8},{16,20},{20,16},{24,28},{28,24},{1,5},{5... | collective-permute-start | bytes 221192 | tf_op jit(solution)/shard_map/ppermute | solution.py:502
  22.6 7.5 %collective-permute-start.7 = (bf16[224,256]{1,0:T(8,128)(2,1)S(1)}, bf16[224,256]{1,0:T(8,128)(2,1)S(1)}, u32[]{:S(2)}, u32[]{:S(2)}) collective-permute-start(bf16[224,256]{1,0:T(8,128)(2,1)S(1)} %get-tuple-element.22), channel_id=1, source_target_pairs={{0,4},{4,0},{8,12},{12,8},{16,20},{20,16},{24,28},{28,24},{1,5},{5... | collective-permute-start | bytes 344072 | tf_op jit(solution)/shard_map/ppermute | solution.py:502
  23.6 6.6 %collective-permute-start.9 = (bf16[224,256]{1,0:T(8,128)(2,1)S(1)}, bf16[224,256]{1,0:T(8,128)(2,1)S(1)}, u32[]{:S(2)}, u32[]{:S(2)}) collective-permute-start(bf16[224,256]{1,0:T(8,128)(2,1)S(1)} %get-tuple-element.24), channel_id=1, source_target_pairs={{0,12},{4,8},{8,4},{12,0},{16,28},{20,24},{24,20},{28,16},{1,13},{... | collective-permute-start | bytes 344072 | tf_op jit(solution)/shard_map/ppermute | solution.py:502
  25.5 4.7 %collective-permute-start.8 = (bf16[208,256]{1,0:T(8,128)(2,1)S(1)}, bf16[208,256]{1,0:T(8,128)(2,1)S(1)}, u32[]{:S(2)}, u32[]{:S(2)}) collective-permute-start(bf16[208,256]{1,0:T(8,128)(2,1)S(1)} %get-tuple-element.23), channel_id=1, source_target_pairs={{0,8},{4,12},{8,0},{12,4},{16,24},{20,28},{24,16},{28,20},{1,9},{5... | collective-permute-start | bytes 319496 | tf_op jit(solution)/shard_map/ppermute | solution.py:502
  30.3 5.4 %collective-permute-start.10 = (bf16[160,256]{1,0:T(8,128)(2,1)S(1)}, bf16[160,256]{1,0:T(8,128)(2,1)S(1)}, u32[]{:S(2)}, u32[]{:S(2)}) collective-permute-start(bf16[160,256]{1,0:T(8,128)(2,1)S(1)} %get-tuple-element.26), channel_id=1, source_target_pairs={{0,16},{4,20},{8,24},{12,28},{16,0},{20,4},{24,8},{28,12},{1,17},{... | collective-permute-start | bytes 245768 | tf_op jit(solution)/shard_map/ppermute | solution.py:502
  35.7 3.1 %collective-permute-start.13 = (f32[3,3,128]{2,1,0:T(4,128)S(1)}, f32[3,3,128]{2,1,0:T(4,128)S(1)}, u32[]{:S(2)}, u32[]{:S(2)}) collective-permute-start(f32[3,3,128]{2,1,0:T(4,128)S(1)} %sums.1), channel_id=1, source_target_pairs={{0,3},{1,2},{2,1},{3,0},{4,7},{5,6},{6,5},{7,4},{8,11},{9,10},{10,... | collective-permute-start | bytes 13832 | tf_op jit(solution)/shard_map/ppermute | solution.py:601
  35.7 3.7 %collective-permute-start.12 = (f32[3,3,128]{2,1,0:T(4,128)S(1)}, f32[3,3,128]{2,1,0:T(4,128)S(1)}, u32[]{:S(2)}, u32[]{:S(2)}) collective-permute-start(f32[3,3,128]{2,1,0:T(4,128)S(1)} %sums.1), channel_id=1, source_target_pairs={{0,2},{1,3},{2,0},{3,1},{4,6},{5,7},{6,4},{7,5},{8,10},{9,11},{10,... | collective-permute-start | bytes 13832 | tf_op jit(solution)/shard_map/ppermute | solution.py:601
  37.3 2.1 %collective-permute-start.11 = (f32[3,3,128]{2,1,0:T(4,128)S(1)}, f32[3,3,128]{2,1,0:T(4,128)S(1)}, u32[]{:S(2)}, u32[]{:S(2)}) collective-permute-start(f32[3,3,128]{2,1,0:T(4,128)S(1)} %sums.1), channel_id=1, source_target_pairs={{0,1},{1,0},{2,3},{3,2},{4,5},{5,4},{6,7},{7,6},{8,9},{9,8},{10,11... | collective-permute-start | bytes 13832 | tf_op jit(solution)/shard_map/ppermute | solution.py:601

commit v2 on v1

--- a/solution.py
+++ b/solution.py
@@ -80,10 +80,55 @@
     out_ref[2 * span :] = jnp.concatenate(tails, axis=0).astype(jnp.bfloat16)
 
 
+def relay_kernel(ctx_count, direct, own_ref, across_ref, *out_refs):
+    group = ctx_count // 2
+    me = lax.axis_index("ctx")
+    low = me < group
+    sent = Slots((None,) + out_refs if direct else out_refs, me)
+    rows = own_ref.shape[0] - TAIL
+    span = rows // 2
+
+    def send(step, carry):
+        flip = step + 1
+        target = partner(me, flip)
+        message = sent[flip]
+        message[:span] = across_ref[:span]
+
+        @pl.when(low)
+        def _():
+            message[span : 2 * span] = across_ref[span:rows]
+
+            @pl.when(target > me)
+            def _():
+                message[2 * span : 3 * span] = own_ref[:span]
+
+            @pl.when(target < me)
+            def _():
+                message[2 * span : 3 * span] = own_ref[span:rows]
+
+        @pl.when(jnp.logical_not(low))
+        def _():
+            message[span : 3 * span] = own_ref[:rows]
+
+        if not direct or flip & (flip + 1) == 0:
+
+            @pl.when(jnp.abs(target - me) == 1)
+            def _():
+                message[3 * span :] = own_ref[rows:]
+
+            @pl.when(jnp.abs(target - me) != 1)
+            def _():
+                message[3 * span :] = across_ref[rows:]
+
+        return carry
+
+    loop(group - 1, send, 0, 16 if direct else 1)
+
+
 def grads_kernel(ctx_count, direct, lengths_ref, filters_ref, q_hbm, d_out_hbm, *refs):
     group = ctx_count // 2
-    arrays = group if direct else 1
-    near_in, far_in, refs = refs[:arrays], refs[arrays : 2 * arrays], refs[2 * arrays :]
+    arrays = group - 1 if direct else 1
+    own_ref, across_ref, received_refs, refs = refs[0], refs[1], refs[2 : 2 + arrays], refs[2 + arrays :]
     dq_hbm, dq_tail_ref, own_near_ref, own_far_ref = refs[:4]
     arrays = group - 1 if direct else 1
     out_refs, refs = refs[4 : 4 + arrays], refs[4 + arrays :]
@@ -102,7 +147,7 @@
     length = 2 * half_rows
     blocks = 2 * ctx_count
     me = lax.axis_index("ctx")
-    near_in, far_in = Slots(near_in, me), Slots(far_in, me)
+    received = Slots((None,) + received_refs if direct else received_refs, me)
     sent = Slots((own_far_ref,) + out_refs if direct else out_refs, me)
     scale = LANES**-0.5
     log2_scale = scale * 1.4426950408889634
@@ -126,21 +171,41 @@
         same_two_scr[pl.ds(8 + start, 1)] = zeros[:1]
         same_two_scr[pl.ds(9 + start, 1)] = zeros[:1]
 
-    def place_blocks(flip, carry):
-        for message, index in (
-            (near_in[flip], partner(me, flip)),
-            (far_in[flip], partner(me, flip + group)),
-        ):
-            early = aligned(8 + index * span, 8)
-            late = aligned(8 + (blocks - 1 - index) * span, 8)
-            for tensor in range(2):
-                lanes = slice(tensor * LANES, (tensor + 1) * LANES)
-                kv_scr[tensor, pl.ds(early, span)] = message[:span, lanes].astype(f32)
-                kv_scr[tensor, pl.ds(late, span)] = message[span : 2 * span, lanes].astype(f32)
-            rim_scr[index] = message[2 * span :].astype(f32)
+    def place(index, block):
+        for tensor in range(2):
+            lanes = slice(tensor * LANES, (tensor + 1) * LANES)
+            kv_scr[tensor, pl.ds(aligned(8 + index * span, 8), span)] = block[:, lanes].astype(f32)
+
+    def clear(index, carry):
+        for tensor in range(2):
+            kv_scr[tensor, pl.ds(aligned(8 + index * span, 8), span)] = jnp.zeros((span, LANES), f32)
         return carry
 
-    loop(group, place_blocks, 0)
+    low = me < group
+
+    def place_received(step, carry):
+        flip = step + 1
+        source = partner(me, flip)
+        across = partner(source, group)
+        message = received[flip]
+        late = blocks - 1 - source
+        places = [
+            across,
+            jnp.where(low, blocks - 1 - across, source),
+            jnp.where(low & (source < me), source, late),
+        ]
+        for at, index in enumerate(places):
+            place(index, message[at * span : (at + 1) * span])
+        if not direct or flip & (flip + 1) == 0:
+            rim_scr[jnp.where(jnp.abs(source - me) == 1, source, across)] = message[3 * span :].astype(f32)
+        return carry
+
+    loop(blocks, clear, 0)
+    for block_ref, index in ((own_ref, me), (across_ref, partner(me, group))):
+        place(index, block_ref[:span])
+        place(blocks - 1 - index, block_ref[span : 2 * span])
+        rim_scr[index] = block_ref[2 * span :].astype(f32)
+    loop(group - 1, place_received, 0, 16 if direct else 1)
 
     def taps(tensor):
         return [filters_ref[tensor, tap : tap + 1] for tap in range(3)]
@@ -318,8 +383,6 @@
             carry[at + 2] += fold_rows(own * two * kv_scr[tensor, pl.ds(base + 6, span)])
         return tuple(carry)
 
-    low = me < group
-
     def finish(step, carry):
         flip = step + 1
         owner = partner(me, flip)
@@ -501,11 +564,6 @@
     def flipped(array, flip):
         return lax.ppermute(array, "ctx", [(i, i ^ flip) for i in range(ctx_count)])
 
-    def gathered(array):
-        if direct:
-            return [array] + [flipped(array, flip) for flip in range(1, group)]
-        return [lax.all_gather(array, "ctx", axis_index_groups=halves)]
-
     def delivered(arrays):
         if direct:
             return [flipped(array, step + 1) for step, array in enumerate(arrays)]
@@ -525,7 +583,21 @@
         name="pack",
     )(*[in_hbm(array) for array in (k_pre, value_before_filter, q_pre)])
     across = flipped(packed, group)
-    received = gathered(packed) + gathered(across)
+    if direct:
+        relay_shapes = [
+            (3 * span + (rim if flip & (flip + 1) == 0 else 0), 2 * LANES) for flip in range(1, group)
+        ]
+    else:
+        relay_shapes = [(group, 3 * span + rim, 2 * LANES)]
+    relayed = pl.pallas_call(
+        functools.partial(relay_kernel, ctx_count, direct),
+        out_shape=[jax.ShapeDtypeStruct(shape, bf16) for shape in relay_shapes],
+        in_specs=[vmem, vmem],
+        out_specs=[vmem] * len(relay_shapes),
+        compiler_params=pltpu.CompilerParams(vmem_limit_bytes=(4 if direct else 40) * MIB),
+        name="relay",
+    )(packed, across)
+    received = [packed, across] + delivered(relayed)
 
     window = span * ctx_count + span
     if direct:

time: 40.4 us -> 42 us (1.040)
  waiting for transfers between devices: 10.5 us -> 15.6 us
  starting transfers between devices: 20.1 us -> 16.7 us
    ppermute x11 -> x8, waiting for transfers between devices: 9.9 us -> 15 us  [flipped(): return lax.ppermute(array, 'ctx', [(i, i ^ flip) for i in range(ctx_count)])]
    ppermute x11 -> x8, starting transfers between devices: 18.2 us -> 14.9 us  [flipped(): return lax.ppermute(array, 'ctx', [(i, i ^ flip) for i in range(ctx_count)])]
  transfers between devices with their start and end apart: 14 -> 11, of which waited for: 8 -> 6; matrix products, arithmetic and copies ran while one was open for 0% -> 0% of each run, Pallas kernels for 3% -> 3%
where the time goes in v2:
time: 42 us; the launch traced here: 41.8 us
  starting transfers between devices  16.7 us (40%)
  waiting for transfers between devices  15.6 us (37%)
  Pallas kernels  8.24 us (20%)
  between operations  0.68 us (2%)
  other arithmetic  0.6 us (1%)
    ppermute x8, waiting for transfers between devices, flipped(): return lax.ppermute(array, 'ctx', [(i, i ^ flip) for i in range(ctx_count)])  15 us
    ppermute x8, starting transfers between devices, flipped(): return lax.ppermute(array, 'ctx', [(i, i ^ flip) for i in range(ctx_count)])  14.9 us
    pallas_call x1, Pallas kernels, shards(): pl.pallas_call(functools.partial(grads_kernel, ctx_count, direct), out_sh...  5.89 us
    ppermute x3, starting transfers between devices, shards(): lax.ppermute(sums, 'tp', [(i, i ^ flip) for i in range(count)])  1.86 us
    pallas_call x1, Pallas kernels, shards(): pl.pallas_call(functools.partial(finish_kernel, ctx_count), out_shape=(ja...  1.26 us
    pallas_call x1, Pallas kernels, shards(): pl.pallas_call(pack_kernel, grid=(1,), out_shape=jax.ShapeDtypeStruct((ms...  0.9 us
  transfers between devices with their start and end apart: 11, of which 6 were waited for; matrix products, arithmetic and copies ran while one was open for 0% of the time, Pallas kernels for 3%

profile of v2, /device:TPU:0, one launch (start us, length us, event | category | flops | bytes accessed | tf_op | source)
XLA Modules:
  0.0 41.8 jit_solution(2729660396582561739)
XLA Ops:
  0.6 0.9 %pack.1.own_ref.refs_0_ = bf16[144,256]{1,0:T(8,128)(2,1)S(1)} custom-call(bf16[2,64,128]{2,1,0:T(8,128)(2,1)} %k_ref.1, bf16[2,64,128]{2,1,0:T(8,128)(2,1)} %v_ref.1, bf16[2,64,1024]{2,1,0:T(8,128)(2,1)} %q_hbm.1), custom_call_target="tpu_custom_call" | custom-call | tf_op jit(solution)/shard_map/pack/pallas_call | solution.py:572
  1.5 4.1 %collective-permute-start = (bf16[144,256]{1,0:T(8,128)(2,1)S(1)}, bf16[144,256]{1,0:T(8,128)(2,1)S(1)}, u32[]{:S(2)}, u32[]{:S(2)}) collective-permute-start(bf16[144,256]{1,0:T(8,128)(2,1)S(1)} %pack.1.own_ref.refs_0_), channel_id=1, source_target_pairs={{0,16},{4,20},{8,24},{12,28},{16,0},{20,4},{24,8},{28,12},{1,17},{... | collective-permute-start | bytes 221192 | tf_op jit(solution)/shard_map/ppermute | solution.py:565
  5.6 3.9 %collective-permute-done.across_ref.refs_1_ = bf16[144,256]{1,0:T(8,128)(2,1)S(1)} collective-permute-done((bf16[144,256]{1,0:T(8,128)(2,1)S(1)}, bf16[144,256]{1,0:T(8,128)(2,1)S(1)}, u32[]{:S(2)}, u32[]{:S(2)}) %collective-permute-start) | collective-permute-done | bytes 73760 | tf_op jit(solution)/shard_map/ppermute | solution.py:565
  9.5 0.0 copy-start
  9.5 0.1 relay.1
  9.6 1.8 %collective-permute-start.1 = (bf16[208,256]{1,0:T(8,128)(2,1)S(1)}, bf16[208,256]{1,0:T(8,128)(2,1)S(1)}, u32[]{:S(2)}, u32[]{:S(2)}) collective-permute-start(bf16[208,256]{1,0:T(8,128)(2,1)S(1)} %get-tuple-element.21), channel_id=1, source_target_pairs={{0,4},{4,0},{8,12},{12,8},{16,20},{20,16},{24,28},{28,24},{1,5},{5... | collective-permute-start | bytes 319496 | tf_op jit(solution)/shard_map/ppermute | solution.py:565
  11.4 0.0 copy-start.1
  11.4 0.4 collective-permute-start.3
  11.8 1.4 %collective-permute-start.2 = (bf16[192,256]{1,0:T(8,128)(2,1)S(1)}, bf16[192,256]{1,0:T(8,128)(2,1)S(1)}, u32[]{:S(2)}, u32[]{:S(2)}) collective-permute-start(bf16[192,256]{1,0:T(8,128)(2,1)S(1)} %get-tuple-element.22), channel_id=1, source_target_pairs={{0,8},{4,12},{8,0},{12,4},{16,24},{20,28},{24,16},{28,20},{1,9},{5... | collective-permute-start | bytes 294920 | tf_op jit(solution)/shard_map/ppermute | solution.py:565
  13.2 3.7 %collective-permute-done.2.refs_3_ = bf16[192,256]{1,0:T(8,128)(2,1)S(1)} collective-permute-done((bf16[192,256]{1,0:T(8,128)(2,1)S(1)}, bf16[192,256]{1,0:T(8,128)(2,1)S(1)}, u32[]{:S(2)}, u32[]{:S(2)}) %collective-permute-start.2) | collective-permute-done | bytes 98336 | tf_op jit(solution)/shard_map/ppermute | solution.py:565
  16.9 0.0 collective-permute-done.1.refs_2_
  16.9 0.1 collective-permute-done.3.refs_4_
  17.0 0.0 copy-done
  17.0 0.0 copy-done.1
  17.0 5.9 %grads.1 = (f32[2,64,1024]{2,1,0:T(8,128)}, f32[2,8,1024]{2,1,0:T(8,128)S(1)}, f32[128,256]{1,0:T(8,128)S(1)}, f32[136,256]{1,0:T(8,128)S(1)}, bf16[224,256]{1,0...) custom-call(s32[8]{0:T(128)S(1)} %copy-done.1, f32[3,3,128]{2,1,0:T(4,128)S(1)} %copy-done, ...), custom_call_target="tpu_custom_call" | custom-call | tf_op jit(solution)/shard_map/grads/pallas_call | solution.py:631
  22.9 1.7 %collective-permute-start.4 = (bf16[224,256]{1,0:T(8,128)(2,1)S(1)}, bf16[224,256]{1,0:T(8,128)(2,1)S(1)}, u32[]{:S(2)}, u32[]{:S(2)}) collective-permute-start(bf16[224,256]{1,0:T(8,128)(2,1)S(1)} %get-tuple-element.28), channel_id=1, source_target_pairs={{0,4},{4,0},{8,12},{12,8},{16,20},{20,16},{24,28},{28,24},{1,5},{5... | collective-permute-start | bytes 344072 | tf_op jit(solution)/shard_map/ppermute | solution.py:565
  24.6 1.1 %collective-permute-start.6 = (bf16[224,256]{1,0:T(8,128)(2,1)S(1)}, bf16[224,256]{1,0:T(8,128)(2,1)S(1)}, u32[]{:S(2)}, u32[]{:S(2)}) collective-permute-start(bf16[224,256]{1,0:T(8,128)(2,1)S(1)} %get-tuple-element.30), channel_id=1, source_target_pairs={{0,12},{4,8},{8,4},{12,0},{16,28},{20,24},{24,20},{28,16},{1,13},{... | collective-permute-start | bytes 344072 | tf_op jit(solution)/shard_map/ppermute | solution.py:565
  25.7 0.7 %collective-permute-start.5 = (bf16[208,256]{1,0:T(8,128)(2,1)S(1)}, bf16[208,256]{1,0:T(8,128)(2,1)S(1)}, u32[]{:S(2)}, u32[]{:S(2)}) collective-permute-start(bf16[208,256]{1,0:T(8,128)(2,1)S(1)} %get-tuple-element.29), channel_id=1, source_target_pairs={{0,8},{4,12},{8,0},{12,4},{16,24},{20,28},{24,16},{28,20},{1,9},{5... | collective-permute-start | bytes 319496 | tf_op jit(solution)/shard_map/ppermute | solution.py:565
  26.4 4.0 %collective-permute-done.5.refs_1_ = bf16[208,256]{1,0:T(8,128)(2,1)S(1)} collective-permute-done((bf16[208,256]{1,0:T(8,128)(2,1)S(1)}, bf16[208,256]{1,0:T(8,128)(2,1)S(1)}, u32[]{:S(2)}, u32[]{:S(2)}) %collective-permute-start.5) | collective-permute-done | bytes 106528 | tf_op jit(solution)/shard_map/ppermute | solution.py:565
  30.4 0.0 collective-permute-done.4.refs_0_
  30.4 0.0 collective-permute-done.6.refs_2_
  30.4 0.1 merge.1
  30.6 3.7 %collective-permute-start.7 = (bf16[160,256]{1,0:T(8,128)(2,1)S(1)}, bf16[160,256]{1,0:T(8,128)(2,1)S(1)}, u32[]{:S(2)}, u32[]{:S(2)}) collective-permute-start(bf16[160,256]{1,0:T(8,128)(2,1)S(1)} %get-tuple-element.32), channel_id=1, source_target_pairs={{0,16},{4,20},{8,24},{12,28},{16,0},{20,4},{24,8},{28,12},{1,17},{... | collective-permute-start | bytes 245768 | tf_op jit(solution)/shard_map/ppermute | solution.py:565
  34.2 3.3 %collective-permute-done.7.far_ref = bf16[160,256]{1,0:T(8,128)(2,1)S(1)} collective-permute-done((bf16[160,256]{1,0:T(8,128)(2,1)S(1)}, bf16[160,256]{1,0:T(8,128)(2,1)S(1)}, u32[]{:S(2)}, u32[]{:S(2)}) %collective-permute-start.7) | collective-permute-done | bytes 81952 | tf_op jit(solution)/shard_map/ppermute | solution.py:565
  37.5 0.0 collective-permute-start.10
  37.6 1.6 %collective-permute-start.9 = (f32[3,3,128]{2,1,0:T(4,128)S(1)}, f32[3,3,128]{2,1,0:T(4,128)S(1)}, u32[]{:S(2)}, u32[]{:S(2)}) collective-permute-start(f32[3,3,128]{2,1,0:T(4,128)S(1)} %sums.1), channel_id=1, source_target_pairs={{0,2},{1,3},{2,0},{3,1},{4,6},{5,7},{6,4},{7,5},{8,10},{9,11},{10,... | collective-permute-start | bytes 13832 | tf_op jit(solution)/shard_map/ppermute | solution.py:673
  39.1 0.3 collective-permute-start.8
  39.4 1.3 %finish.1 = (f32[2,64,1024]{2,1,0:T(8,128)}, f32[2,64,128]{2,1,0:T(8,128)}, f32[2,64,128]{2,1,0:T(8,128)}) custom-call(s32[8]{0:T(128)S(1)} %copy-done.1, f32[3,3,128]{2,1,0:T(4,128)S(1)} %copy-done, f32[2,64,1024]{2,1,0:T(8,128)} %get-tuple-element.24.dq_in_hbm, f32[2,8,1024]{2,1,0:T(8,128)S(1)} %get-tuple-element.25.tail_ref, ...), custom_call_target="tpu_custom_call", output_to_operand_aliasing={{0}: (2, {})} | custom-call | tf_op jit(solution)/shard_map/finish/pallas_call | solution.py:676
  40.7 0.0 collective-permute-done.10
  40.7 0.6 %collective-permute-done.9 = f32[3,3,128]{2,1,0:T(4,128)S(1)} collective-permute-done((f32[3,3,128]{2,1,0:T(4,128)S(1)}, f32[3,3,128]{2,1,0:T(4,128)S(1)}, u32[]{:S(2)}, u32[]{:S(2)}) %collective-permute-start.9) | collective-permute-done | bytes 4640 | tf_op jit(solution)/shard_map/ppermute | solution.py:673
  41.2 0.0 collective-permute-done.8
  41.2 0.6 %add_add_fusion = f32[3,3,128]{2,1,0:T(4,128)} fusion(f32[3,3,128]{2,1,0:T(4,128)S(1)} %collective-permute-done.9, f32[3,3,128]{2,1,0:T(4,128)S(1)} %collective-permute-done.10, f32[3,3,128]{2,1,0:T(4,128)S(1)} %sums.1, f32[3,3,128]{2,1,0:T(4,128)S(1)} %collective-permute-done.8), kind=kLoop, calls=%fused_computation | loop fusion | flops 3456 | bytes 23040 | tf_op jit(solution)/shard_map/add | solution.py:697
  (1 shorter events, 0.0 us)
Async XLA Ops:
  1.5 8.0 %collective-permute-start = (bf16[144,256]{1,0:T(8,128)(2,1)S(1)}, bf16[144,256]{1,0:T(8,128)(2,1)S(1)}, u32[]{:S(2)}, u32[]{:S(2)}) collective-permute-start(bf16[144,256]{1,0:T(8,128)(2,1)S(1)} %pack.1.own_ref.refs_0_), channel_id=1, source_target_pairs={{0,16},{4,20},{8,24},{12,28},{16,0},{20,4},{24,8},{28,12},{1,17},{... | collective-permute-start | bytes 221192 | tf_op jit(solution)/shard_map/ppermute | solution.py:565
  9.5 7.4 %copy-start = (f32[3,3,128]{2,1,0:T(4,128)S(1)}, f32[3,3,128]{2,1,0:T(4,128)}, u32[]{:S(2)}) copy-start(f32[3,3,128]{2,1,0:T(4,128)} %filters_ref.3) | copy-start | bytes 13828
  9.6 7.3 %collective-permute-start.1 = (bf16[208,256]{1,0:T(8,128)(2,1)S(1)}, bf16[208,256]{1,0:T(8,128)(2,1)S(1)}, u32[]{:S(2)}, u32[]{:S(2)}) collective-permute-start(bf16[208,256]{1,0:T(8,128)(2,1)S(1)} %get-tuple-element.21), channel_id=1, source_target_pairs={{0,4},{4,0},{8,12},{12,8},{16,20},{20,16},{24,28},{28,24},{1,5},{5... | collective-permute-start | bytes 319496 | tf_op jit(solution)/shard_map/ppermute | solution.py:565
  11.4 5.6 %copy-start.1 = (s32[8]{0:T(128)S(1)}, s32[8]{0:T(128)}, u32[]{:S(2)}) copy-start(s32[8]{0:T(128)} %lengths_ref.3) | copy-start | bytes 100
  11.4 5.6 %collective-permute-start.3 = (bf16[208,256]{1,0:T(8,128)(2,1)S(1)}, bf16[208,256]{1,0:T(8,128)(2,1)S(1)}, u32[]{:S(2)}, u32[]{:S(2)}) collective-permute-start(bf16[208,256]{1,0:T(8,128)(2,1)S(1)} %get-tuple-element.23), channel_id=1, source_target_pairs={{0,12},{4,8},{8,4},{12,0},{16,28},{20,24},{24,20},{28,16},{1,13},{... | collective-permute-start | bytes 319496 | tf_op jit(solution)/shard_map/ppermute | solution.py:565
  11.8 5.1 %collective-permute-start.2 = (bf16[192,256]{1,0:T(8,128)(2,1)S(1)}, bf16[192,256]{1,0:T(8,128)(2,1)S(1)}, u32[]{:S(2)}, u32[]{:S(2)}) collective-permute-start(bf16[192,256]{1,0:T(8,128)(2,1)S(1)} %get-tuple-element.22), channel_id=1, source_target_pairs={{0,8},{4,12},{8,0},{12,4},{16,24},{20,28},{24,16},{28,20},{1,9},{5... | collective-permute-start | bytes 294920 | tf_op jit(solution)/shard_map/ppermute | solution.py:565
  22.9 7.5 %collective-permute-start.4 = (bf16[224,256]{1,0:T(8,128)(2,1)S(1)}, bf16[224,256]{1,0:T(8,128)(2,1)S(1)}, u32[]{:S(2)}, u32[]{:S(2)}) collective-permute-start(bf16[224,256]{1,0:T(8,128)(2,1)S(1)} %get-tuple-element.28), channel_id=1, source_target_pairs={{0,4},{4,0},{8,12},{12,8},{16,20},{20,16},{24,28},{28,24},{1,5},{5... | collective-permute-start | bytes 344072 | tf_op jit(solution)/shard_map/ppermute | solution.py:565
  24.6 5.8 %collective-permute-start.6 = (bf16[224,256]{1,0:T(8,128)(2,1)S(1)}, bf16[224,256]{1,0:T(8,128)(2,1)S(1)}, u32[]{:S(2)}, u32[]{:S(2)}) collective-permute-start(bf16[224,256]{1,0:T(8,128)(2,1)S(1)} %get-tuple-element.30), channel_id=1, source_target_pairs={{0,12},{4,8},{8,4},{12,0},{16,28},{20,24},{24,20},{28,16},{1,13},{... | collective-permute-start | bytes 344072 | tf_op jit(solution)/shard_map/ppermute | solution.py:565
  25.7 4.7 %collective-permute-start.5 = (bf16[208,256]{1,0:T(8,128)(2,1)S(1)}, bf16[208,256]{1,0:T(8,128)(2,1)S(1)}, u32[]{:S(2)}, u32[]{:S(2)}) collective-permute-start(bf16[208,256]{1,0:T(8,128)(2,1)S(1)} %get-tuple-element.29), channel_id=1, source_target_pairs={{0,8},{4,12},{8,0},{12,4},{16,24},{20,28},{24,16},{28,20},{1,9},{5... | collective-permute-start | bytes 319496 | tf_op jit(solution)/shard_map/ppermute | solution.py:565
  30.6 7.0 %collective-permute-start.7 = (bf16[160,256]{1,0:T(8,128)(2,1)S(1)}, bf16[160,256]{1,0:T(8,128)(2,1)S(1)}, u32[]{:S(2)}, u32[]{:S(2)}) collective-permute-start(bf16[160,256]{1,0:T(8,128)(2,1)S(1)} %get-tuple-element.32), channel_id=1, source_target_pairs={{0,16},{4,20},{8,24},{12,28},{16,0},{20,4},{24,8},{28,12},{1,17},{... | collective-permute-start | bytes 245768 | tf_op jit(solution)/shard_map/ppermute | solution.py:565
  37.5 3.1 %collective-permute-start.10 = (f32[3,3,128]{2,1,0:T(4,128)S(1)}, f32[3,3,128]{2,1,0:T(4,128)S(1)}, u32[]{:S(2)}, u32[]{:S(2)}) collective-permute-start(f32[3,3,128]{2,1,0:T(4,128)S(1)} %sums.1), channel_id=1, source_target_pairs={{0,3},{1,2},{2,1},{3,0},{4,7},{5,6},{6,5},{7,4},{8,11},{9,10},{10,... | collective-permute-start | bytes 13832 | tf_op jit(solution)/shard_map/ppermute | solution.py:673
  37.6 3.7 %collective-permute-start.9 = (f32[3,3,128]{2,1,0:T(4,128)S(1)}, f32[3,3,128]{2,1,0:T(4,128)S(1)}, u32[]{:S(2)}, u32[]{:S(2)}) collective-permute-start(f32[3,3,128]{2,1,0:T(4,128)S(1)} %sums.1), channel_id=1, source_target_pairs={{0,2},{1,3},{2,0},{3,1},{4,6},{5,7},{6,4},{7,5},{8,10},{9,11},{10,... | collective-permute-start | bytes 13832 | tf_op jit(solution)/shard_map/ppermute | solution.py:673
  39.1 2.1 %collective-permute-start.8 = (f32[3,3,128]{2,1,0:T(4,128)S(1)}, f32[3,3,128]{2,1,0:T(4,128)S(1)}, u32[]{:S(2)}, u32[]{:S(2)}) collective-permute-start(f32[3,3,128]{2,1,0:T(4,128)S(1)} %sums.1), channel_id=1, source_target_pairs={{0,1},{1,0},{2,3},{3,2},{4,5},{5,4},{6,7},{7,6},{8,9},{9,8},{10,11... | collective-permute-start | bytes 13832 | tf_op jit(solution)/shard_map/ppermute | solution.py:673

commit v3 on v1

--- a/solution.py
+++ b/solution.py
@@ -15,6 +15,7 @@
 TAIL = 16
 MAX_CHUNK = 640
 MAX_DIRECT = 4
+WINDOWS = (2, 4, 6)
 MIB = 1 << 20
 
 
@@ -186,7 +187,7 @@
             qc_scr[half, head * span : (head + 1) * span] = total.astype(bf16)
             do_scr[half, head * span : (head + 1) * span] = d_out_ref[half, :, lanes]
 
-    def attend(half, window, first_key, add):
+    def attend(half, window, first_key):
         chunks = 1
         while window // chunks > MAX_CHUNK or window % (16 * chunks):
             chunks += 1
@@ -254,10 +255,7 @@
                 dv = lax.dot_general(probs, grads, NN, preferred_element_type=f32)
                 target = pl.ds(aligned(first_key + step * size, 16), size)
                 for tensor, terms in enumerate((dk, dv)):
-                    if add or at:
-                        dkv_scr[tensor, target] += terms
-                    else:
-                        dkv_scr[tensor, target] = terms
+                    dkv_scr[tensor, target] += terms
                 if keys_t is not None:
                     return lax.dot_general(keys_t, score_grads, NN, preferred_element_type=f32)
                 keys = conv_scr[0, key_rows(step)]
@@ -269,10 +267,30 @@
                 head = at * (wide // span) + part
                 dq_scr[half, head, :span] = dq[part * span : (part + 1) * span]
 
+    def clear(index, carry):
+        for tensor in range(2):
+            dkv_scr[tensor, pl.ds(aligned(index * span, 8), span)] = jnp.zeros((span, LANES), f32)
+        return carry
+
+    loop(blocks, clear, 0)
     for tensor in range(2):
-        dkv_scr[tensor, half_rows:] = jnp.zeros((half_rows + 8, LANES), f32)
-    attend(0, half_rows, 0, False)
-    attend(1, half_rows + span, (ctx_count - 1 - me) * span, True)
+        dkv_scr[tensor, length:] = zeros
+
+    for half in range(2):
+        widest = ctx_count + half
+        lowest = jnp.int32(0)
+        for start in starts[1:]:
+            lowest = jnp.where(first_place[half] >= start, start, lowest)
+        needed = first_place[half] // span - lowest // span + 1
+        below = 0
+        for count in [count for count in WINDOWS if direct and count < widest] + [widest]:
+
+            @pl.when((needed > below) & (needed <= count))
+            def _(half=half, count=count):
+                first_key = jnp.maximum(first_place[half] + span - count * span, 0)
+                attend(half, count * span, first_key)
+
+            below = count
 
     next_rows = jnp.where(middle, dq_scr[1, :, :8], 0.0)
     dq_scr[0, :, span:] = next_rows
@@ -429,7 +447,8 @@
 def finish_kernel(
     ctx_count, lengths_ref, filters_ref, dq_in_hbm, tail_ref, near_ref, far_ref, rims_ref, *refs
 ):
-    dq_hbm, dk_hbm, dv_hbm, dq_ref, dk_ref, dv_ref, sems = refs
+    sums_refs, refs = refs[:-9], refs[-9:]
+    dq_hbm, dk_hbm, dv_hbm, d_filters_hbm, dq_ref, dk_ref, dv_ref, d_filters_ref, sems = refs
     f32 = jnp.float32
     group = ctx_count // 2
     span = dk_ref.shape[1]
@@ -444,9 +463,14 @@
     stores = [
         pltpu.make_async_copy(dk_ref, dk_hbm, sems.at[0]),
         pltpu.make_async_copy(dv_ref, dv_hbm, sems.at[1]),
-        pltpu.make_async_copy(dq_ref, dq_hbm.at[:, pl.ds(span - 8, 8)], sems.at[2]),
+        pltpu.make_async_copy(d_filters_ref, d_filters_hbm, sems.at[2]),
+        pltpu.make_async_copy(dq_ref, dq_hbm.at[:, pl.ds(span - 8, 8)], sems.at[3]),
     ]
-    for store in stores[:2]:
+    level = [ref[...] for ref in sums_refs]
+    while len(level) > 1:
+        level = [level[at] + level[at + 1] for at in range(0, len(level), 2)]
+    d_filters_ref[...] = level[0]
+    for store in stores[:3]:
         store.start()
 
     def same(place):
@@ -472,7 +496,7 @@
         last = one * (taps[1] * rows[0:1]) + (one * two) * (taps[2] * rows[1:2])
         extra = jnp.where(row == 6, last_but_one, jnp.where(row == 7, last, 0.0))
         dq_ref[half] = tail_ref[half] + extra
-    stores[2].start()
+    stores[3].start()
     for store in stores:
         store.wait()
 
@@ -597,34 +621,30 @@
         name="sums",
     )(half_sums, from_half)
     count = lax.axis_size("tp")
-    level = [sums] + [
+    all_sums = [sums] + [
         lax.ppermute(sums, "tp", [(i, i ^ flip) for i in range(count)]) for flip in range(1, count)
     ]
-
-    d_q_pre, d_k_pre, d_v_pre = pl.pallas_call(
+    return pl.pallas_call(
         functools.partial(finish_kernel, ctx_count),
         out_shape=(
             jax.ShapeDtypeStruct(q_pre.shape, f32),
             jax.ShapeDtypeStruct(k_pre.shape, f32),
             jax.ShapeDtypeStruct(k_pre.shape, f32),
+            jax.ShapeDtypeStruct(filters.shape, f32),
         ),
-        in_specs=[smem, vmem, hbm, vmem, vmem, vmem, vmem],
-        out_specs=(hbm, hbm, hbm),
+        in_specs=[smem, vmem, hbm] + [vmem] * (4 + count),
+        out_specs=(hbm, hbm, hbm, hbm),
         scratch_shapes=[
             pltpu.VMEM((2, 8, width), f32),
             pltpu.VMEM(k_pre.shape, f32),
             pltpu.VMEM(k_pre.shape, f32),
-            pltpu.SemaphoreType.DMA((3,)),
+            pltpu.VMEM(filters.shape, f32),
+            pltpu.SemaphoreType.DMA((4,)),
         ],
         input_output_aliases={2: 0},
         compiler_params=pltpu.CompilerParams(vmem_limit_bytes=4 * MIB),
         name="finish",
-    )(doc_lengths, filters, d_q_main, d_q_tail, near, from_half, rims)
-
-    while len(level) > 1:
-        level = [level[at] + level[at + 1] for at in range(0, len(level), 2)]
-    d_filters = level[0]
-    return (d_q_pre, d_k_pre, d_v_pre, d_filters)
+    )(doc_lengths, filters, d_q_main, d_q_tail, near, from_half, rims, *all_sums)
 
 
 def solution(mesh):

time: 40.4 us -> 41.1 us (1.017); the launches traced: 40 us -> 41.2 us
  waiting for transfers between devices: 10.5 us -> 13.9 us
  Pallas kernels: 8.17 us -> 6.82 us
  other arithmetic: 0.6 us -> 0 us
    ppermute x11, waiting for transfers between devices: 9.9 us -> 12 us  [flipped(): return lax.ppermute(array, 'ctx', [(i, i ^ flip) for i in range(ctx_count)])]
    pallas_call x1, Pallas kernels: 5.87 us -> 4.51 us  [shards(): pl.pallas_call(functools.partial(grads_kernel, ctx_count, direct), out_sh...]
    ppermute x3, waiting for transfers between devices: 0.56 us -> 1.83 us  [shards(): lax.ppermute(sums, 'tp', [(i, i ^ flip) for i in range(count)])]
    add x1 -> x0, other arithmetic: 0.6 us -> none  [shards(): level = [level[at] + level[at + 1] for at in range(0, len(level), 2)]]
  transfers between devices with their start and end apart: 14 -> 14, of which waited for: 8 -> 9; matrix products, arithmetic and copies ran while one was open for 0% -> 0% of each run, Pallas kernels for 3% -> 0%
where the time goes in v3:
time: 41.1 us; the launch traced here: 41.2 us
  starting transfers between devices  19.8 us (48%)
  waiting for transfers between devices  13.9 us (34%)
  Pallas kernels  6.82 us (17%)
  between operations  0.68 us (2%)
    ppermute x11, starting transfers between devices, flipped(): return lax.ppermute(array, 'ctx', [(i, i ^ flip) for i in range(ctx_count)])  18 us
    ppermute x11, waiting for transfers between devices, flipped(): return lax.ppermute(array, 'ctx', [(i, i ^ flip) for i in range(ctx_count)])  12 us
    pallas_call x1, Pallas kernels, shards(): pl.pallas_call(functools.partial(grads_kernel, ctx_count, direct), out_sh...  4.51 us
    ppermute x3, starting transfers between devices, shards(): lax.ppermute(sums, 'tp', [(i, i ^ flip) for i in range(count)])  1.86 us
    ppermute x3, waiting for transfers between devices, shards(): lax.ppermute(sums, 'tp', [(i, i ^ flip) for i in range(count)])  1.83 us
    pallas_call x1, Pallas kernels, shards(): pl.pallas_call(functools.partial(finish_kernel, ctx_count), out_shape=(ja...  1.27 us
    pallas_call x1, Pallas kernels, shards(): pl.pallas_call(pack_kernel, grid=(1,), out_shape=jax.ShapeDtypeStruct((ms...  0.91 us
  transfers between devices with their start and end apart: 14, of which 9 were waited for; matrix products, arithmetic and copies ran while one was open for 0% of the time, Pallas kernels for 0%

profile of v3, /device:TPU:0, one launch (start us, length us, event | category | flops | bytes accessed | tf_op | source)
XLA Modules:
  0.0 41.2 jit_solution(14005513862155619103)
XLA Ops:
  0.6 0.0 copy-start.1
  0.6 0.0 copy-start
  0.7 0.9 %pack.1.refs_0_ = bf16[144,256]{1,0:T(8,128)(2,1)S(1)} custom-call(bf16[2,64,128]{2,1,0:T(8,128)(2,1)} %k_ref.1, bf16[2,64,128]{2,1,0:T(8,128)(2,1)} %v_ref.1, bf16[2,64,1024]{2,1,0:T(8,128)(2,1)} %q_hbm.1), custom_call_target="tpu_custom_call" | custom-call | tf_op jit(solution)/shard_map/pack/pallas_call | solution.py:538
  1.6 4.1 %collective-permute-start.3 = (bf16[144,256]{1,0:T(8,128)(2,1)S(1)}, bf16[144,256]{1,0:T(8,128)(2,1)S(1)}, u32[]{:S(2)}, u32[]{:S(2)}) collective-permute-start(bf16[144,256]{1,0:T(8,128)(2,1)S(1)} %pack.1.refs_0_), channel_id=1, source_target_pairs={{0,16},{4,20},{8,24},{12,28},{16,0},{20,4},{24,8},{28,12},{1,17},{... | collective-permute-start | bytes 221192 | tf_op jit(solution)/shard_map/ppermute | solution.py:526
  5.7 2.5 %collective-permute-start.2 = (bf16[144,256]{1,0:T(8,128)(2,1)S(1)}, bf16[144,256]{1,0:T(8,128)(2,1)S(1)}, u32[]{:S(2)}, u32[]{:S(2)}) collective-permute-start(bf16[144,256]{1,0:T(8,128)(2,1)S(1)} %pack.1.refs_0_), channel_id=1, source_target_pairs={{0,12},{4,8},{8,4},{12,0},{16,28},{20,24},{24,20},{28,16},{1,13},{... | collective-permute-start | bytes 221192 | tf_op jit(solution)/shard_map/ppermute | solution.py:526
  8.2 0.4 %collective-permute-start.1 = (bf16[144,256]{1,0:T(8,128)(2,1)S(1)}, bf16[144,256]{1,0:T(8,128)(2,1)S(1)}, u32[]{:S(2)}, u32[]{:S(2)}) collective-permute-start(bf16[144,256]{1,0:T(8,128)(2,1)S(1)} %pack.1.refs_0_), channel_id=1, source_target_pairs={{0,8},{4,12},{8,0},{12,4},{16,24},{20,28},{24,16},{28,20},{1,9},{5... | collective-permute-start | bytes 221192 | tf_op jit(solution)/shard_map/ppermute | solution.py:526
  8.6 0.5 %collective-permute-start = (bf16[144,256]{1,0:T(8,128)(2,1)S(1)}, bf16[144,256]{1,0:T(8,128)(2,1)S(1)}, u32[]{:S(2)}, u32[]{:S(2)}) collective-permute-start(bf16[144,256]{1,0:T(8,128)(2,1)S(1)} %pack.1.refs_0_), channel_id=1, source_target_pairs={{0,4},{4,0},{8,12},{12,8},{16,20},{20,16},{24,28},{28,24},{1,5},{5... | collective-permute-start | bytes 221192 | tf_op jit(solution)/shard_map/ppermute | solution.py:526
  9.2 0.0 collective-permute-done.3.refs_4_
  9.2 2.5 %collective-permute-start.6 = (bf16[144,256]{1,0:T(8,128)(2,1)S(1)}, bf16[144,256]{1,0:T(8,128)(2,1)S(1)}, u32[]{:S(2)}, u32[]{:S(2)}) collective-permute-start(bf16[144,256]{1,0:T(8,128)(2,1)S(1)} %collective-permute-done.3.refs_4_), channel_id=1, source_target_pairs={{0,12},{4,8},{8,4},{12,0},{16,28},{20,24},{24,20},{28,16},{1,13},{... | collective-permute-start | bytes 221192 | tf_op jit(solution)/shard_map/ppermute | solution.py:526
  11.7 0.7 %collective-permute-start.5 = (bf16[144,256]{1,0:T(8,128)(2,1)S(1)}, bf16[144,256]{1,0:T(8,128)(2,1)S(1)}, u32[]{:S(2)}, u32[]{:S(2)}) collective-permute-start(bf16[144,256]{1,0:T(8,128)(2,1)S(1)} %collective-permute-done.3.refs_4_), channel_id=1, source_target_pairs={{0,8},{4,12},{8,0},{12,4},{16,24},{20,28},{24,16},{28,20},{1,9},{5... | collective-permute-start | bytes 221192 | tf_op jit(solution)/shard_map/ppermute | solution.py:526
  12.4 0.0 collective-permute-done.2.refs_3_
  12.4 0.9 %collective-permute-start.4 = (bf16[144,256]{1,0:T(8,128)(2,1)S(1)}, bf16[144,256]{1,0:T(8,128)(2,1)S(1)}, u32[]{:S(2)}, u32[]{:S(2)}) collective-permute-start(bf16[144,256]{1,0:T(8,128)(2,1)S(1)} %collective-permute-done.3.refs_4_), channel_id=1, source_target_pairs={{0,4},{4,0},{8,12},{12,8},{16,20},{20,16},{24,28},{28,24},{1,5},{5... | collective-permute-start | bytes 221192 | tf_op jit(solution)/shard_map/ppermute | solution.py:526
  13.3 0.1 collective-permute-done.1.refs_2_
  13.4 0.9 %collective-permute-done.refs_1_ = bf16[144,256]{1,0:T(8,128)(2,1)S(1)} collective-permute-done((bf16[144,256]{1,0:T(8,128)(2,1)S(1)}, bf16[144,256]{1,0:T(8,128)(2,1)S(1)}, u32[]{:S(2)}, u32[]{:S(2)}) %collective-permute-start) | collective-permute-done | bytes 73760 | tf_op jit(solution)/shard_map/ppermute | solution.py:526
  14.3 0.8 %collective-permute-done.6.refs_7_ = bf16[144,256]{1,0:T(8,128)(2,1)S(1)} collective-permute-done((bf16[144,256]{1,0:T(8,128)(2,1)S(1)}, bf16[144,256]{1,0:T(8,128)(2,1)S(1)}, u32[]{:S(2)}, u32[]{:S(2)}) %collective-permute-start.6) | collective-permute-done | bytes 73760 | tf_op jit(solution)/shard_map/ppermute | solution.py:526
  15.1 0.9 %collective-permute-done.5.refs_6_ = bf16[144,256]{1,0:T(8,128)(2,1)S(1)} collective-permute-done((bf16[144,256]{1,0:T(8,128)(2,1)S(1)}, bf16[144,256]{1,0:T(8,128)(2,1)S(1)}, u32[]{:S(2)}, u32[]{:S(2)}) %collective-permute-start.5) | collective-permute-done | bytes 73760 | tf_op jit(solution)/shard_map/ppermute | solution.py:526
  16.0 0.7 %collective-permute-done.4.refs_5_ = bf16[144,256]{1,0:T(8,128)(2,1)S(1)} collective-permute-done((bf16[144,256]{1,0:T(8,128)(2,1)S(1)}, bf16[144,256]{1,0:T(8,128)(2,1)S(1)}, u32[]{:S(2)}, u32[]{:S(2)}) %collective-permute-start.4) | collective-permute-done | bytes 73760 | tf_op jit(solution)/shard_map/ppermute | solution.py:526
  16.7 0.0 copy-done.1
  16.7 0.0 copy-done
  16.7 4.5 %grads.1 = (f32[2,64,1024]{2,1,0:T(8,128)}, f32[2,8,1024]{2,1,0:T(8,128)S(1)}, f32[128,256]{1,0:T(8,128)S(1)}, f32[136,256]{1,0:T(8,128)S(1)}, bf16[224,256]{1,0...) custom-call(s32[8]{0:T(128)S(1)} %copy-done.1, f32[3,3,128]{2,1,0:T(4,128)S(1)} %copy-done, ...), custom_call_target="tpu_custom_call" | custom-call | tf_op jit(solution)/shard_map/grads/pallas_call | solution.py:583
  21.3 1.0 %collective-permute-start.7 = (bf16[224,256]{1,0:T(8,128)(2,1)S(1)}, bf16[224,256]{1,0:T(8,128)(2,1)S(1)}, u32[]{:S(2)}, u32[]{:S(2)}) collective-permute-start(bf16[224,256]{1,0:T(8,128)(2,1)S(1)} %get-tuple-element.19), channel_id=1, source_target_pairs={{0,4},{4,0},{8,12},{12,8},{16,20},{20,16},{24,28},{28,24},{1,5},{5... | collective-permute-start | bytes 344072 | tf_op jit(solution)/shard_map/ppermute | solution.py:526
  22.2 2.9 %collective-permute-start.9 = (bf16[224,256]{1,0:T(8,128)(2,1)S(1)}, bf16[224,256]{1,0:T(8,128)(2,1)S(1)}, u32[]{:S(2)}, u32[]{:S(2)}) collective-permute-start(bf16[224,256]{1,0:T(8,128)(2,1)S(1)} %get-tuple-element.21), channel_id=1, source_target_pairs={{0,12},{4,8},{8,4},{12,0},{16,28},{20,24},{24,20},{28,16},{1,13},{... | collective-permute-start | bytes 344072 | tf_op jit(solution)/shard_map/ppermute | solution.py:526
  25.1 0.0 collective-permute-start.8
  25.1 4.7 %collective-permute-done.8.refs_1_ = bf16[208,256]{1,0:T(8,128)(2,1)S(1)} collective-permute-done((bf16[208,256]{1,0:T(8,128)(2,1)S(1)}, bf16[208,256]{1,0:T(8,128)(2,1)S(1)}, u32[]{:S(2)}, u32[]{:S(2)}) %collective-permute-start.8) | collective-permute-done | bytes 106528 | tf_op jit(solution)/shard_map/ppermute | solution.py:526
  29.8 0.0 collective-permute-done.7.refs_0_
  29.8 0.0 collective-permute-done.9.refs_2_
  29.8 0.1 merge.1
  30.0 2.4 %collective-permute-start.10 = (bf16[160,256]{1,0:T(8,128)(2,1)S(1)}, bf16[160,256]{1,0:T(8,128)(2,1)S(1)}, u32[]{:S(2)}, u32[]{:S(2)}) collective-permute-start(bf16[160,256]{1,0:T(8,128)(2,1)S(1)} %get-tuple-element.23), channel_id=1, source_target_pairs={{0,16},{4,20},{8,24},{12,28},{16,0},{20,4},{24,8},{28,12},{1,17},{... | collective-permute-start | bytes 245768 | tf_op jit(solution)/shard_map/ppermute | solution.py:526
  32.4 3.9 %collective-permute-done.10.far_ref = bf16[160,256]{1,0:T(8,128)(2,1)S(1)} collective-permute-done((bf16[160,256]{1,0:T(8,128)(2,1)S(1)}, bf16[160,256]{1,0:T(8,128)(2,1)S(1)}, u32[]{:S(2)}, u32[]{:S(2)}) %collective-permute-start.10) | collective-permute-done | bytes 81952 | tf_op jit(solution)/shard_map/ppermute | solution.py:526
  36.3 0.0 collective-permute-start.13
  36.3 1.6 %collective-permute-start.12 = (f32[3,3,128]{2,1,0:T(4,128)S(1)}, f32[3,3,128]{2,1,0:T(4,128)S(1)}, u32[]{:S(2)}, u32[]{:S(2)}) collective-permute-start(f32[3,3,128]{2,1,0:T(4,128)S(1)} %sums.1.refs_0_), channel_id=1, source_target_pairs={{0,2},{1,3},{2,0},{3,1},{4,6},{5,7},{6,4},{7,5},{8,10},{9,11},{10,... | collective-permute-start | bytes 13832 | tf_op jit(solution)/shard_map/ppermute | solution.py:625
  37.8 0.3 collective-permute-start.11
  38.1 1.2 %collective-permute-done.13.refs_3_ = f32[3,3,128]{2,1,0:T(4,128)S(1)} collective-permute-done((f32[3,3,128]{2,1,0:T(4,128)S(1)}, f32[3,3,128]{2,1,0:T(4,128)S(1)}, u32[]{:S(2)}, u32[]{:S(2)}) %collective-permute-start.13) | collective-permute-done | bytes 4640 | tf_op jit(solution)/shard_map/ppermute | solution.py:625
  39.3 0.6 %collective-permute-done.12.refs_2_ = f32[3,3,128]{2,1,0:T(4,128)S(1)} collective-permute-done((f32[3,3,128]{2,1,0:T(4,128)S(1)}, f32[3,3,128]{2,1,0:T(4,128)S(1)}, u32[]{:S(2)}, u32[]{:S(2)}) %collective-permute-start.12) | collective-permute-done | bytes 4640 | tf_op jit(solution)/shard_map/ppermute | solution.py:625
  39.9 0.0 collective-permute-done.11.refs_1_
  39.9 1.3 %finish.1 = (f32[2,64,1024]{2,1,0:T(8,128)}, f32[2,64,128]{2,1,0:T(8,128)}, f32[2,64,128]{2,1,0:T(8,128)}, f32[3,3,128]{2,1,0:T(4,128)}) custom-call(s32[8]{0:T(128)S(1)} %copy-done.1, f32[3,3,128]{2,1,0:T(4,128)S(1)} %copy-done, f32[2,64,1024]{2,1,0:T(8,128)} %get-tuple-element.15.dq_in_hbm, ...), custom_call_target="tpu_custom_call", output_to_operand_aliasing={{0}: (2, {})} | custom-call | tf_op jit(solution)/shard_map/finish/pallas_call | solution.py:627
  (1 shorter events, 0.0 us)
Async XLA Ops:
  0.6 16.1 %copy-start.1 = (s32[8]{0:T(128)S(1)}, s32[8]{0:T(128)}, u32[]{:S(2)}) copy-start(s32[8]{0:T(128)} %lengths_ref.3) | copy-start | bytes 100
  0.6 16.1 %copy-start = (f32[3,3,128]{2,1,0:T(4,128)S(1)}, f32[3,3,128]{2,1,0:T(4,128)}, u32[]{:S(2)}) copy-start(f32[3,3,128]{2,1,0:T(4,128)} %filters_ref.3) | copy-start | bytes 13828
  1.6 7.6 %collective-permute-start.3 = (bf16[144,256]{1,0:T(8,128)(2,1)S(1)}, bf16[144,256]{1,0:T(8,128)(2,1)S(1)}, u32[]{:S(2)}, u32[]{:S(2)}) collective-permute-start(bf16[144,256]{1,0:T(8,128)(2,1)S(1)} %pack.1.refs_0_), channel_id=1, source_target_pairs={{0,16},{4,20},{8,24},{12,28},{16,0},{20,4},{24,8},{28,12},{1,17},{... | collective-permute-start | bytes 221192 | tf_op jit(solution)/shard_map/ppermute | solution.py:526
  5.7 6.7 %collective-permute-start.2 = (bf16[144,256]{1,0:T(8,128)(2,1)S(1)}, bf16[144,256]{1,0:T(8,128)(2,1)S(1)}, u32[]{:S(2)}, u32[]{:S(2)}) collective-permute-start(bf16[144,256]{1,0:T(8,128)(2,1)S(1)} %pack.1.refs_0_), channel_id=1, source_target_pairs={{0,12},{4,8},{8,4},{12,0},{16,28},{20,24},{24,20},{28,16},{1,13},{... | collective-permute-start | bytes 221192 | tf_op jit(solution)/shard_map/ppermute | solution.py:526
  8.2 5.2 %collective-permute-start.1 = (bf16[144,256]{1,0:T(8,128)(2,1)S(1)}, bf16[144,256]{1,0:T(8,128)(2,1)S(1)}, u32[]{:S(2)}, u32[]{:S(2)}) collective-permute-start(bf16[144,256]{1,0:T(8,128)(2,1)S(1)} %pack.1.refs_0_), channel_id=1, source_target_pairs={{0,8},{4,12},{8,0},{12,4},{16,24},{20,28},{24,16},{28,20},{1,9},{5... | collective-permute-start | bytes 221192 | tf_op jit(solution)/shard_map/ppermute | solution.py:526
  8.6 5.7 %collective-permute-start = (bf16[144,256]{1,0:T(8,128)(2,1)S(1)}, bf16[144,256]{1,0:T(8,128)(2,1)S(1)}, u32[]{:S(2)}, u32[]{:S(2)}) collective-permute-start(bf16[144,256]{1,0:T(8,128)(2,1)S(1)} %pack.1.refs_0_), channel_id=1, source_target_pairs={{0,4},{4,0},{8,12},{12,8},{16,20},{20,16},{24,28},{28,24},{1,5},{5... | collective-permute-start | bytes 221192 | tf_op jit(solution)/shard_map/ppermute | solution.py:526
  9.2 6.0 %collective-permute-start.6 = (bf16[144,256]{1,0:T(8,128)(2,1)S(1)}, bf16[144,256]{1,0:T(8,128)(2,1)S(1)}, u32[]{:S(2)}, u32[]{:S(2)}) collective-permute-start(bf16[144,256]{1,0:T(8,128)(2,1)S(1)} %collective-permute-done.3.refs_4_), channel_id=1, source_target_pairs={{0,12},{4,8},{8,4},{12,0},{16,28},{20,24},{24,20},{28,16},{1,13},{... | collective-permute-start | bytes 221192 | tf_op jit(solution)/shard_map/ppermute | solution.py:526
  11.7 4.4 %collective-permute-start.5 = (bf16[144,256]{1,0:T(8,128)(2,1)S(1)}, bf16[144,256]{1,0:T(8,128)(2,1)S(1)}, u32[]{:S(2)}, u32[]{:S(2)}) collective-permute-start(bf16[144,256]{1,0:T(8,128)(2,1)S(1)} %collective-permute-done.3.refs_4_), channel_id=1, source_target_pairs={{0,8},{4,12},{8,0},{12,4},{16,24},{20,28},{24,16},{28,20},{1,9},{5... | collective-permute-start | bytes 221192 | tf_op jit(solution)/shard_map/ppermute | solution.py:526
  12.4 4.4 %collective-permute-start.4 = (bf16[144,256]{1,0:T(8,128)(2,1)S(1)}, bf16[144,256]{1,0:T(8,128)(2,1)S(1)}, u32[]{:S(2)}, u32[]{:S(2)}) collective-permute-start(bf16[144,256]{1,0:T(8,128)(2,1)S(1)} %collective-permute-done.3.refs_4_), channel_id=1, source_target_pairs={{0,4},{4,0},{8,12},{12,8},{16,20},{20,16},{24,28},{28,24},{1,5},{5... | collective-permute-start | bytes 221192 | tf_op jit(solution)/shard_map/ppermute | solution.py:526
  21.3 8.6 %collective-permute-start.7 = (bf16[224,256]{1,0:T(8,128)(2,1)S(1)}, bf16[224,256]{1,0:T(8,128)(2,1)S(1)}, u32[]{:S(2)}, u32[]{:S(2)}) collective-permute-start(bf16[224,256]{1,0:T(8,128)(2,1)S(1)} %get-tuple-element.19), channel_id=1, source_target_pairs={{0,4},{4,0},{8,12},{12,8},{16,20},{20,16},{24,28},{28,24},{1,5},{5... | collective-permute-start | bytes 344072 | tf_op jit(solution)/shard_map/ppermute | solution.py:526
  22.2 7.6 %collective-permute-start.9 = (bf16[224,256]{1,0:T(8,128)(2,1)S(1)}, bf16[224,256]{1,0:T(8,128)(2,1)S(1)}, u32[]{:S(2)}, u32[]{:S(2)}) collective-permute-start(bf16[224,256]{1,0:T(8,128)(2,1)S(1)} %get-tuple-element.21), channel_id=1, source_target_pairs={{0,12},{4,8},{8,4},{12,0},{16,28},{20,24},{24,20},{28,16},{1,13},{... | collective-permute-start | bytes 344072 | tf_op jit(solution)/shard_map/ppermute | solution.py:526
  25.1 4.7 %collective-permute-start.8 = (bf16[208,256]{1,0:T(8,128)(2,1)S(1)}, bf16[208,256]{1,0:T(8,128)(2,1)S(1)}, u32[]{:S(2)}, u32[]{:S(2)}) collective-permute-start(bf16[208,256]{1,0:T(8,128)(2,1)S(1)} %get-tuple-element.20), channel_id=1, source_target_pairs={{0,8},{4,12},{8,0},{12,4},{16,24},{20,28},{24,16},{28,20},{1,9},{5... | collective-permute-start | bytes 319496 | tf_op jit(solution)/shard_map/ppermute | solution.py:526
  30.0 6.3 %collective-permute-start.10 = (bf16[160,256]{1,0:T(8,128)(2,1)S(1)}, bf16[160,256]{1,0:T(8,128)(2,1)S(1)}, u32[]{:S(2)}, u32[]{:S(2)}) collective-permute-start(bf16[160,256]{1,0:T(8,128)(2,1)S(1)} %get-tuple-element.23), channel_id=1, source_target_pairs={{0,16},{4,20},{8,24},{12,28},{16,0},{20,4},{24,8},{28,12},{1,17},{... | collective-permute-start | bytes 245768 | tf_op jit(solution)/shard_map/ppermute | solution.py:526
  36.3 3.1 %collective-permute-start.13 = (f32[3,3,128]{2,1,0:T(4,128)S(1)}, f32[3,3,128]{2,1,0:T(4,128)S(1)}, u32[]{:S(2)}, u32[]{:S(2)}) collective-permute-start(f32[3,3,128]{2,1,0:T(4,128)S(1)} %sums.1.refs_0_), channel_id=1, source_target_pairs={{0,3},{1,2},{2,1},{3,0},{4,7},{5,6},{6,5},{7,4},{8,11},{9,10},{10,... | collective-permute-start | bytes 13832 | tf_op jit(solution)/shard_map/ppermute | solution.py:625
  36.3 3.7 %collective-permute-start.12 = (f32[3,3,128]{2,1,0:T(4,128)S(1)}, f32[3,3,128]{2,1,0:T(4,128)S(1)}, u32[]{:S(2)}, u32[]{:S(2)}) collective-permute-start(f32[3,3,128]{2,1,0:T(4,128)S(1)} %sums.1.refs_0_), channel_id=1, source_target_pairs={{0,2},{1,3},{2,0},{3,1},{4,6},{5,7},{6,4},{7,5},{8,10},{9,11},{10,... | collective-permute-start | bytes 13832 | tf_op jit(solution)/shard_map/ppermute | solution.py:625
  37.8 2.1 %collective-permute-start.11 = (f32[3,3,128]{2,1,0:T(4,128)S(1)}, f32[3,3,128]{2,1,0:T(4,128)S(1)}, u32[]{:S(2)}, u32[]{:S(2)}) collective-permute-start(f32[3,3,128]{2,1,0:T(4,128)S(1)} %sums.1.refs_0_), channel_id=1, source_target_pairs={{0,1},{1,0},{2,3},{3,2},{4,5},{5,4},{6,7},{7,6},{8,9},{9,8},{10,11... | collective-permute-start | bytes 13832 | tf_op jit(solution)/shard_map/ppermute | solution.py:625

commit v4 on v3

--- a/solution.py
+++ b/solution.py
@@ -70,7 +70,7 @@
     return lax.bitwise_xor(me, jnp.int32(flip))
 
 
-def pack_kernel(k_ref, v_ref, q_ref, out_ref):
+def pack_kernel(ctx_count, direct, k_ref, v_ref, q_ref, out_ref, *near_refs):
     span = k_ref.shape[1]
     kv = jnp.concatenate([k_ref[...], v_ref[...]], axis=2).reshape(2 * span, 2 * LANES)
     tails = []
@@ -78,12 +78,35 @@
         last = q_ref[half].astype(jnp.float32)[TAIL - 2 :]
         tails += [last[:, at : at + 2 * LANES] for at in range(0, last.shape[1], 2 * LANES)]
     out_ref[: 2 * span] = kv
-    out_ref[2 * span :] = jnp.concatenate(tails, axis=0).astype(jnp.bfloat16)
+    tail = jnp.concatenate(tails, axis=0).astype(jnp.bfloat16)
+    out_ref[2 * span :] = tail
+    me = lax.axis_index("ctx")
+    near = Slots((None,) + near_refs if direct else near_refs, me)
+
+    def send(step, carry):
+        flip = step + 1
+        near[flip][:span] = jnp.where(partner(me, flip) > me, kv[:span], kv[span:])
+        if not direct or flip & (flip + 1) == 0:
+            near[flip][span:] = tail
+        return carry
+
+    loop(ctx_count // 2 - 1, send, 0, 16 if direct else 1)
+
+
+def relay_kernel(ctx_count, own_ref, across_ref, body_ref, full_ref):
+    span = own_ref.shape[0] // 2 - TAIL // 2
+    low = lax.axis_index("ctx") < ctx_count // 2
+    second = jnp.where(low, across_ref[span : 2 * span], own_ref[:span])
+    for out_ref in (body_ref, full_ref):
+        out_ref[:span] = across_ref[:span]
+        out_ref[span : 2 * span] = second
+    full_ref[2 * span :] = across_ref[2 * span :]
 
 
 def grads_kernel(ctx_count, direct, lengths_ref, filters_ref, q_hbm, d_out_hbm, *refs):
     group = ctx_count // 2
-    arrays = group if direct else 1
+    arrays = group - 1 if direct else 1
+    own_ref, across_ref, refs = refs[0], refs[1], refs[2:]
     near_in, far_in, refs = refs[:arrays], refs[arrays : 2 * arrays], refs[2 * arrays :]
     dq_hbm, dq_tail_ref, own_near_ref, own_far_ref = refs[:4]
     arrays = group - 1 if direct else 1
@@ -103,7 +126,8 @@
     length = 2 * half_rows
     blocks = 2 * ctx_count
     me = lax.axis_index("ctx")
-    near_in, far_in = Slots(near_in, me), Slots(far_in, me)
+    near_in = Slots((None,) + near_in if direct else near_in, me)
+    far_in = Slots((None,) + far_in if direct else far_in, me)
     sent = Slots((own_far_ref,) + out_refs if direct else out_refs, me)
     scale = LANES**-0.5
     log2_scale = scale * 1.4426950408889634
@@ -127,21 +151,38 @@
         same_two_scr[pl.ds(8 + start, 1)] = zeros[:1]
         same_two_scr[pl.ds(9 + start, 1)] = zeros[:1]
 
-    def place_blocks(flip, carry):
-        for message, index in (
-            (near_in[flip], partner(me, flip)),
-            (far_in[flip], partner(me, flip + group)),
-        ):
-            early = aligned(8 + index * span, 8)
-            late = aligned(8 + (blocks - 1 - index) * span, 8)
-            for tensor in range(2):
-                lanes = slice(tensor * LANES, (tensor + 1) * LANES)
-                kv_scr[tensor, pl.ds(early, span)] = message[:span, lanes].astype(f32)
-                kv_scr[tensor, pl.ds(late, span)] = message[span : 2 * span, lanes].astype(f32)
-            rim_scr[index] = message[2 * span :].astype(f32)
+    def place(index, block):
+        for tensor in range(2):
+            lanes = slice(tensor * LANES, (tensor + 1) * LANES)
+            kv_scr[tensor, pl.ds(aligned(8 + index * span, 8), span)] = block[:, lanes].astype(f32)
+
+    def clear_kv(index, carry):
+        for tensor in range(2):
+            kv_scr[tensor, pl.ds(aligned(8 + index * span, 8), span)] = jnp.zeros((span, LANES), f32)
         return carry
 
-    loop(group, place_blocks, 0)
+    low = me < group
+
+    def place_received(step, carry):
+        flip = step + 1
+        source = partner(me, flip)
+        across = partner(source, group)
+        near, far = near_in[flip], far_in[flip]
+        place(jnp.where(source < me, source, blocks - 1 - source), near[:span])
+        place(across, far[:span])
+        place(jnp.where(low, blocks - 1 - across, source), far[span : 2 * span])
+        if not direct or flip & (flip + 1) == 0:
+            rim_scr[source] = near[span:].astype(f32)
+        if not direct or flip == group - 1:
+            rim_scr[across] = far[2 * span :].astype(f32)
+        return carry
+
+    loop(blocks, clear_kv, 0)
+    for block_ref, index in ((own_ref, me), (across_ref, partner(me, group))):
+        place(index, block_ref[:span])
+        place(blocks - 1 - index, block_ref[span : 2 * span])
+        rim_scr[index] = block_ref[2 * span :].astype(f32)
+    loop(group - 1, place_received, 0, 16 if direct else 1)
 
     def taps(tensor):
         return [filters_ref[tensor, tap : tap + 1] for tap in range(3)]
@@ -336,8 +377,6 @@
             carry[at + 2] += fold_rows(own * two * kv_scr[tensor, pl.ds(base + 6, span)])
         return tuple(carry)
 
-    low = me < group
-
     def finish(step, carry):
         flip = step + 1
         owner = partner(me, flip)
@@ -526,8 +565,6 @@
         return lax.ppermute(array, "ctx", [(i, i ^ flip) for i in range(ctx_count)])
 
     def gathered(array):
-        if direct:
-            return [array] + [flipped(array, flip) for flip in range(1, group)]
         return [lax.all_gather(array, "ctx", axis_index_groups=halves)]
 
     def delivered(arrays):
@@ -535,21 +572,43 @@
             return [flipped(array, step + 1) for step, array in enumerate(arrays)]
         return [lax.all_to_all(arrays[0], "ctx", 0, 0, axis_index_groups=halves, tiled=True)]
 
-    packed = pl.pallas_call(
-        pack_kernel,
+    if direct:
+        near_shapes = [
+            (span + (rim if flip & (flip + 1) == 0 else 0), 2 * LANES) for flip in range(1, group)
+        ]
+    else:
+        near_shapes = [(group, span + rim, 2 * LANES)]
+    packed, *near = pl.pallas_call(
+        functools.partial(pack_kernel, ctx_count, direct),
         grid=(1,),
-        out_shape=jax.ShapeDtypeStruct((msg_rows, 2 * LANES), bf16),
+        out_shape=[
+            jax.ShapeDtypeStruct(shape, bf16) for shape in [(msg_rows, 2 * LANES)] + near_shapes
+        ],
         in_specs=[
             whole(k_pre.shape),
             whole(k_pre.shape),
             pl.BlockSpec((2, TAIL, width), lambda i: (0, span // TAIL - 1, 0)),
         ],
-        out_specs=whole((msg_rows, 2 * LANES)),
-        compiler_params=pltpu.CompilerParams(vmem_limit_bytes=4 * MIB),
+        out_specs=[whole(shape) for shape in [(msg_rows, 2 * LANES)] + near_shapes],
+        compiler_params=pltpu.CompilerParams(vmem_limit_bytes=(4 if direct else 16) * MIB),
         name="pack",
     )(*[in_hbm(array) for array in (k_pre, value_before_filter, q_pre)])
     across = flipped(packed, group)
-    received = gathered(packed) + gathered(across)
+    near = delivered(near)
+    across, *near = lax.optimization_barrier((across, *near))
+    body, full = pl.pallas_call(
+        functools.partial(relay_kernel, ctx_count),
+        out_shape=[jax.ShapeDtypeStruct((rows, 2 * LANES), bf16) for rows in (2 * span, msg_rows)],
+        in_specs=[vmem, vmem],
+        out_specs=[vmem, vmem],
+        compiler_params=pltpu.CompilerParams(vmem_limit_bytes=4 * MIB),
+        name="relay",
+    )(packed, across)
+    if direct:
+        far = [flipped(full if flip == group - 1 else body, flip) for flip in range(1, group)]
+    else:
+        far = gathered(full)
+    received = [packed, across] + near + far
 
     window = span * ctx_count + span
     if direct:

time: 41.1 us -> 44.5 us (1.083)
  waiting for transfers between devices: 13.9 us -> 18.9 us
  starting transfers between devices: 19.8 us -> 17.8 us
    ppermute x11, waiting for transfers between devices: 12 us -> 17.1 us  [flipped(): return lax.ppermute(array, 'ctx', [(i, i ^ flip) for i in range(ctx_count)])]
    ppermute x11, starting transfers between devices: 18 us -> 15.9 us  [flipped(): return lax.ppermute(array, 'ctx', [(i, i ^ flip) for i in range(ctx_count)])]
    pallas_call x1 -> x2, Pallas kernels: 0.91 us -> 0.93 us  [the longest x1 0.91 us: shards(): pl.pallas_call(functools.partial(pack_kernel, ctx_count, direct), grid=(1...]
  transfers between devices with their start and end apart: 14 -> 14, of which waited for: 9 -> 7; matrix products, arithmetic and copies ran while one was open for 0% -> 0% of each run, Pallas kernels for 0% -> 0%
where the time goes in v4:
time: 44.5 us; the launch traced here: 44.2 us
  waiting for transfers between devices  18.9 us (42%)
  starting transfers between devices  17.8 us (40%)
  Pallas kernels  6.86 us (15%)
  between operations  0.69 us (2%)
    ppermute x11, waiting for transfers between devices, flipped(): return lax.ppermute(array, 'ctx', [(i, i ^ flip) for i in range(ctx_count)])  17.1 us
    ppermute x11, starting transfers between devices, flipped(): return lax.ppermute(array, 'ctx', [(i, i ^ flip) for i in range(ctx_count)])  15.9 us
    pallas_call x1, Pallas kernels, shards(): pl.pallas_call(functools.partial(grads_kernel, ctx_count, direct), out_sh...  4.53 us
    ppermute x3, starting transfers between devices, shards(): lax.ppermute(sums, 'tp', [(i, i ^ flip) for i in range(count)])  1.86 us
    ppermute x3, waiting for transfers between devices, shards(): lax.ppermute(sums, 'tp', [(i, i ^ flip) for i in range(count)])  1.83 us
    pallas_call x1, Pallas kernels, shards(): pl.pallas_call(functools.partial(finish_kernel, ctx_count), out_shape=(ja...  1.27 us
    pallas_call x1, Pallas kernels, shards(): pl.pallas_call(functools.partial(pack_kernel, ctx_count, direct), grid=(1...  0.91 us
  transfers between devices with their start and end apart: 14, of which 7 were waited for; matrix products, arithmetic and copies ran while one was open for 0% of the time, Pallas kernels for 0%

profile of v4, /device:TPU:0, one launch (start us, length us, event | category | flops | bytes accessed | tf_op | source)
XLA Modules:
  0.0 44.2 jit_solution(17130173475256430064)
XLA Ops:
  0.6 0.9 %pack.1 = (bf16[144,256]{1,0:T(8,128)(2,1)S(1)}, bf16[80,256]{1,0:T(8,128)(2,1)S(1)}, bf16[64,256]{1,0:T(8,128)(2,1)S(1)}, bf16[80,256]{1,0:T(8,128)(2,1)S(1)}) custom-call(bf16[2,64,128]{2,1,0:T(8,128)(2,1)} %k_ref.1, bf16[2,64,128]{2,1,0:T(8,128)(2,1)} %v_ref.1, bf16[2,64,1024]{2,1,0:T(8,128)(2,1)} %q_hbm.1), custom_call_target="tpu_custom_call" | custom-call | tf_op jit(solution)/shard_map/pack/pallas_call | solution.py:581
  1.5 4.1 %collective-permute-start = (bf16[144,256]{1,0:T(8,128)(2,1)S(1)}, bf16[144,256]{1,0:T(8,128)(2,1)S(1)}, u32[]{:S(2)}, u32[]{:S(2)}) collective-permute-start(bf16[144,256]{1,0:T(8,128)(2,1)S(1)} %get-tuple-element.25.own_ref.refs_0_), channel_id=1, source_target_pairs={{0,16},{4,20},{8,24},{12,28},{16,0},{20,4},{24,8},{28,12},{1,17},{... | collective-permute-start | bytes 221192 | tf_op jit(solution)/shard_map/ppermute | solution.py:565
  5.6 1.5 %collective-permute-start.1 = (bf16[80,256]{1,0:T(8,128)(2,1)S(1)}, bf16[80,256]{1,0:T(8,128)(2,1)S(1)}, u32[]{:S(2)}, u32[]{:S(2)}) collective-permute-start(bf16[80,256]{1,0:T(8,128)(2,1)S(1)} %get-tuple-element.26), channel_id=1, source_target_pairs={{0,4},{4,0},{8,12},{12,8},{16,20},{20,16},{24,28},{28,24},{1,5},{5... | collective-permute-start | bytes 122888 | tf_op jit(solution)/shard_map/ppermute | solution.py:565
  7.1 1.5 %collective-permute-start.3 = (bf16[80,256]{1,0:T(8,128)(2,1)S(1)}, bf16[80,256]{1,0:T(8,128)(2,1)S(1)}, u32[]{:S(2)}, u32[]{:S(2)}) collective-permute-start(bf16[80,256]{1,0:T(8,128)(2,1)S(1)} %get-tuple-element.28), channel_id=1, source_target_pairs={{0,12},{4,8},{8,4},{12,0},{16,28},{20,24},{24,20},{28,16},{1,13},{... | collective-permute-start | bytes 122888 | tf_op jit(solution)/shard_map/ppermute | solution.py:565
  8.7 0.4 %collective-permute-start.2 = (bf16[64,256]{1,0:T(8,128)(2,1)S(1)}, bf16[64,256]{1,0:T(8,128)(2,1)S(1)}, u32[]{:S(2)}, u32[]{:S(2)}) collective-permute-start(bf16[64,256]{1,0:T(8,128)(2,1)S(1)} %get-tuple-element.27), channel_id=1, source_target_pairs={{0,8},{4,12},{8,0},{12,4},{16,24},{20,28},{24,16},{28,20},{1,9},{5... | collective-permute-start | bytes 98312 | tf_op jit(solution)/shard_map/ppermute | solution.py:565
  9.1 3.5 %collective-permute-done.2.refs_3_ = bf16[64,256]{1,0:T(8,128)(2,1)S(1)} collective-permute-done((bf16[64,256]{1,0:T(8,128)(2,1)S(1)}, bf16[64,256]{1,0:T(8,128)(2,1)S(1)}, u32[]{:S(2)}, u32[]{:S(2)}) %collective-permute-start.2) | collective-permute-done | bytes 32800 | tf_op jit(solution)/shard_map/ppermute | solution.py:565
  12.6 0.0 collective-permute-done.1.refs_2_
  12.6 0.0 collective-permute-done.3.refs_4_
  12.6 0.0 collective-permute-done.across_ref.refs_1_
  12.6 0.0 copy-start
  12.6 0.0 copy-start.1
  12.7 1.4 %collective-permute-start.6 = (bf16[144,256]{1,0:T(8,128)(2,1)S(1)}, bf16[144,256]{1,0:T(8,128)(2,1)S(1)}, u32[]{:S(2)}, u32[]{:S(2)}) collective-permute-start(bf16[144,256]{1,0:T(8,128)(2,1)S(1)} %get-tuple-element.34), channel_id=1, source_target_pairs={{0,12},{4,8},{8,4},{12,0},{16,28},{20,24},{24,20},{28,16},{1,13},{... | collective-permute-start | bytes 221192 | tf_op jit(solution)/shard_map/ppermute | solution.py:565
  14.1 1.6 %collective-permute-start.5 = (bf16[128,256]{1,0:T(8,128)(2,1)S(1)}, bf16[128,256]{1,0:T(8,128)(2,1)S(1)}, u32[]{:S(2)}, u32[]{:S(2)}) collective-permute-start(bf16[128,256]{1,0:T(8,128)(2,1)S(1)} %get-tuple-element.33), channel_id=1, source_target_pairs={{0,8},{4,12},{8,0},{12,4},{16,24},{20,28},{24,16},{28,20},{1,9},{5... | collective-permute-start | bytes 196616 | tf_op jit(solution)/shard_map/ppermute | solution.py:565
  15.7 0.5 %collective-permute-start.4 = (bf16[128,256]{1,0:T(8,128)(2,1)S(1)}, bf16[128,256]{1,0:T(8,128)(2,1)S(1)}, u32[]{:S(2)}, u32[]{:S(2)}) collective-permute-start(bf16[128,256]{1,0:T(8,128)(2,1)S(1)} %get-tuple-element.33), channel_id=1, source_target_pairs={{0,4},{4,0},{8,12},{12,8},{16,20},{20,16},{24,28},{28,24},{1,5},{5... | collective-permute-start | bytes 196616 | tf_op jit(solution)/shard_map/ppermute | solution.py:565
  16.2 2.5 %collective-permute-done.5.refs_6_ = bf16[128,256]{1,0:T(8,128)(2,1)S(1)} collective-permute-done((bf16[128,256]{1,0:T(8,128)(2,1)S(1)}, bf16[128,256]{1,0:T(8,128)(2,1)S(1)}, u32[]{:S(2)}, u32[]{:S(2)}) %collective-permute-start.5) | collective-permute-done | bytes 65568 | tf_op jit(solution)/shard_map/ppermute | solution.py:565
  18.7 1.2 %collective-permute-done.4.refs_5_ = bf16[128,256]{1,0:T(8,128)(2,1)S(1)} collective-permute-done((bf16[128,256]{1,0:T(8,128)(2,1)S(1)}, bf16[128,256]{1,0:T(8,128)(2,1)S(1)}, u32[]{:S(2)}, u32[]{:S(2)}) %collective-permute-start.4) | collective-permute-done | bytes 65568 | tf_op jit(solution)/shard_map/ppermute | solution.py:565
  19.9 0.0 collective-permute-done.6.refs_7_
  20.0 0.0 copy-done
  20.0 0.0 copy-done.1
  20.0 4.5 %grads.1 = (f32[2,64,1024]{2,1,0:T(8,128)}, f32[2,8,1024]{2,1,0:T(8,128)S(1)}, f32[128,256]{1,0:T(8,128)S(1)}, f32[136,256]{1,0:T(8,128)S(1)}, bf16[224,256]{1,0...) custom-call(s32[8]{0:T(128)S(1)} %copy-done.1, f32[3,3,128]{2,1,0:T(4,128)S(1)} %copy-done, ...), custom_call_target="tpu_custom_call" | custom-call | tf_op jit(solution)/shard_map/grads/pallas_call | solution.py:642
  24.5 0.8 %collective-permute-start.7 = (bf16[224,256]{1,0:T(8,128)(2,1)S(1)}, bf16[224,256]{1,0:T(8,128)(2,1)S(1)}, u32[]{:S(2)}, u32[]{:S(2)}) collective-permute-start(bf16[224,256]{1,0:T(8,128)(2,1)S(1)} %get-tuple-element.39), channel_id=1, source_target_pairs={{0,4},{4,0},{8,12},{12,8},{16,20},{20,16},{24,28},{28,24},{1,5},{5... | collective-permute-start | bytes 344072 | tf_op jit(solution)/shard_map/ppermute | solution.py:565
  25.3 1.2 %collective-permute-start.9 = (bf16[224,256]{1,0:T(8,128)(2,1)S(1)}, bf16[224,256]{1,0:T(8,128)(2,1)S(1)}, u32[]{:S(2)}, u32[]{:S(2)}) collective-permute-start(bf16[224,256]{1,0:T(8,128)(2,1)S(1)} %get-tuple-element.41), channel_id=1, source_target_pairs={{0,12},{4,8},{8,4},{12,0},{16,28},{20,24},{24,20},{28,16},{1,13},{... | collective-permute-start | bytes 344072 | tf_op jit(solution)/shard_map/ppermute | solution.py:565
  26.5 1.6 %collective-permute-start.8 = (bf16[208,256]{1,0:T(8,128)(2,1)S(1)}, bf16[208,256]{1,0:T(8,128)(2,1)S(1)}, u32[]{:S(2)}, u32[]{:S(2)}) collective-permute-start(bf16[208,256]{1,0:T(8,128)(2,1)S(1)} %get-tuple-element.40), channel_id=1, source_target_pairs={{0,8},{4,12},{8,0},{12,4},{16,24},{20,28},{24,16},{28,20},{1,9},{5... | collective-permute-start | bytes 319496 | tf_op jit(solution)/shard_map/ppermute | solution.py:565
  28.1 4.8 %collective-permute-done.8.refs_1_ = bf16[208,256]{1,0:T(8,128)(2,1)S(1)} collective-permute-done((bf16[208,256]{1,0:T(8,128)(2,1)S(1)}, bf16[208,256]{1,0:T(8,128)(2,1)S(1)}, u32[]{:S(2)}, u32[]{:S(2)}) %collective-permute-start.8) | collective-permute-done | bytes 106528 | tf_op jit(solution)/shard_map/ppermute | solution.py:565
  32.8 0.0 collective-permute-done.7.refs_0_
  32.8 0.0 collective-permute-done.9.refs_2_
  32.8 0.1 merge.1
  33.0 1.2 %collective-permute-start.10 = (bf16[160,256]{1,0:T(8,128)(2,1)S(1)}, bf16[160,256]{1,0:T(8,128)(2,1)S(1)}, u32[]{:S(2)}, u32[]{:S(2)}) collective-permute-start(bf16[160,256]{1,0:T(8,128)(2,1)S(1)} %get-tuple-element.43), channel_id=1, source_target_pairs={{0,16},{4,20},{8,24},{12,28},{16,0},{20,4},{24,8},{28,12},{1,17},{... | collective-permute-start | bytes 245768 | tf_op jit(solution)/shard_map/ppermute | solution.py:565
  34.2 5.1 %collective-permute-done.10.far_ref = bf16[160,256]{1,0:T(8,128)(2,1)S(1)} collective-permute-done((bf16[160,256]{1,0:T(8,128)(2,1)S(1)}, bf16[160,256]{1,0:T(8,128)(2,1)S(1)}, u32[]{:S(2)}, u32[]{:S(2)}) %collective-permute-start.10) | collective-permute-done | bytes 81952 | tf_op jit(solution)/shard_map/ppermute | solution.py:565
  39.3 0.0 collective-permute-start.13
  39.3 1.6 %collective-permute-start.12 = (f32[3,3,128]{2,1,0:T(4,128)S(1)}, f32[3,3,128]{2,1,0:T(4,128)S(1)}, u32[]{:S(2)}, u32[]{:S(2)}) collective-permute-start(f32[3,3,128]{2,1,0:T(4,128)S(1)} %sums.1.refs_0_), channel_id=1, source_target_pairs={{0,2},{1,3},{2,0},{3,1},{4,6},{5,7},{6,4},{7,5},{8,10},{9,11},{10,... | collective-permute-start | bytes 13832 | tf_op jit(solution)/shard_map/ppermute | solution.py:684
  40.8 0.3 collective-permute-start.11
  41.1 1.2 %collective-permute-done.13.refs_3_ = f32[3,3,128]{2,1,0:T(4,128)S(1)} collective-permute-done((f32[3,3,128]{2,1,0:T(4,128)S(1)}, f32[3,3,128]{2,1,0:T(4,128)S(1)}, u32[]{:S(2)}, u32[]{:S(2)}) %collective-permute-start.13) | collective-permute-done | bytes 4640 | tf_op jit(solution)/shard_map/ppermute | solution.py:684
  42.3 0.6 %collective-permute-done.12.refs_2_ = f32[3,3,128]{2,1,0:T(4,128)S(1)} collective-permute-done((f32[3,3,128]{2,1,0:T(4,128)S(1)}, f32[3,3,128]{2,1,0:T(4,128)S(1)}, u32[]{:S(2)}, u32[]{:S(2)}) %collective-permute-start.12) | collective-permute-done | bytes 4640 | tf_op jit(solution)/shard_map/ppermute | solution.py:684
  43.0 0.0 collective-permute-done.11.refs_1_
  43.0 1.3 %finish.1 = (f32[2,64,1024]{2,1,0:T(8,128)}, f32[2,64,128]{2,1,0:T(8,128)}, f32[2,64,128]{2,1,0:T(8,128)}, f32[3,3,128]{2,1,0:T(4,128)}) custom-call(s32[8]{0:T(128)S(1)} %copy-done.1, f32[3,3,128]{2,1,0:T(4,128)S(1)} %copy-done, f32[2,64,1024]{2,1,0:T(8,128)} %get-tuple-element.35.dq_in_hbm, ...), custom_call_target="tpu_custom_call", output_to_operand_aliasing={{0}: (2, {})} | custom-call | tf_op jit(solution)/shard_map/finish/pallas_call | solution.py:686
  (2 shorter events, 0.0 us)
Async XLA Ops:
  1.5 11.1 %collective-permute-start = (bf16[144,256]{1,0:T(8,128)(2,1)S(1)}, bf16[144,256]{1,0:T(8,128)(2,1)S(1)}, u32[]{:S(2)}, u32[]{:S(2)}) collective-permute-start(bf16[144,256]{1,0:T(8,128)(2,1)S(1)} %get-tuple-element.25.own_ref.refs_0_), channel_id=1, source_target_pairs={{0,16},{4,20},{8,24},{12,28},{16,0},{20,4},{24,8},{28,12},{1,17},{... | collective-permute-start | bytes 221192 | tf_op jit(solution)/shard_map/ppermute | solution.py:565
  5.6 7.0 %collective-permute-start.1 = (bf16[80,256]{1,0:T(8,128)(2,1)S(1)}, bf16[80,256]{1,0:T(8,128)(2,1)S(1)}, u32[]{:S(2)}, u32[]{:S(2)}) collective-permute-start(bf16[80,256]{1,0:T(8,128)(2,1)S(1)} %get-tuple-element.26), channel_id=1, source_target_pairs={{0,4},{4,0},{8,12},{12,8},{16,20},{20,16},{24,28},{28,24},{1,5},{5... | collective-permute-start | bytes 122888 | tf_op jit(solution)/shard_map/ppermute | solution.py:565
  7.1 5.5 %collective-permute-start.3 = (bf16[80,256]{1,0:T(8,128)(2,1)S(1)}, bf16[80,256]{1,0:T(8,128)(2,1)S(1)}, u32[]{:S(2)}, u32[]{:S(2)}) collective-permute-start(bf16[80,256]{1,0:T(8,128)(2,1)S(1)} %get-tuple-element.28), channel_id=1, source_target_pairs={{0,12},{4,8},{8,4},{12,0},{16,28},{20,24},{24,20},{28,16},{1,13},{... | collective-permute-start | bytes 122888 | tf_op jit(solution)/shard_map/ppermute | solution.py:565
  8.7 3.9 %collective-permute-start.2 = (bf16[64,256]{1,0:T(8,128)(2,1)S(1)}, bf16[64,256]{1,0:T(8,128)(2,1)S(1)}, u32[]{:S(2)}, u32[]{:S(2)}) collective-permute-start(bf16[64,256]{1,0:T(8,128)(2,1)S(1)} %get-tuple-element.27), channel_id=1, source_target_pairs={{0,8},{4,12},{8,0},{12,4},{16,24},{20,28},{24,16},{28,20},{1,9},{5... | collective-permute-start | bytes 98312 | tf_op jit(solution)/shard_map/ppermute | solution.py:565
  12.6 7.3 %copy-start = (f32[3,3,128]{2,1,0:T(4,128)S(1)}, f32[3,3,128]{2,1,0:T(4,128)}, u32[]{:S(2)}) copy-start(f32[3,3,128]{2,1,0:T(4,128)} %filters_ref.3) | copy-start | bytes 13828
  12.6 7.3 %copy-start.1 = (s32[8]{0:T(128)S(1)}, s32[8]{0:T(128)}, u32[]{:S(2)}) copy-start(s32[8]{0:T(128)} %lengths_ref.3) | copy-start | bytes 100
  12.7 7.3 %collective-permute-start.6 = (bf16[144,256]{1,0:T(8,128)(2,1)S(1)}, bf16[144,256]{1,0:T(8,128)(2,1)S(1)}, u32[]{:S(2)}, u32[]{:S(2)}) collective-permute-start(bf16[144,256]{1,0:T(8,128)(2,1)S(1)} %get-tuple-element.34), channel_id=1, source_target_pairs={{0,12},{4,8},{8,4},{12,0},{16,28},{20,24},{24,20},{28,16},{1,13},{... | collective-permute-start | bytes 221192 | tf_op jit(solution)/shard_map/ppermute | solution.py:565
  14.1 4.6 %collective-permute-start.5 = (bf16[128,256]{1,0:T(8,128)(2,1)S(1)}, bf16[128,256]{1,0:T(8,128)(2,1)S(1)}, u32[]{:S(2)}, u32[]{:S(2)}) collective-permute-start(bf16[128,256]{1,0:T(8,128)(2,1)S(1)} %get-tuple-element.33), channel_id=1, source_target_pairs={{0,8},{4,12},{8,0},{12,4},{16,24},{20,28},{24,16},{28,20},{1,9},{5... | collective-permute-start | bytes 196616 | tf_op jit(solution)/shard_map/ppermute | solution.py:565
  15.7 4.3 %collective-permute-start.4 = (bf16[128,256]{1,0:T(8,128)(2,1)S(1)}, bf16[128,256]{1,0:T(8,128)(2,1)S(1)}, u32[]{:S(2)}, u32[]{:S(2)}) collective-permute-start(bf16[128,256]{1,0:T(8,128)(2,1)S(1)} %get-tuple-element.33), channel_id=1, source_target_pairs={{0,4},{4,0},{8,12},{12,8},{16,20},{20,16},{24,28},{28,24},{1,5},{5... | collective-permute-start | bytes 196616 | tf_op jit(solution)/shard_map/ppermute | solution.py:565
  24.5 8.3 %collective-permute-start.7 = (bf16[224,256]{1,0:T(8,128)(2,1)S(1)}, bf16[224,256]{1,0:T(8,128)(2,1)S(1)}, u32[]{:S(2)}, u32[]{:S(2)}) collective-permute-start(bf16[224,256]{1,0:T(8,128)(2,1)S(1)} %get-tuple-element.39), channel_id=1, source_target_pairs={{0,4},{4,0},{8,12},{12,8},{16,20},{20,16},{24,28},{28,24},{1,5},{5... | collective-permute-start | bytes 344072 | tf_op jit(solution)/shard_map/ppermute | solution.py:565
  25.3 7.5 %collective-permute-start.9 = (bf16[224,256]{1,0:T(8,128)(2,1)S(1)}, bf16[224,256]{1,0:T(8,128)(2,1)S(1)}, u32[]{:S(2)}, u32[]{:S(2)}) collective-permute-start(bf16[224,256]{1,0:T(8,128)(2,1)S(1)} %get-tuple-element.41), channel_id=1, source_target_pairs={{0,12},{4,8},{8,4},{12,0},{16,28},{20,24},{24,20},{28,16},{1,13},{... | collective-permute-start | bytes 344072 | tf_op jit(solution)/shard_map/ppermute | solution.py:565
  26.5 6.4 %collective-permute-start.8 = (bf16[208,256]{1,0:T(8,128)(2,1)S(1)}, bf16[208,256]{1,0:T(8,128)(2,1)S(1)}, u32[]{:S(2)}, u32[]{:S(2)}) collective-permute-start(bf16[208,256]{1,0:T(8,128)(2,1)S(1)} %get-tuple-element.40), channel_id=1, source_target_pairs={{0,8},{4,12},{8,0},{12,4},{16,24},{20,28},{24,16},{28,20},{1,9},{5... | collective-permute-start | bytes 319496 | tf_op jit(solution)/shard_map/ppermute | solution.py:565
  33.0 6.3 %collective-permute-start.10 = (bf16[160,256]{1,0:T(8,128)(2,1)S(1)}, bf16[160,256]{1,0:T(8,128)(2,1)S(1)}, u32[]{:S(2)}, u32[]{:S(2)}) collective-permute-start(bf16[160,256]{1,0:T(8,128)(2,1)S(1)} %get-tuple-element.43), channel_id=1, source_target_pairs={{0,16},{4,20},{8,24},{12,28},{16,0},{20,4},{24,8},{28,12},{1,17},{... | collective-permute-start | bytes 245768 | tf_op jit(solution)/shard_map/ppermute | solution.py:565
  39.3 3.1 %collective-permute-start.13 = (f32[3,3,128]{2,1,0:T(4,128)S(1)}, f32[3,3,128]{2,1,0:T(4,128)S(1)}, u32[]{:S(2)}, u32[]{:S(2)}) collective-permute-start(f32[3,3,128]{2,1,0:T(4,128)S(1)} %sums.1.refs_0_), channel_id=1, source_target_pairs={{0,3},{1,2},{2,1},{3,0},{4,7},{5,6},{6,5},{7,4},{8,11},{9,10},{10,... | collective-permute-start | bytes 13832 | tf_op jit(solution)/shard_map/ppermute | solution.py:684
  39.3 3.7 %collective-permute-start.12 = (f32[3,3,128]{2,1,0:T(4,128)S(1)}, f32[3,3,128]{2,1,0:T(4,128)S(1)}, u32[]{:S(2)}, u32[]{:S(2)}) collective-permute-start(f32[3,3,128]{2,1,0:T(4,128)S(1)} %sums.1.refs_0_), channel_id=1, source_target_pairs={{0,2},{1,3},{2,0},{3,1},{4,6},{5,7},{6,4},{7,5},{8,10},{9,11},{10,... | collective-permute-start | bytes 13832 | tf_op jit(solution)/shard_map/ppermute | solution.py:684
  40.8 2.1 %collective-permute-start.11 = (f32[3,3,128]{2,1,0:T(4,128)S(1)}, f32[3,3,128]{2,1,0:T(4,128)S(1)}, u32[]{:S(2)}, u32[]{:S(2)}) collective-permute-start(f32[3,3,128]{2,1,0:T(4,128)S(1)} %sums.1.refs_0_), channel_id=1, source_target_pairs={{0,1},{1,0},{2,3},{3,2},{4,5},{5,4},{6,7},{7,6},{8,9},{9,8},{10,11... | collective-permute-start | bytes 13832 | tf_op jit(solution)/shard_map/ppermute | solution.py:684
